TPU v7x, 32 devices: a whole 2x2x4 slice. The times are simulated.
32 devices in a mesh: gx: 4 (over y, core), gy: 8 (over z, x).
Axes of the slice: x: 2, y: 2, z: 4, core: 2. Of those that a mesh axis runs over, the one named last changes fastest.
Arguments:
- log_perm: float32 [32, 256, 128], P('gx', 'gy'), may hold values from -4 to 4
- perturb: float32 [32, 256, 128], P('gx', 'gy'), may hold values from -6 to 6
- storage: float32 [32, 256, 128], P('gx', 'gy'), may hold values from 0.03 to 1
- base_press: float32 [2, 32, 256, 128], P(None, 'gx', 'gy'), may hold values from -6 to 6
- well_rows: float32 [1024, 512], P(('gx', 'gy')), may hold values from 0.002 to 0.02
- well_cells: int32 [1024], P(('gx', 'gy')), may hold values from 0 to 32767
- well_counts: int32 [1024], P(('gx', 'gy')), may hold values from 1 to 512, as said below
- well_owner: int32 [1024, 1], P(('gx', 'gy')), may hold values from 0 to 31; in each aligned block of 32 rows (0 to 31, 32 to 63, ...) at most 2 rows name the same one
- well_start: int32 [1024], P(('gx', 'gy')), may hold values from 0 to 1
Outputs:
- hess_action: float32 [32, 256, 128], P('gx', 'gy')
- final_change: float32 [32, 256, 128], P('gx', 'gy')
Inputs may be any that keep to these rules, and one draw needn't show every extreme that they name: `well_owner`: names the device, counted as gx index times 8 plus gy index, whose tile holds the well; among the wells listed on one device no owner appears more than 2 times, and in every draw some device names some owner exactly 2 times. `well_cells`: index x * 32 * 128 + y * 128 + z of the well's cell within its owner's tile. `well_counts`: every draw has a well with all 512 samples and one with a single sample.
All inputs are finite; a program needn't handle non-finite values.
Results may differ from a plain program's by a relative error of at most 0.0001.
Values sent between devices are 32-bit elements; how exact they have to be, the bound alone decides.
No kernel may reach another device: no remote copies, remote signals or barrier semaphores. Data moves between devices by JAX's collectives and lax.ppermute only.
A program may use at most 128 MiB of HBM per device.

v0:
```python
import jax
import jax.numpy as jnp
from jax import lax
from jax.sharding import PartitionSpec as P

TSTEPS = 2
VCYCLES = 2
SWEEPS = 2
CSWEEPS = 4
SAMPLES = 512
CAP = 2


OMEGA = 0.8


def extended(block, sides, width):
    for axis, dim in sides:
        count = lax.axis_size(axis)
        forward = [(i, i + 1) for i in range(count - 1)]
        backward = [(target, source) for source, target in forward]
        low = lax.ppermute(
            lax.slice_in_dim(block, block.shape[dim] - width, None, axis=dim), axis, forward
        )
        high = lax.ppermute(lax.slice_in_dim(block, 0, width, axis=dim), axis, backward)
        block = jnp.concatenate([low, block, high], axis=dim)
    return block


def lower_pad(values):
    return jnp.pad(values, ((0, 0), (0, 0), (0, 1)))


def upper_pad(values):
    return jnp.pad(values, ((0, 0), (0, 0), (1, 0)))


def fine_rim(values):
    return extended(values, (("gx", 1), ("gy", 2)), 1)


def middle_rim(values):
    return extended(values, (("gx", 1), ("gy", 2)), 1)


def coarse_rim(values):
    return extended(values, (("gx", 1), ("gy", 2)), 1)


def coarsen(values):
    size_x, size_y, size_z = values.shape
    return values.reshape(size_x // 2, 2, size_y // 2, 2, size_z // 2, 2).mean(axis=(1, 3, 5))


def prolong(values):
    return jnp.repeat(jnp.repeat(jnp.repeat(values, 2, 0), 2, 1), 2, 2)


def coefficients(log_pad, storage_level, factor):
    center = log_pad[1:-1, 1:-1]
    along_x = factor * jnp.exp(0.5 * (log_pad[:-1, 1:-1] + log_pad[1:, 1:-1]))
    along_y = factor * jnp.exp(0.5 * (log_pad[1:-1, :-1] + log_pad[1:-1, 1:]))
    along_z = factor * jnp.exp(0.5 * (center[:, :, :-1] + center[:, :, 1:]))
    diagonal = storage_level + along_x[1:] + along_x[:-1] + along_y[:, 1:] + along_y[:, :-1]
    diagonal = diagonal + lower_pad(along_z) + upper_pad(along_z)
    return (along_x, along_y, along_z, diagonal)


def apply_operator(value_pad, coeffs):
    along_x, along_y, along_z, diagonal = coeffs
    center = value_pad[1:-1, 1:-1]
    beside = along_x[1:] * value_pad[2:, 1:-1] + along_x[:-1] * value_pad[:-2, 1:-1]
    beside = beside + along_y[:, 1:] * value_pad[1:-1, 2:] + along_y[:, :-1] * value_pad[1:-1, :-2]
    beside = beside + lower_pad(along_z * center[:, :, 1:]) + upper_pad(along_z * center[:, :, :-1])
    return diagonal * center - beside


def perturbed(pressure_pad, change_pad, coeffs):
    along_x, along_y, along_z, diagonal = coeffs
    pressure = pressure_pad[1:-1, 1:-1]
    change = change_pad[1:-1, 1:-1]
    summed = (
        along_x[1:] * 0.5 * (change + change_pad[2:, 1:-1]) * (pressure - pressure_pad[2:, 1:-1])
    )
    summed = summed + along_x[:-1] * 0.5 * (change + change_pad[:-2, 1:-1]) * (
        pressure - pressure_pad[:-2, 1:-1]
    )
    summed = summed + along_y[:, 1:] * 0.5 * (change + change_pad[1:-1, 2:]) * (
        pressure - pressure_pad[1:-1, 2:]
    )
    summed = summed + along_y[:, :-1] * 0.5 * (change + change_pad[1:-1, :-2]) * (
        pressure - pressure_pad[1:-1, :-2]
    )
    vertical = (
        along_z
        * 0.5
        * (change[:, :, :-1] + change[:, :, 1:])
        * (pressure[:, :, :-1] - pressure[:, :, 1:])
    )
    return summed + lower_pad(vertical) - upper_pad(vertical)


def curvature(pressure_pad, adjoint_pad, coeffs):
    along_x, along_y, along_z, diagonal = coeffs
    pressure = pressure_pad[1:-1, 1:-1]
    adjoint = adjoint_pad[1:-1, 1:-1]
    summed = (
        0.5 * along_x[1:] * (pressure - pressure_pad[2:, 1:-1]) * (adjoint - adjoint_pad[2:, 1:-1])
    )
    summed = summed + 0.5 * along_x[:-1] * (pressure - pressure_pad[:-2, 1:-1]) * (
        adjoint - adjoint_pad[:-2, 1:-1]
    )
    summed = summed + 0.5 * along_y[:, 1:] * (pressure - pressure_pad[1:-1, 2:]) * (
        adjoint - adjoint_pad[1:-1, 2:]
    )
    summed = summed + 0.5 * along_y[:, :-1] * (pressure - pressure_pad[1:-1, :-2]) * (
        adjoint - adjoint_pad[1:-1, :-2]
    )
    vertical = (
        0.5
        * along_z
        * (pressure[:, :, :-1] - pressure[:, :, 1:])
        * (adjoint[:, :, :-1] - adjoint[:, :, 1:])
    )
    return summed + lower_pad(vertical) + upper_pad(vertical)


def jacobi_sweep(iterate, right_side, coeffs, padder):
    if iterate is None:
        return OMEGA * right_side / coeffs[3]
    padded = padder(iterate[None])[0]
    return iterate + OMEGA * (right_side - apply_operator(padded, coeffs)) / coeffs[3]


def vcycle(iterate, right_side, fine_coeffs, middle_coeffs, fine_pad, middle_pad, coarse_solve):
    current = iterate
    for sweep_index in range(SWEEPS):
        current = jacobi_sweep(current, right_side, fine_coeffs, fine_pad)
    residual = right_side - apply_operator(fine_pad(current[None])[0], fine_coeffs)
    middle_side = coarsen(residual)
    middle = None
    for sweep_index in range(SWEEPS):
        middle = jacobi_sweep(middle, middle_side, middle_coeffs, middle_pad)
    middle_res = middle_side - apply_operator(middle_pad(middle[None])[0], middle_coeffs)
    middle = middle + prolong(coarse_solve(coarsen(middle_res)))
    for sweep_index in range(SWEEPS):
        middle = jacobi_sweep(middle, middle_side, middle_coeffs, middle_pad)
    current = current + prolong(middle)
    for sweep_index in range(SWEEPS):
        current = jacobi_sweep(current, right_side, fine_coeffs, fine_pad)
    return current


def multigrid_solve(right_side, fine_coeffs, middle_coeffs, fine_pad, middle_pad, coarse_solve):
    current = None
    for cycle_index in range(VCYCLES):
        current = vcycle(
            current, right_side, fine_coeffs, middle_coeffs, fine_pad, middle_pad, coarse_solve
        )
    return current


def well_weights(records, counts, starts):
    sample_pos = jnp.arange(SAMPLES, dtype=jnp.int32)
    counted = jnp.where(sample_pos[None, :] < counts[:, None], records, 0.0)
    per_step = counted.reshape(records.shape[0], TSTEPS, SAMPLES // TSTEPS).sum(axis=2)
    step_pos = jnp.arange(TSTEPS, dtype=jnp.int32)
    return jnp.where(step_pos[None, :] >= starts[:, None], per_step, 0.0)


def local(
    log_perm,
    perturb,
    storage,
    base_press,
    well_rows,
    well_cells,
    well_counts,
    well_owner,
    well_start,
):
    devices = lax.axis_size("gx") * lax.axis_size("gy")
    owner_ids = well_owner[:, 0]
    listed = owner_ids.shape[0]
    same_owner = owner_ids[:, None] == owner_ids[None, :]
    earlier = (
        jnp.arange(listed, dtype=jnp.int32)[None, :] < jnp.arange(listed, dtype=jnp.int32)[:, None]
    )
    slot_rank = jnp.sum(jnp.logical_and(same_owner, earlier), axis=1)
    slot_index = owner_ids * CAP + slot_rank
    slot_total = devices * CAP
    send_rows = jnp.zeros((slot_total, SAMPLES), jnp.float32).at[slot_index].set(well_rows)
    packed = jnp.stack([well_cells, well_counts, well_start], axis=1)
    send_ints = jnp.zeros((slot_total, 3), jnp.int32).at[slot_index].set(packed)
    got_rows, got_ints = (
        lax.all_to_all(send_rows, ("gx", "gy"), split_axis=0, concat_axis=0, tiled=True),
        lax.all_to_all(send_ints, ("gx", "gy"), split_axis=0, concat_axis=0, tiled=True),
    )
    weights = well_weights(got_rows, got_ints[:, 1], got_ints[:, 2])
    cell_ids = got_ints[:, 0]
    source = jnp.zeros((TSTEPS, log_perm.size), jnp.float32).at[:, cell_ids].add(weights.T)
    source = source.reshape((TSTEPS,) + log_perm.shape)
    padded = fine_rim(jnp.concatenate([log_perm[None], perturb[None], base_press], axis=0))
    fine_coeffs = coefficients(padded[0], storage, 1.0)
    middle_log = coarsen(log_perm)
    middle_store = coarsen(storage)
    middle_coeffs = coefficients(middle_rim(middle_log[None])[0], middle_store, 0.25)
    coarse_log = coarsen(middle_log)
    coarse_store = coarsen(middle_store)
    coarse_coeffs = coefficients(coarse_rim(coarse_log[None])[0], coarse_store, 0.0625)

    def coarse_solve(right_side):
        iterate = None
        for sweep_index in range(CSWEEPS):
            iterate = jacobi_sweep(iterate, right_side, coarse_coeffs, coarse_rim)
        return iterate

    def solve_field(right_side):
        return multigrid_solve(
            right_side, fine_coeffs, middle_coeffs, fine_rim, middle_rim, coarse_solve
        )

    previous = jnp.zeros(log_perm.shape, jnp.float32)
    changes = []
    for step_index in range(TSTEPS):
        right_side = storage * previous - perturbed(padded[2 + step_index], padded[1], fine_coeffs)
        previous = solve_field(right_side)
        changes.append(previous)
    adjoint_next = jnp.zeros(log_perm.shape, jnp.float32)
    adjoints = [None] * TSTEPS
    for step_index in range(TSTEPS - 1, -1, -1):
        right_side = storage * adjoint_next + source[step_index] * changes[step_index]
        adjoint_next = solve_field(right_side)
        adjoints[step_index] = adjoint_next
    adjoint_pad = fine_rim(jnp.stack(adjoints))
    hessian = jnp.zeros(log_perm.shape, jnp.float32)
    for step_index in range(TSTEPS):
        hessian = hessian - curvature(padded[2 + step_index], adjoint_pad[step_index], fine_coeffs)
    return (hessian, changes[-1])


def solution(mesh):
    return jax.shard_map(
        local,
        mesh=mesh,
        in_specs=(
            P("gx", "gy", None),
            P("gx", "gy", None),
            P("gx", "gy", None),
            P(None, "gx", "gy", None),
            P(("gx", "gy"), None),
            P(("gx", "gy")),
            P(("gx", "gy")),
            P(("gx", "gy"), None),
            P(("gx", "gy")),
        ),
        out_specs=(P("gx", "gy", None), P("gx", "gy", None)),
        check_vma=False,
    )
```

profile of v0, /device:TPU:0, one launch (start us, length us, event | category | flops | bytes accessed | tf_op | source)
XLA Modules:
  0.0 1673.3 jit_solution(16518120901940981600)
XLA Ops:
  5.9 10.5 reshape.257
  29.6 9.7 reshape.256
  94.5 9.7 reshape.255
  149.5 5.9 collective-permute-start.30
  296.6 9.7 reshape.265
  334.2 5.7 collective-permute-start.74
  460.3 5.9 collective-permute-start.106
  483.5 9.7 reshape.273
  521.0 5.7 collective-permute-start.118
  678.2 5.7 collective-permute-start.158
  685.5 9.7 reshape.281
  707.6 5.7 collective-permute-start.162
  723.1 6.1 collective-permute-start.166
  801.0 12.8 all-to-all-start
  826.6 7.0 all-to-all-start.1
  846.4 7.8 scatter_custom_fusion.2
  860.1 20.6 %slice_reduce_fusion = (f32[32768]{0:T(1024)S(1)}, f32[32768]{0:T(1024)S(1)}) fusion(f32[2,32768]{0,1:T(8,128)} %scatter_custom_fusion.2), kind=kLoop, calls=%fused_computation.3 | loop fusion | bytes 524288 | tf_op jit(solution)/shard_map/slice | solution.py:232
  888.4 5.7 collective-permute-start.198
  909.4 9.7 reshape.289
  1073.2 5.7 collective-permute-start.242
  1111.7 9.7 reshape.297
  1133.8 5.7 collective-permute-start.254
  1149.3 5.9 collective-permute-start.258
  1290.9 5.7 collective-permute-start.294
  1298.2 9.7 reshape.305
  1320.3 5.7 collective-permute-start.298
  1335.8 5.7 collective-permute-start.302
  1446.1 5.9 collective-permute-start.330
  1462.0 5.7 collective-permute-start.334
  1477.8 5.7 collective-permute-start.338
  1500.8 9.7 reshape.313
  1664.4 5.7 collective-permute-start.382
  (1487 shorter events, 1414.1 us)
Async XLA Ops:
  1.5 52.1 %collective-permute-start.1 = (f32[4,1,32,128]{3,2,1,0:T(8,128)S(1)}, f32[4,1,32,128]{3,2,1,0:T(8,128)S(1)}, u32[]{:S(2)}, u32[]{:S(2)}) collective-permute-start(f32[4,1,32,128]{3,2,1,0:T(8,128)S(1)} %get-tuple-element.28), channel_id=1, source_target_pairs={{8,0},{16,8},{24,16},{9,1},{17,9},{25,17},{10,2},{18,10},{26,18},{... | collective-permute-start | bytes 196616 | tf_op jit(solution)/shard_map/ppermute | solution.py:25
  2.8 50.8 %collective-permute-start = (f32[4,1,32,128]{3,2,1,0:T(8,128)S(1)}, f32[4,1,32,128]{3,2,1,0:T(8,128)S(1)}, u32[]{:S(2)}, u32[]{:S(2)}) collective-permute-start(f32[4,1,32,128]{3,2,1,0:T(8,128)S(1)} %get-tuple-element.27), channel_id=1, source_target_pairs={{0,8},{8,16},{16,24},{1,9},{9,17},{17,25},{2,10},{10,18},{18,26},{... | collective-permute-start | bytes 196616 | tf_op jit(solution)/shard_map/ppermute | solution.py:22
  21.7 21.7 %collective-permute-start.25 = (f32[1,1,8,32]{3,2,1,0:T(8,128)S(1)}, f32[1,1,8,32]{3,2,1,0:T(8,128)S(1)}, u32[]{:S(2)}, u32[]{:S(2)}) collective-permute-start(f32[1,1,8,32]{3,2,1,0:T(8,128)S(1)} %get-tuple-element.603), channel_id=1, source_target_pairs={{8,0},{16,8},{24,16},{9,1},{17,9},{25,17},{10,2},{18,10},{26,18},{... | collective-permute-start | bytes 3080 | tf_op jit(solution)/shard_map/ppermute | solution.py:25
  23.0 24.6 %collective-permute-start.24 = (f32[1,1,8,32]{3,2,1,0:T(8,128)S(1)}, f32[1,1,8,32]{3,2,1,0:T(8,128)S(1)}, u32[]{:S(2)}, u32[]{:S(2)}) collective-permute-start(f32[1,1,8,32]{3,2,1,0:T(8,128)S(1)} %get-tuple-element.602), channel_id=1, source_target_pairs={{0,8},{8,16},{16,24},{1,9},{9,17},{17,25},{2,10},{10,18},{18,26},{... | collective-permute-start | bytes 3080 | tf_op jit(solution)/shard_map/ppermute | solution.py:22
  28.2 20.8 %collective-permute-start.13 = (f32[1,1,16,64]{3,2,1,0:T(8,128)S(1)}, f32[1,1,16,64]{3,2,1,0:T(8,128)S(1)}, u32[]{:S(2)}, u32[]{:S(2)}) collective-permute-start(f32[1,1,16,64]{3,2,1,0:T(8,128)S(1)} %get-tuple-element.500), channel_id=1, source_target_pairs={{8,0},{16,8},{24,16},{9,1},{17,9},{25,17},{10,2},{18,10},{26,18},{... | collective-permute-start | bytes 12296 | tf_op jit(solution)/shard_map/ppermute | solution.py:25
  43.3 10.2 collective-permute-start.12
  47.7 66.8 %collective-permute-start.27 = (f32[1,4,1,32]{3,2,1,0:T(1,128)S(1)}, f32[1,4,1,32]{3,2,1,0:T(1,128)S(1)}, u32[]{:S(2)}, u32[]{:S(2)}) collective-permute-start(f32[1,4,1,32]{3,2,1,0:T(1,128)S(1)} %get-tuple-element.553), channel_id=1, source_target_pairs={{1,0},{2,1},{3,2},{4,3},{5,4},{6,5},{7,6},{9,8},{10,9},{11,10},{12... | collective-permute-start | bytes 1544 | tf_op jit(solution)/shard_map/ppermute | solution.py:25
  49.0 65.5 %collective-permute-start.26 = (f32[1,4,1,32]{3,2,1,0:T(1,128)S(1)}, f32[1,4,1,32]{3,2,1,0:T(1,128)S(1)}, u32[]{:S(2)}, u32[]{:S(2)}) collective-permute-start(f32[1,4,1,32]{3,2,1,0:T(1,128)S(1)} %get-tuple-element.552), channel_id=1, source_target_pairs={{0,1},{1,2},{2,3},{3,4},{4,5},{5,6},{6,7},{8,9},{9,10},{10,11},{11... | collective-permute-start | bytes 1544 | tf_op jit(solution)/shard_map/ppermute | solution.py:22
  53.6 7.6 collective-permute-start.3
  54.9 11.7 collective-permute-start.2
  59.9 8.8 collective-permute-start.15
  61.2 10.5 collective-permute-start.14
  130.8 8.3 collective-permute-start.23
  148.2 7.2 collective-permute-start.31
  459.0 7.2 collective-permute-start.107
  460.3 7.2 collective-permute-start.106
  721.8 7.4 collective-permute-start.167
  793.5 20.2 %collective-permute-start.185 = (f32[1,1,16,64]{3,2,1,0:T(8,128)S(1)}, f32[1,1,16,64]{3,2,1,0:T(8,128)S(1)}, u32[]{:S(2)}, u32[]{:S(2)}) collective-permute-start(f32[1,1,16,64]{3,2,1,0:T(8,128)S(1)} %get-tuple-element.465), channel_id=1, source_target_pairs={{8,0},{16,8},{24,16},{9,1},{17,9},{25,17},{10,2},{18,10},{26,18},{... | collective-permute-start | bytes 12296 | tf_op jit(solution)/shard_map/ppermute | solution.py:25
  794.8 18.9 %collective-permute-start.184 = (f32[1,1,16,64]{3,2,1,0:T(8,128)S(1)}, f32[1,1,16,64]{3,2,1,0:T(8,128)S(1)}, u32[]{:S(2)}, u32[]{:S(2)}) collective-permute-start(f32[1,1,16,64]{3,2,1,0:T(8,128)S(1)} %get-tuple-element.464), channel_id=1, source_target_pairs={{0,8},{8,16},{16,24},{1,9},{9,17},{17,25},{2,10},{10,18},{18,26},{... | collective-permute-start | bytes 12296 | tf_op jit(solution)/shard_map/ppermute | solution.py:22
  801.0 25.6 %all-to-all-start = ((s32[32,2,3]{2,1,0:T(2,128)}), s32[32,2,3]{2,1,0:T(2,128)S(1)}, u32[]{:S(2)}, u32[]{:S(2)}) async-start(s32[32,2,3]{2,1,0:T(2,128)} %bitcast.10), calls=%async_computation | async-start | bytes 65536 | tf_op jit(solution)/shard_map/all_to_all | solution.py:197
  813.8 7.7 collective-permute-start.187
  822.2 11.5 collective-permute-start.189
  823.5 10.2 collective-permute-start.188
  826.6 14.7 all-to-all-start.1
  833.8 7.7 collective-permute-start.191
  841.8 12.3 collective-permute-start.193
  843.1 11.0 collective-permute-start.192
  854.2 26.5 %collective-permute-start.195 = (f32[1,10,1,128]{3,2,1,0:T(1,128)S(1)}, f32[1,10,1,128]{3,2,1,0:T(1,128)S(1)}, u32[]{:S(2)}, u32[]{:S(2)}) collective-permute-start(f32[1,10,1,128]{3,2,1,0:T(1,128)S(1)} %get-tuple-element.144), channel_id=1, source_target_pairs={{1,0},{2,1},{3,2},{4,3},{5,4},{6,5},{7,6},{9,8},{10,9},{11,10},{12... | collective-permute-start | bytes 15368 | tf_op jit(solution)/shard_map/ppermute | solution.py:25
  855.5 25.2 %collective-permute-start.194 = (f32[1,10,1,128]{3,2,1,0:T(1,128)S(1)}, f32[1,10,1,128]{3,2,1,0:T(1,128)S(1)}, u32[]{:S(2)}, u32[]{:S(2)}) collective-permute-start(f32[1,10,1,128]{3,2,1,0:T(1,128)S(1)} %get-tuple-element.143), channel_id=1, source_target_pairs={{0,1},{1,2},{2,3},{3,4},{4,5},{5,6},{6,7},{8,9},{9,10},{10,11},{11... | collective-permute-start | bytes 15368 | tf_op jit(solution)/shard_map/ppermute | solution.py:22
  1148.0 7.2 collective-permute-start.259
  1444.8 7.3 collective-permute-start.331
  1446.1 7.3 collective-permute-start.330
  (362 other events, 2767.8 us)
where the time goes:
time: 1700 us; the launch traced here: 1670 us
  starting transfers between devices  1260 us (74%)
  waiting for transfers between devices  188 us (11%)
  local copies, waits for them, and re-layouts  139 us (8%)
  other arithmetic  77.2 us (5%)
    ppermute x192, starting transfers between devices, extended(): lax.ppermute(lax.slice_in_dim(block, block.shape[dim] - width, None, axis...  992 us
    ppermute x192, starting transfers between devices, extended(): lax.ppermute(lax.slice_in_dim(block, 0, width, axis=dim), axis, backward)  248 us
    ppermute x192, waiting for transfers between devices, extended(): lax.ppermute(lax.slice_in_dim(block, block.shape[dim] - width, None, axis...  186 us
    reshape x18, local copies, waits for them, and re-layouts, coarsen(): values.reshape(size_x // 2, 2, size_y // 2, 2, size_z // 2, 2)  107 us
    reduce_sum x20, other arithmetic, coarsen(): values.reshape(size_x // 2, 2, size_y // 2, 2, size_z // 2, 2)  41.7 us
  transfers between devices with their start and end apart: 386, of which 180 were waited for; matrix products, arithmetic and copies ran while one was open for 5% of the time, Pallas kernels for 0%

commit v1 on v0

v1 whole, which is shorter than its diff:
```python
import functools

import jax
import jax.numpy as jnp
from jax import lax
from jax.experimental import pallas as pl
from jax.experimental.pallas import tpu as pltpu
from jax.sharding import PartitionSpec as P

OMEGA = 0.8
KEEP = 0.2
VMEM_BYTES = 56 * 2**20

FR, MR, CR = 56, 64, 40
F_OWN, M_OWN = 12, 24
HALO_B, HALO_X = 6, 4
ROWS = 32


def ds(start, size):
    return pl.ds(start, size)


def lanes(shape):
    return lax.broadcasted_iota(jnp.int32, shape, 1)


def loop(count, body, unroll):
    if unroll >= count:
        for index in range(count):
            body(index)
        return

    def step(index, carry):
        body(index)
        return carry

    lax.fori_loop(0, count, step, 0, unroll=unroll)


def neighbours(src, kx, ky, kz, x, start, size, shift):
    rows = ds(start, size)
    center = src[x + 1, rows, :]
    total = kx[x, rows, :] * src[x, rows, :] + kx[x + 1, rows, :] * src[x + 2, rows, :]
    total = total + ky[x, rows, :] * src[x + 1, ds(start + 1, size), :]
    total = total + ky[x, ds(start - 1, size), :] * src[x + 1, ds(start - 1, size), :]
    face = kz[x, rows, :]
    total = total + face * pltpu.roll(center, 128 - shift, 1) + pltpu.roll(face * center, shift, 1)
    return center, total


def sweep(src, dst, coeffs, b, start, size, count, shift, unroll):
    kx, ky, kz, w = coeffs
    rows = ds(start, size)

    def body(x):
        center, total = neighbours(src, kx, ky, kz, x, start, size, shift)
        dst[x + 1, rows, :] = KEEP * center + w[x, rows, :] * (b[x, rows, :] + total)

    loop(count, body, unroll)


def scaled(dst, w, b, start, size, count, unroll):
    rows = ds(start, size)

    def body(x):
        dst[x + 1, rows, :] = w[x, rows, :] * b[x, rows, :]

    loop(count, body, unroll)


def zero_ends(buf, count):
    buf[0] = jnp.zeros(buf.shape[1:], jnp.float32)
    buf[count + 1] = jnp.zeros(buf.shape[1:], jnp.float32)


def seam(buf, count, start, size, fill):
    rows = ds(start, size)
    odd = lanes((size, 128)) % 2 == 1
    buf[0, rows, :] = jnp.where(odd, pltpu.roll(buf[count, rows, :], 1, 1), fill)
    buf[count + 1, rows, :] = jnp.where(odd, fill, pltpu.roll(buf[1, rows, :], 127, 1))


def packed_sweep(src, dst, coeffs, b, start, size, count, shift, unroll):
    sweep(src, dst, coeffs, b, start, size, count, shift, unroll)
    seam(dst, count, start, size, 0.0)


def halve_packed(src, tmp, dst, count):
    for i in range(count // 2):
        tmp[i, ds(8, 48), :] = src[2 * i, ds(8, 48), :] + src[2 * i + 1, ds(8, 48), :]
    low = lanes((24, 128)) % 4 < 2
    for i in range(count // 2):
        both = tmp[i, pl.ds(8, 24, stride=2), :] + tmp[i, pl.ds(9, 24, stride=2), :]
        both = both + jnp.where(low, pltpu.roll(both, 126, 1), pltpu.roll(both, 2, 1))
        dst[i, ds(8, 24), :] = both * 0.125


def middle_solve(own, below, above, mid, coarse, bufs, nx):
    m_b, m_a, m_c, m_res, m_tmp, c_b, c_a, c_c = bufs
    mkx, mky, mkz, mw, mdiag = mid
    count = nx // 4
    for i in range(count):
        m_b[i, ds(8, 16), :] = below(i)
        m_b[i, ds(24, 16), :] = own(i)
        m_b[i, ds(40, 16), :] = above(i)
    scaled(m_c, mw, m_b, 8, 48, count, count)
    seam(m_c, count, 8, 48, 0.0)
    packed_sweep(m_c, m_a, (mkx, mky, mkz, mw), m_b, 8, 48, count, 2, count)
    for i in range(count):
        center, total = neighbours(m_a, mkx, mky, mkz, i, 8, 48, 2)
        m_res[i, ds(8, 48), :] = m_b[i, ds(8, 48), :] + total - mdiag[i, ds(8, 48), :] * center
    halve_packed(m_res, m_tmp, c_b, count)
    half = count // 2
    scaled(c_a, coarse[3], c_b, 8, 24, half, half)
    seam(c_a, half, 8, 24, 0.0)
    packed_sweep(c_a, c_c, coarse, c_b, 8, 24, half, 4, half)
    packed_sweep(c_c, c_a, coarse, c_b, 8, 24, half, 4, half)
    packed_sweep(c_a, c_c, coarse, c_b, 8, 24, half, 4, half)
    for i in range(half):
        value = c_c[i + 1, ds(12, 16), :]
        m_tmp[i, pl.ds(16, 16, stride=2), :] = value
        m_tmp[i, pl.ds(17, 16, stride=2), :] = value
        for j in range(2):
            x = 2 * i + j + 1
            m_a[x, ds(16, 32), :] = m_a[x, ds(16, 32), :] + m_tmp[i, ds(16, 32), :]
    seam(m_a, count, 16, 32, 0.0)
    packed_sweep(m_a, m_c, (mkx, mky, mkz, mw), m_b, 16, 32, count, 2, count)
    packed_sweep(m_c, m_a, (mkx, mky, mkz, mw), m_b, 16, 32, count, 2, count)


def add_correction(x_buf, m_a, f_tmp, nx, unroll):
    count = nx // 4
    odd = lanes((24, 128)) % 2 == 1
    for i in range(count):
        value = m_a[i + 1, ds(20, 24), :]
        first = jnp.where(odd, pltpu.roll(value, 1, 1), value)
        second = jnp.where(odd, value, pltpu.roll(value, 127, 1))
        for part, slab in ((first, i), (second, i + count)):
            f_tmp[slab, pl.ds(4, 24, stride=2), :] = part
            f_tmp[slab, pl.ds(5, 24, stride=2), :] = part

    def body(i):
        value = f_tmp[i, ds(4, 48), :]
        for j in range(2):
            x = 2 * i + j + 1
            x_buf[x, ds(4, 48), :] = x_buf[x, ds(4, 48), :] + value

    loop(nx // 2, body, unroll)


def restricted(x_buf, coeffs, diag, b, f_tmp, outs, nx, unroll):
    kx, ky, kz, w = coeffs
    count = nx // 4

    def body(i):
        both = None
        for j in range(2):
            x = 2 * i + j
            center, total = neighbours(x_buf, kx, ky, kz, x, F_OWN, ROWS, 1)
            part = b[x, ds(F_OWN, ROWS), :] + total - diag[x] * center
            both = part if both is None else both + part
        f_tmp[i, ds(0, ROWS), :] = both

    loop(nx // 2, body, unroll)
    odd = lanes((16, 128)) % 2 == 1
    for i in range(count):
        first = f_tmp[i, pl.ds(0, 16, stride=2), :] + f_tmp[i, pl.ds(1, 16, stride=2), :]
        second = f_tmp[i + count, pl.ds(0, 16, stride=2), :] + f_tmp[i + count, pl.ds(1, 16, stride=2), :]
        value = 0.125 * jnp.where(
            odd, second + pltpu.roll(second, 1, 1), first + pltpu.roll(first, 127, 1)
        )
        for out in outs:
            out(i, value)


def gather_rhs(b_buf, b_own, below, above, nx):
    for x in range(nx):
        b_buf[x, ds(F_OWN, ROWS), :] = b_own[x]
        b_buf[x, ds(F_OWN - HALO_B, HALO_B), :] = below[ds(x * HALO_B, HALO_B), :]
        b_buf[x, ds(F_OWN + ROWS, HALO_B), :] = above[ds(x * HALO_B, HALO_B), :]


def message_writers(ups, downs, b1_own, base):
    def write(i, value):
        ups[ds(base + 16 * i, 16), :] = value
        downs[ds(base + 16 * i, 16), :] = value
        b1_own[i] = value

    return [write]


def message_part(ref, base):
    return lambda i: ref[ds(base + 16 * i, 16), :]


def begin_solve(b_buf, x_a, x_b, coeffs, diag, f_tmp, b_own, b1_own, up, down, nx, unroll):
    scaled(x_a, coeffs[3], b_buf, 8, 40, nx, unroll)
    sweep(x_a, x_b, coeffs, b_buf, 8, 40, nx, 1, unroll)
    base = nx * HALO_B
    restricted(x_b, coeffs, diag, b_buf, f_tmp, message_writers(up, down, b1_own, base), nx, unroll)
    for x in range(nx):
        b_own[x] = b_buf[x, ds(F_OWN, ROWS), :]
        up[ds(x * HALO_B, HALO_B), :] = b_buf[x, ds(F_OWN + ROWS - HALO_B, HALO_B), :]
        down[ds(x * HALO_B, HALO_B), :] = b_buf[x, ds(F_OWN, HALO_B), :]


def first_kernel(log, sto, per, bp, own, up, down, tmp):
    odd = lanes((16, 128)) % 2 == 1
    fields = (log, sto, per, bp.at[0], bp.at[1])
    for f, ref in enumerate(fields):
        for x in range(8):
            own[ds(f * 256 + x * 32, 32), :] = ref[x]
    for f in range(2):
        for x in range(8):
            up[ds(f * 64 + x * 8, 8), :] = fields[f][x, ds(24, 8), :]
            down[ds(f * 64 + x * 8, 8), :] = fields[f][x, ds(0, 8), :]
    for f in range(3):
        for x in range(8):
            up[ds(128 + f * 32 + x * 4, 4), :] = fields[f + 2][x, ds(28, 4), :]
            down[ds(128 + f * 32 + x * 4, 4), :] = fields[f + 2][x, ds(0, 4), :]
    for i in range(4):
        tmp[0, i] = log[2 * i] + log[2 * i + 1]
        tmp[1, i] = sto[2 * i] + sto[2 * i + 1]
    for i in range(4):
        first, second = (
            tmp[f, i, pl.ds(0, 16, stride=2), :] + tmp[f, i, pl.ds(1, 16, stride=2), :] for f in range(2)
        )
        value = 0.125 * jnp.where(
            odd, second + pltpu.roll(second, 1, 1), first + pltpu.roll(first, 127, 1)
        )
        own[ds(1280 + 16 * i, 16), :] = value
        up[ds(224 + 16 * i, 16), :] = value
        down[ds(224 + 16 * i, 16), :] = value


def faces(e, kx, ky, kz, count, size, shift, factor, unroll):
    top = lanes((size, 128)) >= 128 - shift

    def body(x):
        kx[x] = factor * e[x] * e[x + 1]
        center = e[x + 1]
        kz[x] = jnp.where(top, 0.0, factor * center * pltpu.roll(center, 128 - shift, 1))
        ky[x, ds(0, size - 8), :] = factor * e[x + 1, ds(0, size - 8), :] * e[x + 1, ds(1, size - 8), :]
        ky[x, ds(size - 8, 8), :] = jnp.zeros((8, 128), jnp.float32)

    loop(count, body, unroll)
    kx[count] = factor * e[count] * e[count + 1]


def diagonal(sto, kx, ky, kz, x, start, size, shift):
    rows = ds(start, size)
    face = kz[x, rows, :]
    total = sto + kx[x, rows, :] + kx[x + 1, rows, :] + ky[x, rows, :] + ky[x, ds(start - 1, size), :]
    return total + face + pltpu.roll(face, shift, 1)


def inside(size, own_start, own_size, first, last):
    row = lax.broadcasted_iota(jnp.int32, (size, 128), 0)
    return jnp.logical_and(
        jnp.logical_or(row >= own_start, jnp.logical_not(first)),
        jnp.logical_or(row < own_start + own_size, jnp.logical_not(last)),
    )


def second_kernel(nx, n_gy, unroll, *refs):
    tiles = nx // 8
    place = refs[0]
    owns, halos = refs[1 : 1 + tiles], refs[1 + tiles : 1 + 2 * tiles]
    (kx, ky, kz, w, diag, sto_out, d_one, bp_out, mkx, mky, mkz, mw, mdiag, ckx, cky, ckz, cw) = refs[
        1 + 2 * tiles : 18 + 2 * tiles
    ]
    b_own, b1_own, up, down = refs[18 + 2 * tiles : 22 + 2 * tiles]
    e, sto, per, bp0, bp1, x_a, x_b, b_buf, f_tmp, e_mid, s_mid, e_co, s_co, m_tmp, m_tmp2 = refs[22 + 2 * tiles :]
    gx, gy = place[0], place[1]
    first, last = gy == 0, gy == n_gy - 1
    for buf in (e, per, bp0, bp1, x_a, x_b):
        zero_ends(buf, nx)
    half, core = tiles // 2, gx % 2

    def tile_of(index):
        k, other = index % half, index // half
        return ((gx // 2 + half - k) % half) * 2 + (core + other) % 2

    blank = jnp.zeros((4, 128), jnp.float32)
    blank8 = jnp.zeros((8, 128), jnp.float32)
    keep_low = jnp.where(first, 0.0, 1.0)
    keep_high = jnp.where(last, 0.0, 1.0)
    for index in range(tiles):
        own, halo = owns[index], halos[index]
        base = tile_of(index) * 8

        def body(x, own=own, halo=halo, base=base):
            for f, buf in enumerate((e, sto, per, bp0, bp1)):
                slab = base + x + (0 if f == 1 else 1)
                buf[slab, ds(12, 32), :] = own[ds(f * 256 + x * 32, 32), :]
                if f < 2:
                    buf[slab, ds(4, 8), :] = halo[ds(f * 64 + x * 8, 8), :]
                    buf[slab, ds(44, 8), :] = halo[ds(288 + f * 64 + x * 8, 8), :]
                    buf[slab, ds(0, 4), :] = blank
                    buf[slab, ds(52, 4), :] = blank
                else:
                    at = 128 + (f - 2) * 32 + x * 4
                    buf[slab, ds(0, 8), :] = blank8
                    buf[slab, ds(48, 8), :] = blank8
                    buf[slab, ds(8, 4), :] = halo[ds(at, 4), :] * keep_low
                    buf[slab, ds(44, 4), :] = halo[ds(288 + at, 4), :] * keep_high

        for x in range(8):
            body(x)
    fine_inside = inside(FR, F_OWN, ROWS, first, last)

    def exps(x):
        e[x + 1] = jnp.where(fine_inside, jnp.exp(0.5 * e[x + 1]), 1.0)

    loop(nx, exps, unroll)
    e[0] = jnp.ones((FR, 128), jnp.float32)
    e[nx + 1] = jnp.ones((FR, 128), jnp.float32)
    faces(e, kx, ky, kz, nx, FR, 1, 1.0, unroll)
    win_inside = inside(48, F_OWN - 4, ROWS, first, last)

    def diagonals(x):
        value = diagonal(sto[x, ds(4, 48), :], kx, ky, kz, x, 4, 48, 1)
        w[x, ds(4, 48), :] = jnp.where(win_inside, OMEGA / value, 0.0)
        w[x, ds(0, 4), :] = blank
        w[x, ds(52, 4), :] = blank
        diag[x] = value[8:40]
        sto_out[x] = sto[x, ds(8, 40), :]

    loop(nx, diagonals, unroll)

    def changes(x):
        rows, plus, minus = ds(8, 40), ds(9, 40), ds(7, 40)
        kl, kr, kp, km, face = kx[x, rows, :], kx[x + 1, rows, :], ky[x, rows, :], ky[x, minus, :], kz[x, rows, :]
        c = per[x + 1, rows, :]
        weights = (
            kl * 0.5 * (c + per[x, rows, :]),
            kr * 0.5 * (c + per[x + 2, rows, :]),
            km * 0.5 * (c + per[x + 1, minus, :]),
            kp * 0.5 * (c + per[x + 1, plus, :]),
            face * 0.5 * (c + pltpu.roll(c, 127, 1)),
        )
        for t, bp in enumerate((bp0, bp1)):
            p = bp[x + 1, rows, :]
            total = weights[0] * (p - bp[x, rows, :]) + weights[1] * (p - bp[x + 2, rows, :])
            total = total + weights[2] * (p - bp[x + 1, minus, :]) + weights[3] * (p - bp[x + 1, plus, :])
            flux = weights[4] * (p - pltpu.roll(p, 127, 1))
            total = total + flux - pltpu.roll(flux, 1, 1)
            if t == 0:
                b_buf[x, rows, :] = -total
            else:
                d_one[x] = total

    loop(nx, changes, unroll)
    for x in range(10):
        bp_out[0, x] = bp0[gx * 8 + x]
        bp_out[1, x] = bp1[gx * 8 + x]

    count = nx // 4
    odd = lanes((16, 128)) % 2 == 1
    for index in range(tiles):
        own, halo = owns[index], halos[index]
        tile = tile_of(index)
        upper = tile >= half
        base = jnp.where(upper, tile - half, tile) * 4
        mask = odd == upper
        for i in range(4):
            for start, ref, at in ((8, halo, 224 + 16 * i), (24, own, 1280 + 16 * i), (40, halo, 512 + 16 * i)):
                value = ref[ds(at, 16), :]
                left, right = pltpu.roll(value, 127, 1), pltpu.roll(value, 1, 1)
                log_part, sto_part = jnp.where(odd, right, value), jnp.where(odd, value, left)
                rows = ds(start, 16)
                e_mid[base + i + 1, rows, :] = jnp.where(mask, log_part, e_mid[base + i + 1, rows, :])
                s_mid[base + i, rows, :] = jnp.where(mask, sto_part, s_mid[base + i, rows, :])
    for i in range(count):
        m_tmp2[i] = e_mid[i + 1]
    halve_packed(m_tmp2, m_tmp, e_co.at[pl.ds(1, count // 2)], count)
    halve_packed(s_mid, m_tmp, s_co, count)
    levels = (
        (e_mid, s_mid, mkx, mky, mkz, mw, mdiag, count, MR, M_OWN, 16, 2, 0.25),
        (e_co, s_co, ckx, cky, ckz, cw, None, count // 2, CR, 16, 8, 4, 0.0625),
    )
    for e_l, s_l, kx_l, ky_l, kz_l, w_l, diag_l, number, size, own_start, own_size, shift, factor in levels:
        ok = inside(size, own_start, own_size, first, last)
        row = lax.broadcasted_iota(jnp.int32, (size, 128), 0)
        ok = jnp.logical_and(ok, jnp.logical_and(row >= 8, row < size - 8))
        for i in range(number):
            e_l[i + 1] = jnp.where(ok, jnp.exp(0.5 * e_l[i + 1]), 1.0)
        seam(e_l, number, 0, size, 1.0)
        faces(e_l, kx_l, ky_l, kz_l, number, size, shift, factor, number)
        rows = ds(8, size - 16)
        edge = jnp.zeros((8, 128), jnp.float32)
        for i in range(number):
            value = diagonal(s_l[i, rows, :], kx_l, ky_l, kz_l, i, 8, size - 16, shift)
            w_l[i, rows, :] = jnp.where(ok[8 : size - 8], OMEGA / value, 0.0)
            w_l[i, ds(0, 8), :] = edge
            w_l[i, ds(size - 8, 8), :] = edge
            if diag_l is not None:
                diag_l[i, rows, :] = value
                diag_l[i, ds(0, 8), :] = edge
                diag_l[i, ds(size - 8, 8), :] = edge
    begin_solve(b_buf, x_a, x_b, (kx, ky, kz, w), diag, f_tmp, b_own, b1_own, up, down, nx, unroll)


def middle_kernel(nx, unroll, *refs):
    (kx, ky, kz, w, diag, mkx, mky, mkz, mw, mdiag, ckx, cky, ckz, cw) = refs[:14]
    b_own, b1_own, below, above, x_own, b1_out, up, down = refs[14:22]
    x_a, x_b, b_buf, f_tmp = refs[22:26]
    bufs = refs[26:]
    coeffs = (kx, ky, kz, w)
    zero_ends(x_a, nx)
    zero_ends(x_b, nx)
    base = nx * HALO_B
    middle_solve(
        lambda i: b1_own[i],
        message_part(below, base),
        message_part(above, base),
        (mkx, mky, mkz, mw, mdiag),
        (ckx, cky, ckz, cw),
        bufs,
        nx,
    )
    gather_rhs(b_buf, b_own, below, above, nx)
    scaled(x_a, w, b_buf, 4, 48, nx, unroll)
    sweep(x_a, x_b, coeffs, b_buf, 4, 48, nx, 1, unroll)
    add_correction(x_b, bufs[1], f_tmp, nx, unroll)
    sweep(x_b, x_a, coeffs, b_buf, 8, 40, nx, 1, unroll)
    sweep(x_a, x_b, coeffs, b_buf, 8, 40, nx, 1, unroll)
    sweep(x_b, x_a, coeffs, b_buf, 8, 40, nx, 1, unroll)
    sweep(x_a, x_b, coeffs, b_buf, 8, 40, nx, 1, unroll)
    base = nx * HALO_X
    restricted(x_b, coeffs, diag, b_buf, f_tmp, message_writers(up, down, b1_out, base), nx, unroll)
    for x in range(nx):
        x_own[x] = x_b[x + 1, ds(F_OWN, ROWS), :]
        up[ds(x * HALO_X, HALO_X), :] = x_b[x + 1, ds(F_OWN + ROWS - HALO_X, HALO_X), :]
        down[ds(x * HALO_X, HALO_X), :] = x_b[x + 1, ds(F_OWN, HALO_X), :]


def end_kernel(nx, n_gy, unroll, kind, *refs):
    place = refs[0]
    (kx, ky, kz, w, diag, mkx, mky, mkz, mw, mdiag, ckx, cky, ckz, cw) = refs[1:15]
    b_in, below_b, above_b, x_own, b1_in, below, above = refs[15:22]
    extra = {1: 2, 2: 1, 3: 3, 4: 2}[kind]
    extras, rest = refs[22 : 22 + extra], refs[22 + extra :]
    outs = {1: 5, 2: 5, 3: 5, 4: 1}[kind]
    outs, scratch = rest[:outs], rest[outs:]
    x_a, x_b, b_buf, f_tmp = scratch[:4]
    bufs = scratch[4:]
    coeffs = (kx, ky, kz, w)
    gx, gy = place[0], place[1]
    keep_low = jnp.where(gy == 0, 0.0, 1.0)
    keep_high = jnp.where(gy == n_gy - 1, 0.0, 1.0)
    zero_ends(x_a, nx)
    zero_ends(x_b, nx)
    base = nx * HALO_X
    middle_solve(
        lambda i: b1_in[i],
        message_part(below, base),
        message_part(above, base),
        (mkx, mky, mkz, mw, mdiag),
        (ckx, cky, ckz, cw),
        bufs,
        nx,
    )
    gather_rhs(b_buf, b_in, below_b, above_b, nx)
    for x in range(nx):
        x_a[x + 1, ds(F_OWN, ROWS), :] = x_own[x]
        x_a[x + 1, ds(F_OWN - HALO_X, HALO_X), :] = below[ds(x * HALO_X, HALO_X), :] * keep_low
        x_a[x + 1, ds(F_OWN + ROWS, HALO_X), :] = above[ds(x * HALO_X, HALO_X), :] * keep_high
    add_correction(x_a, bufs[1], f_tmp, nx, unroll)
    sweep(x_a, x_b, coeffs, b_buf, 8, 40, nx, 1, unroll)
    sweep(x_b, x_a, coeffs, b_buf, 8, 40, nx, 1, unroll)
    rows = ds(8, 40)
    if kind < 4:
        b_own, b1_own, up, down, kept = outs

        def body(x):
            value = x_a[x + 1, rows, :]
            if kind == 1:
                sto, d_one = extras
                b_buf[x, rows, :] = sto[x] * value - d_one[x]
            elif kind == 2:
                b_buf[x, rows, :] = extras[0][x] * value
            else:
                sto, source, change = extras
                b_buf[x, rows, :] = sto[x] * value + source[x] * change[x]
            if kind == 1:
                kept[x] = value
            elif kind == 3:
                kept[x + 1] = value

        loop(nx, body, unroll)
        if kind == 2:
            for x in range(8):
                kept[x] = x_a[gx * 8 + x + 1, ds(F_OWN, ROWS), :]
        if kind == 3:
            zero_ends(kept, nx)
        begin_solve(b_buf, x_a, x_b, coeffs, diag, f_tmp, b_own, b1_own, up, down, nx, unroll)
    else:
        lam_two, bp = extras
        own, plus, minus = ds(F_OWN, ROWS), ds(F_OWN + 1, ROWS), ds(F_OWN - 1, ROWS)
        for x in range(8):
            at = gx * 8 + x
            kl, kr, kp, km, face = kx[at, own, :], kx[at + 1, own, :], ky[at, own, :], ky[at, minus, :], kz[at, own, :]
            total = None
            for t, (lam, shift) in enumerate(((x_a, 0), (lam_two, 8))):
                low, mid, high = (ds(F_OWN - shift + step, ROWS) for step in (-1, 0, 1))
                p, v = bp[t, x + 1, own, :], lam[at + 1, mid, :]
                part = kl * (p - bp[t, x, own, :]) * (v - lam[at, mid, :])
                part = part + kr * (p - bp[t, x + 2, own, :]) * (v - lam[at + 2, mid, :])
                part = part + km * (p - bp[t, x + 1, minus, :]) * (v - lam[at + 1, low, :])
                part = part + kp * (p - bp[t, x + 1, plus, :]) * (v - lam[at + 1, high, :])
                flux = face * (p - pltpu.roll(p, 127, 1)) * (v - pltpu.roll(v, 127, 1))
                part = part + flux + pltpu.roll(flux, 1, 1)
                total = part if total is None else total + part
            outs[0][x] = -0.5 * total


def call(body, outs, scratch, args, scalars):
    f32 = jnp.float32
    vmem = pl.BlockSpec(memory_space=pltpu.VMEM)
    smem = pl.BlockSpec(memory_space=pltpu.SMEM)
    return pl.pallas_call(
        body,
        out_shape=[jax.ShapeDtypeStruct(s, f32) for s in outs],
        in_specs=[smem] * scalars + [vmem] * (len(args) - scalars),
        out_specs=[vmem] * len(outs),
        scratch_shapes=[pltpu.VMEM(s, f32) for s in scratch],
        compiler_params=pltpu.CompilerParams(vmem_limit_bytes=VMEM_BYTES),
    )(*args)


def cycle(count, step):
    return [(i, (i + step) % count) for i in range(count)]


def gathered(array, tiles):
    half = tiles // 2
    same = [array]
    for k in range(1, half):
        perm = [(2 * a + c, 2 * ((a + k) % half) + c) for a in range(half) for c in range(2)]
        same.append(lax.ppermute(array, "gx", perm))
    swap = [(i, i ^ 1) for i in range(tiles)]
    return same + [lax.ppermute(part, "gx", swap) for part in same]


def well_sources(rows, cells, counts, owners, starts, nx, n_gy):
    listed, samples = rows.shape
    steps = 2
    position = jnp.arange(samples, dtype=jnp.int32)
    counted = jnp.where(position[None, :] < counts[:, None], rows, 0.0)
    per_step = counted.reshape(listed, steps, samples // steps).sum(axis=2)
    weights = jnp.where(jnp.arange(steps, dtype=jnp.int32)[None, :] >= starts[:, None], per_step, 0.0)
    whole = jnp.stack([owners[:, 0], cells], axis=0)
    weights = lax.all_gather(weights.T, ("gx", "gy"), axis=1, tiled=True)
    whole = lax.all_gather(whole, ("gx", "gy"), axis=1, tiled=True)
    owner, cell = whole[0], whole[1]
    x = (owner // n_gy) * 8 + cell // (32 * 128)
    y = (owner % n_gy - lax.axis_index("gy")) * 32 + (cell // 128) % 32 + 4
    spot = jnp.where(jnp.logical_and(y >= 0, y < 40), x * 40 + y, -1)
    z = cell % 128
    total = spot.shape[0]
    chunk = 1024 if total % 1024 == 0 else total

    def part(spot, z, weights):
        left = (spot[None, :] == jnp.arange(nx * 40, dtype=jnp.int32)[:, None]).astype(jnp.float32)
        here = z[:, None] == jnp.arange(128, dtype=jnp.int32)[None, :]
        right = jnp.concatenate([jnp.where(here, weights[t][:, None], 0.0) for t in range(steps)], axis=1)
        return jnp.dot(left, right, precision=lax.Precision.HIGHEST)

    if total == chunk:
        source = part(spot, z, weights)
    else:

        def body(i, acc):
            cut = lambda a: lax.dynamic_slice_in_dim(a, i * chunk, chunk, axis=-1)
            return acc + part(cut(spot), cut(z), cut(weights))

        source = lax.fori_loop(0, total // chunk, body, jnp.zeros((nx * 40, steps * 128), jnp.float32))
    return [source[:, t * 128 : (t + 1) * 128].reshape(nx, 40, 128) for t in range(steps)]


def local(log_perm, perturb, storage, base_press, well_rows, well_cells, well_counts, well_owner, well_start):
    tiles, n_gy = lax.axis_size("gx"), lax.axis_size("gy")
    nx = 8 * tiles
    count, half = nx // 4, nx // 8
    unroll = 8
    up_perm, down_perm = cycle(n_gy, 1), cycle(n_gy, -1)

    def exchange(up, down):
        return lax.ppermute(up, "gy", up_perm), lax.ppermute(down, "gy", down_perm)

    place = jnp.stack([lax.axis_index("gx"), lax.axis_index("gy")]).astype(jnp.int32)
    own, up, down = call(
        first_kernel, [(1344, 128), (288, 128), (288, 128)], [(2, 4, 32, 128)], [log_perm, storage, perturb, base_press], 0
    )
    below, above = exchange(up, down)
    owns = gathered(own, tiles)
    halos = gathered(jnp.concatenate([below, above], axis=0), tiles)

    fine, fine_pad, mid, mid_pad = (nx, FR, 128), (nx + 2, FR, 128), (count, MR, 128), (count + 2, MR, 128)
    coarse, coarse_pad = (half, CR, 128), (half + 2, CR, 128)
    own_shape, window = (nx, ROWS, 128), (nx, 40, 128)
    b1_shape = (count, 16, 128)
    message_b, message_x = (nx * HALO_B + count * 16, 128), (nx * HALO_X + count * 16, 128)
    coeff_shapes = [(nx + 1, FR, 128), fine, fine, fine, own_shape]
    mid_shapes = [(count + 1, MR, 128), mid, mid, mid, mid]
    coarse_shapes = [(half + 1, CR, 128), coarse, coarse, coarse]
    outs = call(
        functools.partial(second_kernel, nx, n_gy, min(unroll, 4)),
        coeff_shapes
        + [window, window, (2, 10, FR, 128)]
        + mid_shapes
        + coarse_shapes
        + [own_shape, b1_shape, message_b, message_b],
        [fine_pad, fine, fine_pad, fine_pad, fine_pad, fine_pad, fine_pad, fine, (nx // 2, FR, 128)]
        + [mid_pad, mid, coarse_pad, coarse, mid, mid],
        [place] + owns + halos,
        1,
    )
    coeffs, (sto, d_one, bp) = outs[:5], outs[5:8]
    coeffs = list(coeffs) + list(outs[8:17])
    begun = outs[17:21]
    sources = well_sources(well_rows, well_cells, well_counts, well_owner, well_start, nx, n_gy)
    scratch = [fine_pad, fine_pad, fine, (nx // 2, FR, 128)]
    scratch += [mid, mid_pad, mid_pad, mid, mid, coarse, coarse_pad, coarse_pad]
    change = None
    for kind in (1, 2, 3, 4):
        b_own, b1_own, up, down = begun
        below_b, above_b = exchange(up, down)
        x_own, b1_mid, up, down = call(
            functools.partial(middle_kernel, nx, unroll),
            [own_shape, b1_shape, message_x, message_x],
            scratch,
            coeffs + [b_own, b1_own, below_b, above_b],
            0,
        )
        below, above = exchange(up, down)
        extras = {1: [sto, d_one], 2: [sources[1]], 3: [sto, sources[0], change], 4: []}[kind]
        begin_shapes = [own_shape, b1_shape, message_b, message_b]
        shapes = {
            1: begin_shapes + [window],
            2: begin_shapes + [(8, ROWS, 128)],
            3: begin_shapes + [(nx + 2, 40, 128)],
            4: [(8, ROWS, 128)],
        }[kind]
        if kind == 4:
            extras = [lam_two, bp]
        outs = call(
            functools.partial(end_kernel, nx, n_gy, unroll, kind),
            shapes,
            scratch,
            [place] + coeffs + [b_own, below_b, above_b, x_own, b1_mid, below, above] + extras,
            1,
        )
        if kind == 1:
            change = outs[4]
        elif kind == 2:
            final_change = outs[4]
        elif kind == 3:
            lam_two = outs[4]
        begun = outs[:4]
    return (outs[0], final_change)


def solution(mesh):
    return jax.shard_map(
        local,
        mesh=mesh,
        in_specs=(
            P("gx", "gy", None),
            P("gx", "gy", None),
            P("gx", "gy", None),
            P(None, "gx", "gy", None),
            P(("gx", "gy"), None),
            P(("gx", "gy")),
            P(("gx", "gy")),
            P(("gx", "gy"), None),
            P(("gx", "gy")),
        ),
        out_specs=(P("gx", "gy", None), P("gx", "gy", None)),
        check_vma=False,
    )
```

time: 1700 us -> 321 us (0.19); the launches traced: 1670 us -> 320 us
  starting transfers between devices: 1260 us -> 48.3 us
  waiting for transfers between devices: 188 us -> 37.7 us
  blocking collectives: 0 us -> 131 us
  local copies, waits for them, and re-layouts: 139 us -> 8.36 us
  Pallas kernels: 0 us -> 88.5 us
  other arithmetic: 77.2 us -> 2.89 us
    ppermute x384 -> x24, starting transfers between devices: 1240 us -> 48.3 us  [the longest x9 35.8 us: exchange(): lax.ppermute(down, 'gy', down_perm)]
    ppermute x384 -> x24, waiting for transfers between devices: 187 us -> 37.7 us  [the longest x9 27.1 us: exchange(): lax.ppermute(up, 'gy', up_perm)]
    all_gather x0 -> x2, blocking collectives: none -> 131 us  [the longest x1 67.7 us: well_sources(): whole = lax.all_gather(whole, ('gx', 'gy'), axis=1, tiled=True)]
    reshape x50 -> x1, local copies, waits for them, and re-layouts: 111 us -> 0.04 us  [well_sources(): per_step = counted.reshape(listed, steps, samples // steps).sum(axis=2)]
    pallas_call x0 -> x10, Pallas kernels: none -> 88.5 us  [call(): pl.pallas_call(body, out_shape=[jax.ShapeDtypeStruct(s, f32) for s in out...]
    reduce_sum x22 -> x1, other arithmetic: 42.1 us -> 0.11 us  [well_sources(): per_step = counted.reshape(listed, steps, samples // steps).sum(axis=2)]
    slice x129 -> x2, local copies, waits for them, and re-layouts: 21.3 us -> 1.14 us  [the longest x1 1.14 us: well_sources(): source[:, t * 128:(t + 1) * 128].reshape(nx, 40, 128)]
    all_to_all x2 -> x0, starting transfers between devices: 19.7 us -> none  [the longest x1 12.8 us: local(): lax.all_to_all(send_ints, ('gx', 'gy'), split_axis=0, concat_axis=0, tile...]
  transfers between devices with their start and end apart: 386 -> 24, of which waited for: 180 -> 18; matrix products, arithmetic and copies ran while one was open for 5% -> 2% of each run, Pallas kernels for 0% -> 0%
where the time goes in v1:
time: 321 us; the launch traced here: 320 us
  blocking collectives  131 us (41%)
  Pallas kernels  88.5 us (28%)
  starting transfers between devices  48.3 us (15%)
  waiting for transfers between devices  37.7 us (12%)
  local copies, waits for them, and re-layouts  8.36 us (3%)
    pallas_call x10, Pallas kernels, call(): pl.pallas_call(body, out_shape=[jax.ShapeDtypeStruct(s, f32) for s in out...  88.5 us
    all_gather x1, blocking collectives, well_sources(): whole = lax.all_gather(whole, ('gx', 'gy'), axis=1, tiled=True)  67.7 us
    all_gather x1, blocking collectives, well_sources(): weights = lax.all_gather(weights.T, ('gx', 'gy'), axis=1, tiled=True)  63.4 us
    ppermute x9, starting transfers between devices, exchange(): lax.ppermute(down, 'gy', down_perm)  35.8 us
    ppermute x9, waiting for transfers between devices, exchange(): lax.ppermute(up, 'gy', up_perm)  27.1 us
    ppermute x9, starting transfers between devices, exchange(): lax.ppermute(up, 'gy', up_perm)  7.16 us
    unnamed x54, local copies, waits for them, and re-layouts  7.15 us
  transfers between devices with their start and end apart: 24, of which 18 were waited for; matrix products, arithmetic and copies ran while one was open for 2% of the time, Pallas kernels for 0%

profile of v1, /device:TPU:0, one launch (start us, length us, event | category | flops | bytes accessed | tf_op | source)
XLA Modules:
  0.0 320.2 jit_solution(12563405589383720635)
XLA Ops:
  0.7 2.2 shard_map.104
  2.8 3.0 collective-permute-start
  7.3 3.2 %collective-permute-start.4 = (f32[288,128]{1,0:T(8,128)}, f32[288,128]{1,0:T(8,128)S(1)}, u32[]{:S(2)}, u32[]{:S(2)}) collective-permute-start(f32[288,128]{1,0:T(8,128)} %get-tuple-element.59), channel_id=1, source_target_pairs={{0,7},{1,0},{2,1},{3,2},{4,3},{5,4},{6,5},{7,6},{8,15},{9,8},{10,9... | collective-permute-start | bytes 442376 | tf_op jit(solution)/shard_map/ppermute | solution.py:591
  12.3 2.8 collective-permute-done.3
  15.2 6.3 %collective-permute-done.refs_2_ = f32[1344,128]{1,0:T(8,128)S(1)} collective-permute-done((f32[1344,128]{1,0:T(8,128)}, f32[1344,128]{1,0:T(8,128)S(1)}, u32[]{:S(2)}, u32[]{:S(2)}) %collective-permute-start) | collective-permute-done | bytes 688160 | tf_op jit(solution)/shard_map/ppermute | solution.py:542
  23.3 67.7 %all-gather = s32[32,32,2]{1,2,0:T(2,128)S(1)} all-gather(s32[1,32,2]{1,2,0:T(2,128)S(1)} %add_bitcast_fusion), channel_id=1, replica_groups=mesh['gx'=4,'gy'=8] {'gx','gy'}, dimensions={0}, use_global_device_ids=true | all-gather | bytes 8448 | tf_op jit(solution)/shard_map/all_gather | solution.py:556
  91.1 63.4 %all-gather.1 = f32[32,32,2]{1,2,0:T(2,128)S(1)} all-gather(f32[1,32,2]{1,2,0:T(2,128)S(1)} %bitcast.34), channel_id=1, replica_groups=mesh['gx'=4,'gy'=8] {'gx','gy'}, dimensions={0}, use_global_device_ids=true | all-gather | bytes 8448 | tf_op jit(solution)/shard_map/all_gather | solution.py:555
  158.4 12.2 %shard_map.105 = (f32[33,56,128]{2,1,0:T(8,128)}, f32[32,56,128]{2,1,0:T(8,128)}, f32[32,56,128]{2,1,0:T(8,128)}, f32[32,56,128]{2,1,0:T(8,128)}, f32[32,32,128]...) custom-call(s32[2]{0:T(128)} %pad_add_fusion.refs_0_, ...), custom_call_target="tpu_custom_call" | custom-call | tf_op jit(solution)/shard_map/pallas_call | solution.py:523
  170.5 2.3 collective-permute-start.8
  172.9 2.5 collective-permute-start.9
  175.3 5.1 %collective-permute-done.8.refs_16_ = f32[320,128]{1,0:T(8,128)S(1)} collective-permute-done((f32[320,128]{1,0:T(8,128)}, f32[320,128]{1,0:T(8,128)S(1)}, u32[]{:S(2)}, u32[]{:S(2)}) %collective-permute-start.8) | collective-permute-done | bytes 163872 | tf_op jit(solution)/shard_map/ppermute | solution.py:591
  183.2 9.8 %shard_map.106 = (f32[32,32,128]{2,1,0:T(8,128)}, f32[8,16,128]{2,1,0:T(8,128)}, f32[256,128]{1,0:T(8,128)}, f32[256,128]{1,0:T(8,128)}) custom-call(f32[33,56,128]{2,1,0:T(8,128)} %get-tuple-element.60.refs_0_.refs_1_, f32[32,56,128]{2,1,0:T(8,128)} %get-tuple-element.61.refs_1_.refs_2_, f32[32,56,128]{2,1,0:T(8,128)} %get-tuple-element.62.refs_2_.refs_3_, ...), custom_call_target="tpu_custom_call" | custom-call | tf_op jit(solution)/shard_map/pallas_call | solution.py:523
  193.4 4.4 %collective-permute-start.11 = (f32[256,128]{1,0:T(8,128)}, f32[256,128]{1,0:T(8,128)S(1)}, u32[]{:S(2)}, u32[]{:S(2)}) collective-permute-start(f32[256,128]{1,0:T(8,128)} %get-tuple-element.81), channel_id=1, source_target_pairs={{0,7},{1,0},{2,1},{3,2},{4,3},{5,4},{6,5},{7,6},{8,15},{9,8},{10,9... | collective-permute-start | bytes 393224 | tf_op jit(solution)/shard_map/ppermute | solution.py:591
  198.3 2.7 collective-permute-done.10.refs_20_
  202.0 9.1 %shard_map.107 = (f32[32,32,128]{2,1,0:T(8,128)}, f32[8,16,128]{2,1,0:T(8,128)}, f32[320,128]{1,0:T(8,128)}, f32[320,128]{1,0:T(8,128)}, f32[32,40,128]{2,1,0:T(8,128)}) custom-call(s32[2]{0:T(128)} %pad_add_fusion.refs_0_, f32[33,56,128]{2,1,0:T(8,128)} %get-tuple-element.60.refs_0_.refs_1_, f32[32,56,128]{2,1,0:T(8,128)} %get-tuple-element.61.refs_1_.refs_2_, ...), custom_call_target="tpu_custom_call" | custom-call | tf_op jit(solution)/shard_map/pallas_call | solution.py:523
  211.2 4.7 %collective-permute-start.13 = (f32[320,128]{1,0:T(8,128)}, f32[320,128]{1,0:T(8,128)S(1)}, u32[]{:S(2)}, u32[]{:S(2)}) collective-permute-start(f32[320,128]{1,0:T(8,128)} %get-tuple-element.86), channel_id=1, source_target_pairs={{0,7},{1,0},{2,1},{3,2},{4,3},{5,4},{6,5},{7,6},{8,15},{9,8},{10,9... | collective-permute-start | bytes 491528 | tf_op jit(solution)/shard_map/ppermute | solution.py:591
  216.0 2.6 fusion
  220.5 9.8 %shard_map.108 = (f32[32,32,128]{2,1,0:T(8,128)}, f32[8,16,128]{2,1,0:T(8,128)}, f32[256,128]{1,0:T(8,128)}, f32[256,128]{1,0:T(8,128)}) custom-call(f32[33,56,128]{2,1,0:T(8,128)} %get-tuple-element.60.refs_0_.refs_1_, f32[32,56,128]{2,1,0:T(8,128)} %get-tuple-element.61.refs_1_.refs_2_, f32[32,56,128]{2,1,0:T(8,128)} %get-tuple-element.62.refs_2_.refs_3_, ...), custom_call_target="tpu_custom_call" | custom-call | tf_op jit(solution)/shard_map/pallas_call | solution.py:523
  230.4 4.7 %collective-permute-start.15 = (f32[256,128]{1,0:T(8,128)}, f32[256,128]{1,0:T(8,128)S(1)}, u32[]{:S(2)}, u32[]{:S(2)}) collective-permute-start(f32[256,128]{1,0:T(8,128)} %get-tuple-element.91), channel_id=1, source_target_pairs={{0,7},{1,0},{2,1},{3,2},{4,3},{5,4},{6,5},{7,6},{8,15},{9,8},{10,9... | collective-permute-start | bytes 393224 | tf_op jit(solution)/shard_map/ppermute | solution.py:591
  238.9 8.7 %shard_map.109 = (f32[32,32,128]{2,1,0:T(8,128)}, f32[8,16,128]{2,1,0:T(8,128)}, f32[320,128]{1,0:T(8,128)}, f32[320,128]{1,0:T(8,128)}, f32[8,32,128]{2,1,0:T(8,128)}) custom-call(s32[2]{0:T(128)} %pad_add_fusion.refs_0_, f32[33,56,128]{2,1,0:T(8,128)} %get-tuple-element.60.refs_0_.refs_1_, f32[32,56,128]{2,1,0:T(8,128)} %get-tuple-element.61.refs_1_.refs_2_, ...), custom_call_target="tpu_custom_call" | custom-call | tf_op jit(solution)/shard_map/pallas_call | solution.py:523
  247.9 4.6 %collective-permute-start.17 = (f32[320,128]{1,0:T(8,128)}, f32[320,128]{1,0:T(8,128)S(1)}, u32[]{:S(2)}, u32[]{:S(2)}) collective-permute-start(f32[320,128]{1,0:T(8,128)} %get-tuple-element.94), channel_id=1, source_target_pairs={{0,7},{1,0},{2,1},{3,2},{4,3},{5,4},{6,5},{7,6},{8,15},{9,8},{10,9... | collective-permute-start | bytes 491528 | tf_op jit(solution)/shard_map/ppermute | solution.py:591
  252.5 3.6 %collective-permute-done.16.refs_16_ = f32[320,128]{1,0:T(8,128)S(1)} collective-permute-done((f32[320,128]{1,0:T(8,128)}, f32[320,128]{1,0:T(8,128)S(1)}, u32[]{:S(2)}, u32[]{:S(2)}) %collective-permute-start.16) | collective-permute-done | bytes 163872 | tf_op jit(solution)/shard_map/ppermute | solution.py:591
  256.9 9.8 %shard_map.110 = (f32[32,32,128]{2,1,0:T(8,128)}, f32[8,16,128]{2,1,0:T(8,128)}, f32[256,128]{1,0:T(8,128)}, f32[256,128]{1,0:T(8,128)}) custom-call(f32[33,56,128]{2,1,0:T(8,128)} %get-tuple-element.60.refs_0_.refs_1_, f32[32,56,128]{2,1,0:T(8,128)} %get-tuple-element.61.refs_1_.refs_2_, f32[32,56,128]{2,1,0:T(8,128)} %get-tuple-element.62.refs_2_.refs_3_, ...), custom_call_target="tpu_custom_call" | custom-call | tf_op jit(solution)/shard_map/pallas_call | solution.py:523
  267.5 4.0 %collective-permute-start.19 = (f32[256,128]{1,0:T(8,128)}, f32[256,128]{1,0:T(8,128)S(1)}, u32[]{:S(2)}, u32[]{:S(2)}) collective-permute-start(f32[256,128]{1,0:T(8,128)} %get-tuple-element.99), channel_id=1, source_target_pairs={{0,7},{1,0},{2,1},{3,2},{4,3},{5,4},{6,5},{7,6},{8,15},{9,8},{10,9... | collective-permute-start | bytes 393224 | tf_op jit(solution)/shard_map/ppermute | solution.py:591
  271.5 3.2 collective-permute-done.18.refs_20_
  275.3 9.4 %shard_map.111 = (f32[32,32,128]{2,1,0:T(8,128)}, f32[8,16,128]{2,1,0:T(8,128)}, f32[320,128]{1,0:T(8,128)}, f32[320,128]{1,0:T(8,128)}, f32[34,40,128]{2,1,0:T(8,128)}) custom-call(s32[2]{0:T(128)} %pad_add_fusion.refs_0_, f32[33,56,128]{2,1,0:T(8,128)} %get-tuple-element.60.refs_0_.refs_1_, f32[32,56,128]{2,1,0:T(8,128)} %get-tuple-element.61.refs_1_.refs_2_, ...), custom_call_target="tpu_custom_call" | custom-call | tf_op jit(solution)/shard_map/pallas_call | solution.py:523
  285.6 4.1 %collective-permute-start.21 = (f32[320,128]{1,0:T(8,128)}, f32[320,128]{1,0:T(8,128)S(1)}, u32[]{:S(2)}, u32[]{:S(2)}) collective-permute-start(f32[320,128]{1,0:T(8,128)} %get-tuple-element.103), channel_id=1, source_target_pairs={{0,7},{1,0},{2,1},{3,2},{4,3},{5,4},{6,5},{7,6},{8,15},{9,8},{10,9... | collective-permute-start | bytes 491528 | tf_op jit(solution)/shard_map/ppermute | solution.py:591
  289.7 3.4 %collective-permute-done.20.refs_16_ = f32[320,128]{1,0:T(8,128)S(1)} collective-permute-done((f32[320,128]{1,0:T(8,128)}, f32[320,128]{1,0:T(8,128)S(1)}, u32[]{:S(2)}, u32[]{:S(2)}) %collective-permute-start.20) | collective-permute-done | bytes 163872 | tf_op jit(solution)/shard_map/ppermute | solution.py:591
  294.1 9.8 %shard_map.112 = (f32[32,32,128]{2,1,0:T(8,128)}, f32[8,16,128]{2,1,0:T(8,128)}, f32[256,128]{1,0:T(8,128)}, f32[256,128]{1,0:T(8,128)}) custom-call(f32[33,56,128]{2,1,0:T(8,128)} %get-tuple-element.60.refs_0_.refs_1_, f32[32,56,128]{2,1,0:T(8,128)} %get-tuple-element.61.refs_1_.refs_2_, f32[32,56,128]{2,1,0:T(8,128)} %get-tuple-element.62.refs_2_.refs_3_, ...), custom_call_target="tpu_custom_call" | custom-call | tf_op jit(solution)/shard_map/pallas_call | solution.py:523
  304.9 3.8 %collective-permute-start.23 = (f32[256,128]{1,0:T(8,128)}, f32[256,128]{1,0:T(8,128)S(1)}, u32[]{:S(2)}, u32[]{:S(2)}) collective-permute-start(f32[256,128]{1,0:T(8,128)} %get-tuple-element.108), channel_id=1, source_target_pairs={{0,7},{1,0},{2,1},{3,2},{4,3},{5,4},{6,5},{7,6},{8,15},{9,8},{10,9... | collective-permute-start | bytes 393224 | tf_op jit(solution)/shard_map/ppermute | solution.py:591
  308.7 3.3 %collective-permute-done.22.refs_20_ = f32[256,128]{1,0:T(8,128)S(1)} collective-permute-done((f32[256,128]{1,0:T(8,128)}, f32[256,128]{1,0:T(8,128)S(1)}, u32[]{:S(2)}, u32[]{:S(2)}) %collective-permute-start.22) | collective-permute-done | bytes 131104 | tf_op jit(solution)/shard_map/ppermute | solution.py:591
  312.6 7.6 %shard_map.113 = f32[8,32,128]{2,1,0:T(8,128)} custom-call(s32[2]{0:T(128)} %pad_add_fusion.refs_0_, f32[33,56,128]{2,1,0:T(8,128)} %get-tuple-element.60.refs_0_.refs_1_, f32[32,56,128]{2,1,0:T(8,128)} %get-tuple-element.61.refs_1_.refs_2_, f32[32,56,128]{2,1,0:T(8,128)} %get-tuple-element.62.refs_2_.refs_3_, ...), custom_call_target="tpu_custom_call" | custom-call | tf_op jit(solution)/shard_map/pallas_call | solution.py:523
  (97 shorter events, 25.8 us)
Async XLA Ops:
  0.6 22.7 %copy-start.24 = (s32[32,1]{0,1:T(1,128)S(1)}, s32[32,1]{0,1:T(1,128)}, u32[]{:S(2)}) copy-start(s32[32,1]{0,1:T(1,128)} %param.16) | copy-start | bytes 388
  0.6 22.7 %copy-start.23 = (s32[32]{0:T(128)S(1)}, s32[32]{0:T(128)}, u32[]{:S(2)}) copy-start(s32[32]{0:T(128)} %param.14) | copy-start | bytes 388
  2.8 18.6 %collective-permute-start = (f32[1344,128]{1,0:T(8,128)}, f32[1344,128]{1,0:T(8,128)S(1)}, u32[]{:S(2)}, u32[]{:S(2)}) collective-permute-start(f32[1344,128]{1,0:T(8,128)} %get-tuple-element.57.refs_1_), channel_id=1, source_target_pairs={{0,16},{8,24},{16,0},{24,8},{1,17},{9,25},{17,1},{25,9},{2,18},{10... | collective-permute-start | bytes 2064392 | tf_op jit(solution)/shard_map/ppermute | solution.py:542
  5.8 150.6 %collective-permute-start.1 = (f32[1344,128]{1,0:T(8,128)}, f32[1344,128]{1,0:T(8,128)S(1)}, u32[]{:S(2)}, u32[]{:S(2)}) collective-permute-start(f32[1344,128]{1,0:T(8,128)} %get-tuple-element.57.refs_1_), channel_id=1, source_target_pairs={{0,8},{8,0},{16,24},{24,16},{1,9},{9,1},{17,25},{25,17},{2,10},{10... | collective-permute-start | bytes 2064392 | tf_op jit(solution)/shard_map/ppermute | solution.py:544
  5.8 9.4 %collective-permute-start.3 = (f32[288,128]{1,0:T(8,128)}, f32[288,128]{1,0:T(8,128)S(1)}, u32[]{:S(2)}, u32[]{:S(2)}) collective-permute-start(f32[288,128]{1,0:T(8,128)} %get-tuple-element.58), channel_id=1, source_target_pairs={{0,1},{1,2},{2,3},{3,4},{4,5},{5,6},{6,7},{7,0},{8,9},{9,10},{10,1... | collective-permute-start | bytes 442376 | tf_op jit(solution)/shard_map/ppermute | solution.py:591
  7.3 14.2 %collective-permute-start.4 = (f32[288,128]{1,0:T(8,128)}, f32[288,128]{1,0:T(8,128)S(1)}, u32[]{:S(2)}, u32[]{:S(2)}) collective-permute-start(f32[288,128]{1,0:T(8,128)} %get-tuple-element.59), channel_id=1, source_target_pairs={{0,7},{1,0},{2,1},{3,2},{4,3},{5,4},{6,5},{7,6},{8,15},{9,8},{10,9... | collective-permute-start | bytes 442376 | tf_op jit(solution)/shard_map/ppermute | solution.py:591
  21.5 135.4 %copy-start = (f32[1344,128]{1,0:T(8,128)}, f32[1344,128]{1,0:T(8,128)S(1)}, u32[]{:S(2)}) copy-start(f32[1344,128]{1,0:T(8,128)S(1)} %collective-permute-done.refs_2_) | copy-start | bytes 2064388
  21.5 135.4 %collective-permute-start.2 = (f32[1344,128]{1,0:T(8,128)S(1)}, f32[1344,128]{1,0:T(8,128)S(1)}, u32[]{:S(2)}, u32[]{:S(2)}) collective-permute-start(f32[1344,128]{1,0:T(8,128)S(1)} %collective-permute-done.refs_2_), channel_id=1, source_target_pairs={{0,8},{8,0},{16,24},{24,16},{1,9},{9,1},{17,25},{25,17},{2,10},{10... | collective-permute-start | bytes 2064392 | tf_op jit(solution)/shard_map/ppermute | solution.py:544
  21.5 135.3 %copy-start.3 = (f32[576,128]{1,0:T(8,128)}, f32[576,128]{1,0:T(8,128)S(1)}, u32[]{:S(2)}) copy-start(f32[576,128]{1,0:T(8,128)S(1)} %constant_dynamic-update-slice_fusion.refs_5_) | copy-start | bytes 884740
  21.5 133.3 %collective-permute-start.5 = (f32[576,128]{1,0:T(8,128)S(1)}, f32[576,128]{1,0:T(8,128)S(1)}, u32[]{:S(2)}, u32[]{:S(2)}) collective-permute-start(f32[576,128]{1,0:T(8,128)S(1)} %constant_dynamic-update-slice_fusion.refs_5_), channel_id=1, source_target_pairs={{0,16},{8,24},{16,0},{24,8},{1,17},{9,25},{17,1},{25,9},{2,18},{10... | collective-permute-start | bytes 884744 | tf_op jit(solution)/shard_map/ppermute | solution.py:542
  154.7 1.6 collective-permute-start.6
  154.8 2.0 copy-start.12
  154.8 2.0 collective-permute-start.7
  156.4 1.0 copy-start.1
  157.5 0.9 copy-start.2
  170.5 9.9 %collective-permute-start.8 = (f32[320,128]{1,0:T(8,128)}, f32[320,128]{1,0:T(8,128)S(1)}, u32[]{:S(2)}, u32[]{:S(2)}) collective-permute-start(f32[320,128]{1,0:T(8,128)} %get-tuple-element.75), channel_id=1, source_target_pairs={{0,1},{1,2},{2,3},{3,4},{4,5},{5,6},{6,7},{7,0},{8,9},{9,10},{10,1... | collective-permute-start | bytes 491528 | tf_op jit(solution)/shard_map/ppermute | solution.py:591
  172.9 9.7 %collective-permute-start.9 = (f32[320,128]{1,0:T(8,128)}, f32[320,128]{1,0:T(8,128)S(1)}, u32[]{:S(2)}, u32[]{:S(2)}) collective-permute-start(f32[320,128]{1,0:T(8,128)} %get-tuple-element.76), channel_id=1, source_target_pairs={{0,7},{1,0},{2,1},{3,2},{4,3},{5,4},{6,5},{7,6},{8,15},{9,8},{10,9... | collective-permute-start | bytes 491528 | tf_op jit(solution)/shard_map/ppermute | solution.py:591
  180.4 2.1 copy-start.6
  193.0 7.9 %collective-permute-start.10 = (f32[256,128]{1,0:T(8,128)}, f32[256,128]{1,0:T(8,128)S(1)}, u32[]{:S(2)}, u32[]{:S(2)}) collective-permute-start(f32[256,128]{1,0:T(8,128)} %get-tuple-element.80), channel_id=1, source_target_pairs={{0,1},{1,2},{2,3},{3,4},{4,5},{5,6},{6,7},{7,0},{8,9},{9,10},{10,1... | collective-permute-start | bytes 393224 | tf_op jit(solution)/shard_map/ppermute | solution.py:591
  193.4 8.0 %collective-permute-start.11 = (f32[256,128]{1,0:T(8,128)}, f32[256,128]{1,0:T(8,128)S(1)}, u32[]{:S(2)}, u32[]{:S(2)}) collective-permute-start(f32[256,128]{1,0:T(8,128)} %get-tuple-element.81), channel_id=1, source_target_pairs={{0,7},{1,0},{2,1},{3,2},{4,3},{5,4},{6,5},{7,6},{8,15},{9,8},{10,9... | collective-permute-start | bytes 393224 | tf_op jit(solution)/shard_map/ppermute | solution.py:591
  211.2 8.4 %collective-permute-start.12 = (f32[320,128]{1,0:T(8,128)}, f32[320,128]{1,0:T(8,128)S(1)}, u32[]{:S(2)}, u32[]{:S(2)}) collective-permute-start(f32[320,128]{1,0:T(8,128)} %get-tuple-element.85), channel_id=1, source_target_pairs={{0,1},{1,2},{2,3},{3,4},{4,5},{5,6},{6,7},{7,0},{8,9},{9,10},{10,1... | collective-permute-start | bytes 491528 | tf_op jit(solution)/shard_map/ppermute | solution.py:591
  211.2 8.6 %collective-permute-start.13 = (f32[320,128]{1,0:T(8,128)}, f32[320,128]{1,0:T(8,128)S(1)}, u32[]{:S(2)}, u32[]{:S(2)}) collective-permute-start(f32[320,128]{1,0:T(8,128)} %get-tuple-element.86), channel_id=1, source_target_pairs={{0,7},{1,0},{2,1},{3,2},{4,3},{5,4},{6,5},{7,6},{8,15},{9,8},{10,9... | collective-permute-start | bytes 491528 | tf_op jit(solution)/shard_map/ppermute | solution.py:591
  230.3 7.9 %collective-permute-start.14 = (f32[256,128]{1,0:T(8,128)}, f32[256,128]{1,0:T(8,128)S(1)}, u32[]{:S(2)}, u32[]{:S(2)}) collective-permute-start(f32[256,128]{1,0:T(8,128)} %get-tuple-element.90), channel_id=1, source_target_pairs={{0,1},{1,2},{2,3},{3,4},{4,5},{5,6},{6,7},{7,0},{8,9},{9,10},{10,1... | collective-permute-start | bytes 393224 | tf_op jit(solution)/shard_map/ppermute | solution.py:591
  230.4 7.8 %collective-permute-start.15 = (f32[256,128]{1,0:T(8,128)}, f32[256,128]{1,0:T(8,128)S(1)}, u32[]{:S(2)}, u32[]{:S(2)}) collective-permute-start(f32[256,128]{1,0:T(8,128)} %get-tuple-element.91), channel_id=1, source_target_pairs={{0,7},{1,0},{2,1},{3,2},{4,3},{5,4},{6,5},{7,6},{8,15},{9,8},{10,9... | collective-permute-start | bytes 393224 | tf_op jit(solution)/shard_map/ppermute | solution.py:591
  247.7 8.4 %collective-permute-start.16 = (f32[320,128]{1,0:T(8,128)}, f32[320,128]{1,0:T(8,128)S(1)}, u32[]{:S(2)}, u32[]{:S(2)}) collective-permute-start(f32[320,128]{1,0:T(8,128)} %get-tuple-element.93), channel_id=1, source_target_pairs={{0,1},{1,2},{2,3},{3,4},{4,5},{5,6},{6,7},{7,0},{8,9},{9,10},{10,1... | collective-permute-start | bytes 491528 | tf_op jit(solution)/shard_map/ppermute | solution.py:591
  247.9 8.4 %collective-permute-start.17 = (f32[320,128]{1,0:T(8,128)}, f32[320,128]{1,0:T(8,128)S(1)}, u32[]{:S(2)}, u32[]{:S(2)}) collective-permute-start(f32[320,128]{1,0:T(8,128)} %get-tuple-element.94), channel_id=1, source_target_pairs={{0,7},{1,0},{2,1},{3,2},{4,3},{5,4},{6,5},{7,6},{8,15},{9,8},{10,9... | collective-permute-start | bytes 491528 | tf_op jit(solution)/shard_map/ppermute | solution.py:591
  266.7 7.9 %collective-permute-start.18 = (f32[256,128]{1,0:T(8,128)}, f32[256,128]{1,0:T(8,128)S(1)}, u32[]{:S(2)}, u32[]{:S(2)}) collective-permute-start(f32[256,128]{1,0:T(8,128)} %get-tuple-element.98), channel_id=1, source_target_pairs={{0,1},{1,2},{2,3},{3,4},{4,5},{5,6},{6,7},{7,0},{8,9},{9,10},{10,1... | collective-permute-start | bytes 393224 | tf_op jit(solution)/shard_map/ppermute | solution.py:591
  267.5 7.1 %collective-permute-start.19 = (f32[256,128]{1,0:T(8,128)}, f32[256,128]{1,0:T(8,128)S(1)}, u32[]{:S(2)}, u32[]{:S(2)}) collective-permute-start(f32[256,128]{1,0:T(8,128)} %get-tuple-element.99), channel_id=1, source_target_pairs={{0,7},{1,0},{2,1},{3,2},{4,3},{5,4},{6,5},{7,6},{8,15},{9,8},{10,9... | collective-permute-start | bytes 393224 | tf_op jit(solution)/shard_map/ppermute | solution.py:591
  284.7 8.4 %collective-permute-start.20 = (f32[320,128]{1,0:T(8,128)}, f32[320,128]{1,0:T(8,128)S(1)}, u32[]{:S(2)}, u32[]{:S(2)}) collective-permute-start(f32[320,128]{1,0:T(8,128)} %get-tuple-element.102), channel_id=1, source_target_pairs={{0,1},{1,2},{2,3},{3,4},{4,5},{5,6},{6,7},{7,0},{8,9},{9,10},{10,1... | collective-permute-start | bytes 491528 | tf_op jit(solution)/shard_map/ppermute | solution.py:591
  285.6 7.8 %collective-permute-start.21 = (f32[320,128]{1,0:T(8,128)}, f32[320,128]{1,0:T(8,128)S(1)}, u32[]{:S(2)}, u32[]{:S(2)}) collective-permute-start(f32[320,128]{1,0:T(8,128)} %get-tuple-element.103), channel_id=1, source_target_pairs={{0,7},{1,0},{2,1},{3,2},{4,3},{5,4},{6,5},{7,6},{8,15},{9,8},{10,9... | collective-permute-start | bytes 491528 | tf_op jit(solution)/shard_map/ppermute | solution.py:591
  303.9 8.0 %collective-permute-start.22 = (f32[256,128]{1,0:T(8,128)}, f32[256,128]{1,0:T(8,128)S(1)}, u32[]{:S(2)}, u32[]{:S(2)}) collective-permute-start(f32[256,128]{1,0:T(8,128)} %get-tuple-element.107), channel_id=1, source_target_pairs={{0,1},{1,2},{2,3},{3,4},{4,5},{5,6},{6,7},{7,0},{8,9},{9,10},{10,1... | collective-permute-start | bytes 393224 | tf_op jit(solution)/shard_map/ppermute | solution.py:591
  304.9 7.1 %collective-permute-start.23 = (f32[256,128]{1,0:T(8,128)}, f32[256,128]{1,0:T(8,128)S(1)}, u32[]{:S(2)}, u32[]{:S(2)}) collective-permute-start(f32[256,128]{1,0:T(8,128)} %get-tuple-element.108), channel_id=1, source_target_pairs={{0,7},{1,0},{2,1},{3,2},{4,3},{5,4},{6,5},{7,6},{8,15},{9,8},{10,9... | collective-permute-start | bytes 393224 | tf_op jit(solution)/shard_map/ppermute | solution.py:591
  (17 other events, 11.4 us)

commit v2 on v1

--- a/solution.py
+++ b/solution.py
@@ -9,11 +9,13 @@
 
 OMEGA = 0.8
 KEEP = 0.2
-VMEM_BYTES = 56 * 2**20
+VMEM_BYTES = 32 * 2**20
+WELLS = 8
 
 FR, MR, CR = 56, 64, 40
 F_OWN, M_OWN = 12, 24
-HALO_B, HALO_X = 6, 4
+HALO_B, SKIP_B, HALO_X, SKIP_X = 4, 2, 3, 1
+REACH_B, REACH_X = 14, 12
 ROWS = 32
 
 
@@ -96,14 +98,14 @@
         dst[i, ds(8, 24), :] = both * 0.125
 
 
-def middle_solve(own, below, above, mid, coarse, bufs, nx):
+def middle_solve(own, below, above, reach, mid, coarse, bufs, nx):
     m_b, m_a, m_c, m_res, m_tmp, c_b, c_a, c_c = bufs
     mkx, mky, mkz, mw, mdiag = mid
     count = nx // 4
     for i in range(count):
-        m_b[i, ds(8, 16), :] = below(i)
-        m_b[i, ds(24, 16), :] = own(i)
-        m_b[i, ds(40, 16), :] = above(i)
+        m_b[i, ds(M_OWN - reach, reach), :] = below(i)
+        m_b[i, ds(M_OWN, 16), :] = own(i)
+        m_b[i, ds(M_OWN + 16, reach), :] = above(i)
     scaled(m_c, mw, m_b, 8, 48, count, count)
     seam(m_c, count, 8, 48, 0.0)
     packed_sweep(m_c, m_a, (mkx, mky, mkz, mw), m_b, 8, 48, count, 2, count)
@@ -174,38 +176,74 @@
             out(i, value)
 
 
-def gather_rhs(b_buf, b_own, below, above, nx):
+def gather_rows(buf, window, below, above, halo, skip, nx, pad, keep_low=None, keep_high=None):
+    low, high = F_OWN - skip - halo, F_OWN + ROWS + skip
     for x in range(nx):
-        b_buf[x, ds(F_OWN, ROWS), :] = b_own[x]
-        b_buf[x, ds(F_OWN - HALO_B, HALO_B), :] = below[ds(x * HALO_B, HALO_B), :]
-        b_buf[x, ds(F_OWN + ROWS, HALO_B), :] = above[ds(x * HALO_B, HALO_B), :]
-
-
-def message_writers(ups, downs, b1_own, base):
+        buf[x + pad, ds(8, 40), :] = window[x]
+        under, over = below[ds(x * halo, halo), :], above[ds(x * halo, halo), :]
+        buf[x + pad, ds(low, halo), :] = under if keep_low is None else under * keep_low
+        buf[x + pad, ds(high, halo), :] = over if keep_high is None else over * keep_high
+
+
+def send_rows(up, down, buf, halo, skip, nx, pad):
+    for x in range(nx):
+        up[ds(x * halo, halo), :] = buf[x + pad, ds(F_OWN + ROWS - skip - halo, halo), :]
+        down[ds(x * halo, halo), :] = buf[x + pad, ds(F_OWN + skip, halo), :]
+
+
+def message_writers(ups, downs, b1_own, base, reach):
     def write(i, value):
-        ups[ds(base + 16 * i, 16), :] = value
-        downs[ds(base + 16 * i, 16), :] = value
+        ups[ds(base + reach * i, reach), :] = value[16 - reach :]
+        downs[ds(base + reach * i, reach), :] = value[:reach]
         b1_own[i] = value
 
     return [write]
 
 
-def message_part(ref, base):
-    return lambda i: ref[ds(base + 16 * i, 16), :]
-
-
-def begin_solve(b_buf, x_a, x_b, coeffs, diag, f_tmp, b_own, b1_own, up, down, nx, unroll):
+def message_part(ref, base, reach):
+    return lambda i: ref[ds(base + reach * i, reach), :]
+
+
+def begin_solve(b_buf, x_a, x_b, coeffs, diag, f_tmp, b_out, x_out, b1_own, up, down, nx, unroll):
     scaled(x_a, coeffs[3], b_buf, 8, 40, nx, unroll)
     sweep(x_a, x_b, coeffs, b_buf, 8, 40, nx, 1, unroll)
-    base = nx * HALO_B
-    restricted(x_b, coeffs, diag, b_buf, f_tmp, message_writers(up, down, b1_own, base), nx, unroll)
+    writers = message_writers(up, down, b1_own, nx * HALO_B, REACH_B)
+    restricted(x_b, coeffs, diag, b_buf, f_tmp, writers, nx, unroll)
     for x in range(nx):
-        b_own[x] = b_buf[x, ds(F_OWN, ROWS), :]
-        up[ds(x * HALO_B, HALO_B), :] = b_buf[x, ds(F_OWN + ROWS - HALO_B, HALO_B), :]
-        down[ds(x * HALO_B, HALO_B), :] = b_buf[x, ds(F_OWN, HALO_B), :]
-
-
-def first_kernel(log, sto, per, bp, own, up, down, tmp):
+        b_out[x] = b_buf[x, ds(8, 40), :]
+        x_out[x] = x_b[x + 1, ds(8, 40), :]
+    send_rows(up, down, b_buf, HALO_B, SKIP_B, nx, 0)
+
+
+def listed_wells(rows, counts, cells, owners, starts, masked):
+    number, samples = rows.shape
+    position = lanes((1, samples))
+    lane = lanes((1, 128))
+    listed = [jnp.full((1, 128), -1.0, jnp.float32)] + [jnp.zeros((1, 128), jnp.float32)] * 2
+    masked[...] = jnp.zeros(masked.shape, jnp.float32)
+    for i in range(number):
+        masked[ds(i, 1), :] = jnp.where(position < counts[i], rows[ds(i, 1), :], 0.0)
+        for j, ref in enumerate((owners, cells, starts)):
+            listed[j] = jnp.where(lane == i, ref[i].astype(jnp.float32), listed[j])
+    step = lax.broadcasted_iota(jnp.int32, (8, samples), 0)
+    taken = jnp.where(lanes((8, samples)) // (samples // 2) == step, 1.0, 0.0)
+    sums = lax.dot_general(
+        taken, masked[...], (((1,), (1,)), ((), ())), precision=lax.Precision.HIGHEST, preferred_element_type=jnp.float32
+    )
+    return listed[0], listed[1], jnp.where(listed[2] <= 0.0, sums[0:1], 0.0), sums[1:2]
+
+
+def first_kernel(use_list, *refs):
+    if use_list:
+        counts, cells, owners, starts, log, sto, per, bp, rows, own, up, down, tmp, masked = refs
+    else:
+        log, sto, per, bp, own, up, down, tmp = refs
+    for ref, at in ((own, 1344), (up, 288), (down, 288)):
+        ref[ds(at, WELLS), :] = jnp.zeros((WELLS, 128), jnp.float32)
+    if use_list:
+        for j, value in enumerate(listed_wells(rows, counts, cells, owners, starts, masked)):
+            for ref, at in ((own, 1344), (up, 288), (down, 288)):
+                ref[ds(at + j, 1), :] = value
     odd = lanes((16, 128)) % 2 == 1
     fields = (log, sto, per, bp.at[0], bp.at[1])
     for f, ref in enumerate(fields):
@@ -241,8 +279,9 @@
         kx[x] = factor * e[x] * e[x + 1]
         center = e[x + 1]
         kz[x] = jnp.where(top, 0.0, factor * center * pltpu.roll(center, 128 - shift, 1))
-        ky[x, ds(0, size - 8), :] = factor * e[x + 1, ds(0, size - 8), :] * e[x + 1, ds(1, size - 8), :]
-        ky[x, ds(size - 8, 8), :] = jnp.zeros((8, 128), jnp.float32)
+        for start, number in ((0, size - 8), (size - 8, 7)):
+            ky[x, ds(start, number), :] = factor * e[x + 1, ds(start, number), :] * e[x + 1, ds(start + 1, number), :]
+        ky[x, ds(size - 1, 1), :] = jnp.zeros((1, 128), jnp.float32)
 
     loop(count, body, unroll)
     kx[count] = factor * e[count] * e[count + 1]
@@ -270,8 +309,8 @@
     (kx, ky, kz, w, diag, sto_out, d_one, bp_out, mkx, mky, mkz, mw, mdiag, ckx, cky, ckz, cw) = refs[
         1 + 2 * tiles : 18 + 2 * tiles
     ]
-    b_own, b1_own, up, down = refs[18 + 2 * tiles : 22 + 2 * tiles]
-    e, sto, per, bp0, bp1, x_a, x_b, b_buf, f_tmp, e_mid, s_mid, e_co, s_co, m_tmp, m_tmp2 = refs[22 + 2 * tiles :]
+    b_out, x_out, b1_own, up, down, wells = refs[18 + 2 * tiles : 24 + 2 * tiles]
+    e, sto, per, bp0, bp1, x_a, x_b, b_buf, f_tmp, e_mid, s_mid, e_co, s_co, m_tmp, m_tmp2 = refs[24 + 2 * tiles :]
     gx, gy = place[0], place[1]
     first, last = gy == 0, gy == n_gy - 1
     for buf in (e, per, bp0, bp1, x_a, x_b):
@@ -296,7 +335,7 @@
                 buf[slab, ds(12, 32), :] = own[ds(f * 256 + x * 32, 32), :]
                 if f < 2:
                     buf[slab, ds(4, 8), :] = halo[ds(f * 64 + x * 8, 8), :]
-                    buf[slab, ds(44, 8), :] = halo[ds(288 + f * 64 + x * 8, 8), :]
+                    buf[slab, ds(44, 8), :] = halo[ds(296 + f * 64 + x * 8, 8), :]
                     buf[slab, ds(0, 4), :] = blank
                     buf[slab, ds(52, 4), :] = blank
                 else:
@@ -304,7 +343,7 @@
                     buf[slab, ds(0, 8), :] = blank8
                     buf[slab, ds(48, 8), :] = blank8
                     buf[slab, ds(8, 4), :] = halo[ds(at, 4), :] * keep_low
-                    buf[slab, ds(44, 4), :] = halo[ds(288 + at, 4), :] * keep_high
+                    buf[slab, ds(44, 4), :] = halo[ds(296 + at, 4), :] * keep_high
 
         for x in range(8):
             body(x)
@@ -356,6 +395,15 @@
         bp_out[0, x] = bp0[gx * 8 + x]
         bp_out[1, x] = bp1[gx * 8 + x]
 
+    lane = lanes((WELLS, 128))
+    listed = 128 // tiles
+    for refs_of, at, out in ((owns, 1344, wells), (halos, 288, up), (halos, 584, down)):
+        value = refs_of[0][ds(at, WELLS), :]
+        for index in range(1, tiles):
+            moved = pltpu.roll(refs_of[index][ds(at, WELLS), :], index * listed, 1)
+            value = jnp.where(lane >= index * listed, moved, value)
+        out[ds(out.shape[0] - WELLS, WELLS), :] = value
+
     count = nx // 4
     odd = lanes((16, 128)) % 2 == 1
     for index in range(tiles):
@@ -365,7 +413,7 @@
         base = jnp.where(upper, tile - half, tile) * 4
         mask = odd == upper
         for i in range(4):
-            for start, ref, at in ((8, halo, 224 + 16 * i), (24, own, 1280 + 16 * i), (40, halo, 512 + 16 * i)):
+            for start, ref, at in ((8, halo, 224 + 16 * i), (24, own, 1280 + 16 * i), (40, halo, 520 + 16 * i)):
                 value = ref[ds(at, 16), :]
                 left, right = pltpu.roll(value, 127, 1), pltpu.roll(value, 1, 1)
                 log_part, sto_part = jnp.where(odd, right, value), jnp.where(odd, value, left)
@@ -399,50 +447,60 @@
                 diag_l[i, rows, :] = value
                 diag_l[i, ds(0, 8), :] = edge
                 diag_l[i, ds(size - 8, 8), :] = edge
-    begin_solve(b_buf, x_a, x_b, (kx, ky, kz, w), diag, f_tmp, b_own, b1_own, up, down, nx, unroll)
+    begin_solve(b_buf, x_a, x_b, (kx, ky, kz, w), diag, f_tmp, b_out, x_out, b1_own, up, down, nx, unroll)
+
+
+def forward(below, above, up, down):
+    up[ds(up.shape[0] - WELLS, WELLS), :] = below[ds(below.shape[0] - WELLS, WELLS), :]
+    down[ds(down.shape[0] - WELLS, WELLS), :] = above[ds(above.shape[0] - WELLS, WELLS), :]
 
 
 def middle_kernel(nx, unroll, *refs):
-    (kx, ky, kz, w, diag, mkx, mky, mkz, mw, mdiag, ckx, cky, ckz, cw) = refs[:14]
-    b_own, b1_own, below, above, x_own, b1_out, up, down = refs[14:22]
-    x_a, x_b, b_buf, f_tmp = refs[22:26]
-    bufs = refs[26:]
+    b1_own, below, above, mkx, mky, mkz, mw, mdiag, ckx, cky, ckz, cw = refs[:12]
+    b_in, x_in, kx, ky, kz, w, diag, x_out, b1_out, up, down = refs[12:23]
+    x_a, x_b, b_buf, f_tmp = refs[23:27]
+    bufs = refs[27:]
     coeffs = (kx, ky, kz, w)
     zero_ends(x_a, nx)
     zero_ends(x_b, nx)
     base = nx * HALO_B
+    forward(below, above, up, down)
     middle_solve(
         lambda i: b1_own[i],
-        message_part(below, base),
-        message_part(above, base),
+        message_part(below, base, REACH_B),
+        message_part(above, base, REACH_B),
+        REACH_B,
         (mkx, mky, mkz, mw, mdiag),
         (ckx, cky, ckz, cw),
         bufs,
         nx,
     )
-    gather_rhs(b_buf, b_own, below, above, nx)
-    scaled(x_a, w, b_buf, 4, 48, nx, unroll)
-    sweep(x_a, x_b, coeffs, b_buf, 4, 48, nx, 1, unroll)
+    gather_rows(b_buf, b_in, below, above, HALO_B, SKIP_B, nx, 0)
+    for start in (0, 40):
+        scaled(x_a, w, b_buf, start, 16, nx, unroll)
+    for x in range(nx):
+        x_b[x + 1, ds(8, 40), :] = x_in[x]
+    for start in (4, 44):
+        sweep(x_a, x_b, coeffs, b_buf, start, 8, nx, 1, unroll)
     add_correction(x_b, bufs[1], f_tmp, nx, unroll)
     sweep(x_b, x_a, coeffs, b_buf, 8, 40, nx, 1, unroll)
     sweep(x_a, x_b, coeffs, b_buf, 8, 40, nx, 1, unroll)
     sweep(x_b, x_a, coeffs, b_buf, 8, 40, nx, 1, unroll)
     sweep(x_a, x_b, coeffs, b_buf, 8, 40, nx, 1, unroll)
     base = nx * HALO_X
-    restricted(x_b, coeffs, diag, b_buf, f_tmp, message_writers(up, down, b1_out, base), nx, unroll)
+    restricted(x_b, coeffs, diag, b_buf, f_tmp, message_writers(up, down, b1_out, base, REACH_X), nx, unroll)
     for x in range(nx):
-        x_own[x] = x_b[x + 1, ds(F_OWN, ROWS), :]
-        up[ds(x * HALO_X, HALO_X), :] = x_b[x + 1, ds(F_OWN + ROWS - HALO_X, HALO_X), :]
-        down[ds(x * HALO_X, HALO_X), :] = x_b[x + 1, ds(F_OWN, HALO_X), :]
+        x_out[x] = x_b[x + 1, ds(8, 40), :]
+    send_rows(up, down, x_b, HALO_X, SKIP_X, nx, 1)
 
 
 def end_kernel(nx, n_gy, unroll, kind, *refs):
     place = refs[0]
-    (kx, ky, kz, w, diag, mkx, mky, mkz, mw, mdiag, ckx, cky, ckz, cw) = refs[1:15]
-    b_in, below_b, above_b, x_own, b1_in, below, above = refs[15:22]
+    b1_in, below, above, mkx, mky, mkz, mw, mdiag, ckx, cky, ckz, cw = refs[1:13]
+    below_b, above_b, b_in, x_in, kx, ky, kz, w, diag = refs[13:22]
     extra = {1: 2, 2: 1, 3: 3, 4: 2}[kind]
     extras, rest = refs[22 : 22 + extra], refs[22 + extra :]
-    outs = {1: 5, 2: 5, 3: 5, 4: 1}[kind]
+    outs = {1: 6, 2: 6, 3: 6, 4: 1}[kind]
     outs, scratch = rest[:outs], rest[outs:]
     x_a, x_b, b_buf, f_tmp = scratch[:4]
     bufs = scratch[4:]
@@ -453,26 +511,26 @@
     zero_ends(x_a, nx)
     zero_ends(x_b, nx)
     base = nx * HALO_X
+    if kind < 4:
+        forward(below, above, outs[3], outs[4])
     middle_solve(
         lambda i: b1_in[i],
-        message_part(below, base),
-        message_part(above, base),
+        message_part(below, base, REACH_X),
+        message_part(above, base, REACH_X),
+        REACH_X,
         (mkx, mky, mkz, mw, mdiag),
         (ckx, cky, ckz, cw),
         bufs,
         nx,
     )
-    gather_rhs(b_buf, b_in, below_b, above_b, nx)
-    for x in range(nx):
-        x_a[x + 1, ds(F_OWN, ROWS), :] = x_own[x]
-        x_a[x + 1, ds(F_OWN - HALO_X, HALO_X), :] = below[ds(x * HALO_X, HALO_X), :] * keep_low
-        x_a[x + 1, ds(F_OWN + ROWS, HALO_X), :] = above[ds(x * HALO_X, HALO_X), :] * keep_high
+    gather_rows(b_buf, b_in, below_b, above_b, HALO_B, SKIP_B, nx, 0)
+    gather_rows(x_a, x_in, below, above, HALO_X, SKIP_X, nx, 1, keep_low, keep_high)
     add_correction(x_a, bufs[1], f_tmp, nx, unroll)
     sweep(x_a, x_b, coeffs, b_buf, 8, 40, nx, 1, unroll)
     sweep(x_b, x_a, coeffs, b_buf, 8, 40, nx, 1, unroll)
     rows = ds(8, 40)
     if kind < 4:
-        b_own, b1_own, up, down, kept = outs
+        b_out, x_out, b1_own, up, down, kept = outs
 
         def body(x):
             value = x_a[x + 1, rows, :]
@@ -495,7 +553,7 @@
                 kept[x] = x_a[gx * 8 + x + 1, ds(F_OWN, ROWS), :]
         if kind == 3:
             zero_ends(kept, nx)
-        begin_solve(b_buf, x_a, x_b, coeffs, diag, f_tmp, b_own, b1_own, up, down, nx, unroll)
+        begin_solve(b_buf, x_a, x_b, coeffs, diag, f_tmp, b_out, x_out, b1_own, up, down, nx, unroll)
     else:
         lam_two, bp = extras
         own, plus, minus = ds(F_OWN, ROWS), ds(F_OWN + 1, ROWS), ds(F_OWN - 1, ROWS)
@@ -516,17 +574,35 @@
             outs[0][x] = -0.5 * total
 
 
-def call(body, outs, scratch, args, scalars):
+def call(body, outs, scratch, args, scalars, limit=VMEM_BYTES):
     f32 = jnp.float32
-    vmem = pl.BlockSpec(memory_space=pltpu.VMEM)
-    smem = pl.BlockSpec(memory_space=pltpu.SMEM)
+    staged = [i for i, arg in enumerate(args) if i >= scalars and arg.ndim == 1]
+    held_at = len(args) + len(outs)
+
+    def kernel(*refs):
+        refs = list(refs)
+        if staged:
+            semaphores = refs[-1]
+            copies = []
+            for j, i in enumerate(staged):
+                copies.append(pltpu.make_async_copy(refs[i], refs[held_at + j], semaphores.at[j]))
+                copies[-1].start()
+            for j, i in enumerate(staged):
+                copies[j].wait()
+                refs[i] = refs[held_at + j]
+            refs = refs[:-1]
+        body(*refs[:held_at], *refs[held_at + len(staged) :])
+
     return pl.pallas_call(
-        body,
-        out_shape=[jax.ShapeDtypeStruct(s, f32) for s in outs],
-        in_specs=[smem] * scalars + [vmem] * (len(args) - scalars),
-        out_specs=[vmem] * len(outs),
-        scratch_shapes=[pltpu.VMEM(s, f32) for s in scratch],
-        compiler_params=pltpu.CompilerParams(vmem_limit_bytes=VMEM_BYTES),
+        kernel,
+        out_shape=[jax.ShapeDtypeStruct(shape, f32) for shape in outs],
+        in_specs=[pl.BlockSpec(memory_space=pltpu.SMEM)] * scalars
+        + [pl.BlockSpec(memory_space=pltpu.VMEM)] * (len(args) - scalars),
+        out_specs=[pl.BlockSpec(memory_space=pltpu.VMEM)] * len(outs),
+        scratch_shapes=[pltpu.SMEM(args[i].shape, args[i].dtype) for i in staged]
+        + [pltpu.VMEM(shape, f32) for shape in scratch]
+        + ([pltpu.SemaphoreType.DMA((len(staged),))] if staged else []),
+        compiler_params=pltpu.CompilerParams(vmem_limit_bytes=limit),
     )(*args)
 
 
@@ -544,20 +620,21 @@
     return same + [lax.ppermute(part, "gx", swap) for part in same]
 
 
-def well_sources(rows, cells, counts, owners, starts, nx, n_gy):
+def gathered_wells(rows, cells, counts, owners, starts):
     listed, samples = rows.shape
-    steps = 2
     position = jnp.arange(samples, dtype=jnp.int32)
     counted = jnp.where(position[None, :] < counts[:, None], rows, 0.0)
-    per_step = counted.reshape(listed, steps, samples // steps).sum(axis=2)
-    weights = jnp.where(jnp.arange(steps, dtype=jnp.int32)[None, :] >= starts[:, None], per_step, 0.0)
-    whole = jnp.stack([owners[:, 0], cells], axis=0)
-    weights = lax.all_gather(weights.T, ("gx", "gy"), axis=1, tiled=True)
-    whole = lax.all_gather(whole, ("gx", "gy"), axis=1, tiled=True)
-    owner, cell = whole[0], whole[1]
+    per_step = counted.reshape(listed, 2, samples // 2).sum(axis=2)
+    weights = jnp.where(jnp.arange(2, dtype=jnp.int32)[None, :] >= starts[:, None], per_step, 0.0)
+    places = jnp.stack([owners, cells], axis=0).astype(jnp.float32)
+    return lax.all_gather(jnp.concatenate([places, weights.T], axis=0), ("gx", "gy"), axis=1, tiled=True)
+
+
+def well_sources(wells, nx, n_gy):
+    owner, cell, weights = wells[0].astype(jnp.int32), wells[1].astype(jnp.int32), wells[2:4]
     x = (owner // n_gy) * 8 + cell // (32 * 128)
     y = (owner % n_gy - lax.axis_index("gy")) * 32 + (cell // 128) % 32 + 4
-    spot = jnp.where(jnp.logical_and(y >= 0, y < 40), x * 40 + y, -1)
+    spot = jnp.where(jnp.logical_and(owner >= 0, jnp.logical_and(y >= 0, y < 40)), x * 40 + y, -1)
     z = cell % 128
     total = spot.shape[0]
     chunk = 1024 if total % 1024 == 0 else total
@@ -565,7 +642,7 @@
     def part(spot, z, weights):
         left = (spot[None, :] == jnp.arange(nx * 40, dtype=jnp.int32)[:, None]).astype(jnp.float32)
         here = z[:, None] == jnp.arange(128, dtype=jnp.int32)[None, :]
-        right = jnp.concatenate([jnp.where(here, weights[t][:, None], 0.0) for t in range(steps)], axis=1)
+        right = jnp.concatenate([jnp.where(here, weights[t][:, None], 0.0) for t in range(2)], axis=1)
         return jnp.dot(left, right, precision=lax.Precision.HIGHEST)
 
     if total == chunk:
@@ -576,23 +653,33 @@
             cut = lambda a: lax.dynamic_slice_in_dim(a, i * chunk, chunk, axis=-1)
             return acc + part(cut(spot), cut(z), cut(weights))
 
-        source = lax.fori_loop(0, total // chunk, body, jnp.zeros((nx * 40, steps * 128), jnp.float32))
-    return [source[:, t * 128 : (t + 1) * 128].reshape(nx, 40, 128) for t in range(steps)]
+        source = lax.fori_loop(0, total // chunk, body, jnp.zeros((nx * 40, 256), jnp.float32))
+    return [source[:, t * 128 : (t + 1) * 128].reshape(nx, 40, 128) for t in range(2)]
 
 
 def local(log_perm, perturb, storage, base_press, well_rows, well_cells, well_counts, well_owner, well_start):
     tiles, n_gy = lax.axis_size("gx"), lax.axis_size("gy")
     nx = 8 * tiles
     count, half = nx // 4, nx // 8
-    unroll = 8
+    unroll = 32
     up_perm, down_perm = cycle(n_gy, 1), cycle(n_gy, -1)
 
     def exchange(up, down):
         return lax.ppermute(up, "gy", up_perm), lax.ppermute(down, "gy", down_perm)
 
     place = jnp.stack([lax.axis_index("gx"), lax.axis_index("gy")]).astype(jnp.int32)
+    listed, samples = well_rows.shape
+    owners = well_owner.reshape(listed)
+    use_list = n_gy == 8 and tiles * listed == 128
     own, up, down = call(
-        first_kernel, [(1344, 128), (288, 128), (288, 128)], [(2, 4, 32, 128)], [log_perm, storage, perturb, base_press], 0
+        functools.partial(first_kernel, use_list),
+        [(1344 + WELLS, 128), (288 + WELLS, 128), (288 + WELLS, 128)],
+        [(2, 4, 32, 128)] + ([(128, samples)] if use_list else []),
+        ([well_counts, well_cells, owners, well_start] if use_list else [])
+        + [log_perm, storage, perturb, base_press]
+        + ([well_rows] if use_list else []),
+        0,
+        60 * 2**20,
     )
     below, above = exchange(up, down)
     owns = gathered(own, tiles)
@@ -602,64 +689,77 @@
     coarse, coarse_pad = (half, CR, 128), (half + 2, CR, 128)
     own_shape, window = (nx, ROWS, 128), (nx, 40, 128)
     b1_shape = (count, 16, 128)
-    message_b, message_x = (nx * HALO_B + count * 16, 128), (nx * HALO_X + count * 16, 128)
+    message_b = (nx * HALO_B + count * REACH_B + WELLS, 128)
+    message_x = (nx * HALO_X + count * REACH_X + WELLS, 128)
     coeff_shapes = [(nx + 1, FR, 128), fine, fine, fine, own_shape]
     mid_shapes = [(count + 1, MR, 128), mid, mid, mid, mid]
     coarse_shapes = [(half + 1, CR, 128), coarse, coarse, coarse]
     outs = call(
-        functools.partial(second_kernel, nx, n_gy, min(unroll, 4)),
+        functools.partial(second_kernel, nx, n_gy, min(unroll, 16)),
         coeff_shapes
         + [window, window, (2, 10, FR, 128)]
         + mid_shapes
         + coarse_shapes
-        + [own_shape, b1_shape, message_b, message_b],
+        + [window, window, b1_shape, message_b, message_b, (WELLS, 128)],
         [fine_pad, fine, fine_pad, fine_pad, fine_pad, fine_pad, fine_pad, fine, (nx // 2, FR, 128)]
         + [mid_pad, mid, coarse_pad, coarse, mid, mid],
         [place] + owns + halos,
         1,
     )
     coeffs, (sto, d_one, bp) = outs[:5], outs[5:8]
-    coeffs = list(coeffs) + list(outs[8:17])
-    begun = outs[17:21]
-    sources = well_sources(well_rows, well_cells, well_counts, well_owner, well_start, nx, n_gy)
+    levels = list(outs[8:17])
+    coeffs = list(coeffs)
+    begun = outs[17:22]
+    wells = None
+    if use_list:
+        lists = [outs[22], begun[3][-WELLS:], begun[4][-WELLS:]]
+    else:
+        wells = gathered_wells(well_rows, well_cells, well_counts, owners, well_start)
     scratch = [fine_pad, fine_pad, fine, (nx // 2, FR, 128)]
     scratch += [mid, mid_pad, mid_pad, mid, mid, coarse, coarse_pad, coarse_pad]
     change = None
     for kind in (1, 2, 3, 4):
-        b_own, b1_own, up, down = begun
+        b_own, x_first, b1_own, up, down = begun
         below_b, above_b = exchange(up, down)
+        if use_list and kind <= 2:
+            lists += [below_b[-WELLS:]] if kind == 2 else [below_b[-WELLS:], above_b[-WELLS:]]
         x_own, b1_mid, up, down = call(
             functools.partial(middle_kernel, nx, unroll),
-            [own_shape, b1_shape, message_x, message_x],
+            [window, b1_shape, message_x, message_x],
             scratch,
-            coeffs + [b_own, b1_own, below_b, above_b],
+            [b1_own, below_b, above_b] + levels + [b_own, x_first] + coeffs,
             0,
         )
         below, above = exchange(up, down)
-        extras = {1: [sto, d_one], 2: [sources[1]], 3: [sto, sources[0], change], 4: []}[kind]
-        begin_shapes = [own_shape, b1_shape, message_b, message_b]
+        if use_list and kind == 1:
+            lists += [below[-WELLS:], above[-WELLS:]]
+        if kind == 2:
+            wells = jnp.concatenate(lists, axis=1) if use_list else wells
+            sources = well_sources(wells, nx, n_gy)
+        extras = {1: lambda: [sto, d_one], 2: lambda: [sources[1]], 3: lambda: [sto, sources[0], change], 4: lambda: [lam_two, bp]}[
+            kind
+        ]()
+        begin_shapes = [window, window, b1_shape, message_b, message_b]
         shapes = {
             1: begin_shapes + [window],
             2: begin_shapes + [(8, ROWS, 128)],
             3: begin_shapes + [(nx + 2, 40, 128)],
             4: [(8, ROWS, 128)],
         }[kind]
-        if kind == 4:
-            extras = [lam_two, bp]
         outs = call(
             functools.partial(end_kernel, nx, n_gy, unroll, kind),
             shapes,
             scratch,
-            [place] + coeffs + [b_own, below_b, above_b, x_own, b1_mid, below, above] + extras,
+            [place, b1_mid, below, above] + levels + [below_b, above_b, b_own, x_own] + coeffs + extras,
             1,
         )
         if kind == 1:
-            change = outs[4]
+            change = outs[5]
         elif kind == 2:
-            final_change = outs[4]
+            final_change = outs[5]
         elif kind == 3:
-            lam_two = outs[4]
-        begun = outs[:4]
+            lam_two = outs[5]
+        begun = outs[:5]
     return (outs[0], final_change)
 
 

time: 321 us -> 144 us (0.45)
  blocking collectives: 131 us -> 0 us
  Pallas kernels: 88.5 us -> 46.8 us
  local copies, waits for them, and re-layouts: 8.36 us -> 1.22 us
  waiting for transfers between devices: 37.7 us -> 43.5 us
    all_gather x2 -> x0, blocking collectives: 131 us -> none  [the longest x1 67.7 us: well_sources(): whole = lax.all_gather(whole, ('gx', 'gy'), axis=1, tiled=True)]
    pallas_call x10, Pallas kernels: 88.5 us -> 46.8 us  [call(): pl.pallas_call(kernel, out_shape=[jax.ShapeDtypeStruct(shape, f32) for sh...]
    ppermute x2, waiting for transfers between devices: 6.26 us -> 14.8 us  [gathered(): same.append(lax.ppermute(array, 'gx', perm))]
    unnamed x54 -> x10, local copies, waits for them, and re-layouts: 7.15 us -> 1.12 us
  transfers between devices with their start and end apart: 24 -> 24, of which waited for: 18 -> 15; matrix products, arithmetic and copies ran while one was open for 2% -> 2% of each run, Pallas kernels for 0% -> 0%
where the time goes in v2:
time: 144 us
  starting transfers between devices  48.2 us (33%)
  Pallas kernels  46.8 us (32%)
  waiting for transfers between devices  43.5 us (30%)
  matrix products  2.63 us (2%)
    pallas_call x10, Pallas kernels, call(): pl.pallas_call(kernel, out_shape=[jax.ShapeDtypeStruct(shape, f32) for sh...  46.8 us
    ppermute x9, starting transfers between devices, exchange(): lax.ppermute(down, 'gy', down_perm)  38.2 us
    ppermute x9, waiting for transfers between devices, exchange(): lax.ppermute(up, 'gy', up_perm)  24.2 us
    ppermute x2, waiting for transfers between devices, gathered(): same.append(lax.ppermute(array, 'gx', perm))  14.8 us
    ppermute x9, starting transfers between devices, exchange(): lax.ppermute(up, 'gy', up_perm)  4.97 us
    ppermute x2, starting transfers between devices, gathered(): same.append(lax.ppermute(array, 'gx', perm))  4.84 us
  transfers between devices with their start and end apart: 24, of which 15 were waited for; matrix products, arithmetic and copies ran while one was open for 2% of the time, Pallas kernels for 0%

profile of v2, /device:TPU:0, one launch (start us, length us, event | category | flops | bytes accessed | tf_op | source)
XLA Modules:
  0.0 143.7 jit_solution(8381991460706284249)
XLA Ops:
  0.6 3.2 %shard_map.104 = (f32[1352,128]{1,0:T(8,128)}, f32[296,128]{1,0:T(8,128)}, f32[296,128]{1,0:T(8,128)}) custom-call(s32[32]{0:T(128)} %refs_0_.1, s32[32]{0:T(128)} %refs_1_.1, s32[32]{0:T(128)} %bitcast.15, s32[32]{0:T(128)} %refs_3_.1, f32[8,32,128]{2,1,0:T(8,128)} %refs_4_.1, f32[8,32,128]{2,1,0:T(8,128)} %refs_5_.1, f32[8,32,128]{2,1,0:T(8,128)} %refs_6_.1, ...), custom_call_target="tpu_custom_call" | custom-call | tf_op jit(solution)/shard_map/pallas_call | solution.py:596
  3.8 3.0 %collective-permute-start = (f32[1352,128]{1,0:T(8,128)}, f32[1352,128]{1,0:T(8,128)S(1)}, u32[]{:S(2)}, u32[]{:S(2)}) collective-permute-start(f32[1352,128]{1,0:T(8,128)} %get-tuple-element.62.refs_1_), channel_id=1, source_target_pairs={{0,16},{8,24},{16,0},{24,8},{1,17},{9,25},{17,1},{25,9},{2,18},{10... | collective-permute-start | bytes 2076680 | tf_op jit(solution)/shard_map/ppermute | solution.py:618
  8.3 3.2 %collective-permute-start.4 = (f32[296,128]{1,0:T(8,128)}, f32[296,128]{1,0:T(8,128)S(1)}, u32[]{:S(2)}, u32[]{:S(2)}) collective-permute-start(f32[296,128]{1,0:T(8,128)} %get-tuple-element.64), channel_id=1, source_target_pairs={{0,7},{1,0},{2,1},{3,2},{4,3},{5,4},{6,5},{7,6},{8,15},{9,8},{10,9... | collective-permute-start | bytes 454664 | tf_op jit(solution)/shard_map/ppermute | solution.py:668
  11.6 3.8 %collective-permute-done.3 = f32[296,128]{1,0:T(8,128)S(1)} collective-permute-done((f32[296,128]{1,0:T(8,128)}, f32[296,128]{1,0:T(8,128)S(1)}, u32[]{:S(2)}, u32[]{:S(2)}) %collective-permute-start.3) | collective-permute-done | bytes 151584 | tf_op jit(solution)/shard_map/ppermute | solution.py:668
  15.3 7.2 %collective-permute-done.refs_2_ = f32[1352,128]{1,0:T(8,128)S(1)} collective-permute-done((f32[1352,128]{1,0:T(8,128)}, f32[1352,128]{1,0:T(8,128)S(1)}, u32[]{:S(2)}, u32[]{:S(2)}) %collective-permute-start) | collective-permute-done | bytes 692256 | tf_op jit(solution)/shard_map/ppermute | solution.py:618
  22.6 1.8 %collective-permute-start.5 = (f32[592,128]{1,0:T(8,128)S(1)}, f32[592,128]{1,0:T(8,128)S(1)}, u32[]{:S(2)}, u32[]{:S(2)}) collective-permute-start(f32[592,128]{1,0:T(8,128)S(1)} %constant_dynamic-update-slice_fusion.refs_5_), channel_id=1, source_target_pairs={{0,16},{8,24},{16,0},{24,8},{1,17},{9,25},{17,1},{25,9},{2,18},{10... | collective-permute-start | bytes 909320 | tf_op jit(solution)/shard_map/ppermute | solution.py:618
  24.6 7.6 %collective-permute-done.5.refs_6_ = f32[592,128]{1,0:T(8,128)S(1)} collective-permute-done((f32[592,128]{1,0:T(8,128)S(1)}, f32[592,128]{1,0:T(8,128)S(1)}, u32[]{:S(2)}, u32[]{:S(2)}) %collective-permute-start.5) | collective-permute-done | bytes 303136 | tf_op jit(solution)/shard_map/ppermute | solution.py:618
  34.9 7.9 %shard_map.105 = (f32[33,56,128]{2,1,0:T(8,128)S(1)}, f32[32,56,128]{2,1,0:T(8,128)S(1)}, f32[32,56,128]{2,1,0:T(8,128)S(1)}, f32[32,56,128]{2,1,0:T(8,128)S(1)}...) custom-call(s32[2]{0:T(128)S(1)} %pad_add_fusion.refs_0_, ...), custom_call_target="tpu_custom_call" | custom-call | tf_op jit(solution)/shard_map/pallas_call | solution.py:596
  44.7 3.1 %collective-permute-start.9 = (f32[248,128]{1,0:T(8,128)S(1)}, f32[248,128]{1,0:T(8,128)S(1)}, u32[]{:S(2)}, u32[]{:S(2)}) collective-permute-start(f32[248,128]{1,0:T(8,128)S(1)} %get-tuple-element.67), channel_id=1, source_target_pairs={{0,7},{1,0},{2,1},{3,2},{4,3},{5,4},{6,5},{7,6},{8,15},{9,8},{10,9... | collective-permute-start | bytes 380936 | tf_op jit(solution)/shard_map/ppermute | solution.py:668
  47.8 3.7 %collective-permute-done.8.refs_1_.refs_13_ = f32[248,128]{1,0:T(8,128)S(1)} collective-permute-done((f32[248,128]{1,0:T(8,128)S(1)}, f32[248,128]{1,0:T(8,128)S(1)}, u32[]{:S(2)}, u32[]{:S(2)}) %collective-permute-start.8) | collective-permute-done | bytes 127008 | tf_op jit(solution)/shard_map/ppermute | solution.py:668
  52.6 4.2 %shard_map.106 = (f32[32,40,128]{2,1,0:T(8,128)S(1)}, f32[8,16,128]{2,1,0:T(8,128)S(1)}, f32[200,128]{1,0:T(8,128)S(1)}, f32[200,128]{1,0:T(8,128)S(1)}) custom-call(f32[8,16,128]{2,1,0:T(8,128)S(1)} %get-tuple-element.65.refs_0_, f32[248,128]{1,0:T(8,128)S(1)} %collective-permute-done.8.refs_1_.refs_13_, ...), custom_call_target="tpu_custom_call" | custom-call | tf_op jit(solution)/shard_map/pallas_call | solution.py:596
  57.1 4.4 %collective-permute-start.11 = (f32[200,128]{1,0:T(8,128)S(1)}, f32[200,128]{1,0:T(8,128)S(1)}, u32[]{:S(2)}, u32[]{:S(2)}) collective-permute-start(f32[200,128]{1,0:T(8,128)S(1)} %get-tuple-element.86), channel_id=1, source_target_pairs={{0,7},{1,0},{2,1},{3,2},{4,3},{5,4},{6,5},{7,6},{8,15},{9,8},{10,9... | collective-permute-start | bytes 307208 | tf_op jit(solution)/shard_map/ppermute | solution.py:668
  61.5 2.7 %collective-permute-done.10.refs_2_ = f32[200,128]{1,0:T(8,128)S(1)} collective-permute-done((f32[200,128]{1,0:T(8,128)S(1)}, f32[200,128]{1,0:T(8,128)S(1)}, u32[]{:S(2)}, u32[]{:S(2)}) %collective-permute-start.10) | collective-permute-done | bytes 102432 | tf_op jit(solution)/shard_map/ppermute | solution.py:668
  64.5 4.5 %shard_map.107 = (f32[32,40,128]{2,1,0:T(8,128)S(1)}, f32[32,40,128]{2,1,0:T(8,128)S(1)}, f32[8,16,128]{2,1,0:T(8,128)S(1)}, f32[248,128]{1,0:T(8,128)S(1)}, f32...) custom-call(s32[2]{0:T(128)S(1)} %pad_add_fusion.refs_0_, f32[8,16,128]{2,1,0:T(8,128)S(1)} %get-tuple-element.84.refs_1_, ...), custom_call_target="tpu_custom_call" | custom-call | tf_op jit(solution)/shard_map/pallas_call | solution.py:596
  69.6 4.1 %collective-permute-start.13 = (f32[248,128]{1,0:T(8,128)S(1)}, f32[248,128]{1,0:T(8,128)S(1)}, u32[]{:S(2)}, u32[]{:S(2)}) collective-permute-start(f32[248,128]{1,0:T(8,128)S(1)} %get-tuple-element.92), channel_id=1, source_target_pairs={{0,7},{1,0},{2,1},{3,2},{4,3},{5,4},{6,5},{7,6},{8,15},{9,8},{10,9... | collective-permute-start | bytes 380936 | tf_op jit(solution)/shard_map/ppermute | solution.py:668
  73.8 3.0 %collective-permute-done.12.refs_1_.refs_13_ = f32[248,128]{1,0:T(8,128)S(1)} collective-permute-done((f32[248,128]{1,0:T(8,128)S(1)}, f32[248,128]{1,0:T(8,128)S(1)}, u32[]{:S(2)}, u32[]{:S(2)}) %collective-permute-start.12) | collective-permute-done | bytes 127008 | tf_op jit(solution)/shard_map/ppermute | solution.py:668
  78.0 4.2 %shard_map.108 = (f32[32,40,128]{2,1,0:T(8,128)S(1)}, f32[8,16,128]{2,1,0:T(8,128)S(1)}, f32[200,128]{1,0:T(8,128)S(1)}, f32[200,128]{1,0:T(8,128)S(1)}) custom-call(f32[8,16,128]{2,1,0:T(8,128)S(1)} %get-tuple-element.90.refs_0_, f32[248,128]{1,0:T(8,128)S(1)} %collective-permute-done.12.refs_1_.refs_13_, ...), custom_call_target="tpu_custom_call" | custom-call | tf_op jit(solution)/shard_map/pallas_call | solution.py:596
  82.3 4.7 %collective-permute-start.15 = (f32[200,128]{1,0:T(8,128)S(1)}, f32[200,128]{1,0:T(8,128)S(1)}, u32[]{:S(2)}, u32[]{:S(2)}) collective-permute-start(f32[200,128]{1,0:T(8,128)S(1)} %get-tuple-element.97), channel_id=1, source_target_pairs={{0,7},{1,0},{2,1},{3,2},{4,3},{5,4},{6,5},{7,6},{8,15},{9,8},{10,9... | collective-permute-start | bytes 307208 | tf_op jit(solution)/shard_map/ppermute | solution.py:668
  87.5 2.6 %fusion = f32[1280,256]{1,0:T(8,128)S(1)} fusion(s32[1024]{0:T(1024)S(1)} %bitcast.14, f32[1024,128]{1,0:T(8,128)S(1)} %get-tuple-element.128, f32[1024,128]{1,0:T(8,128)S(1)} %get-tuple-element.127), kind=kOutput, calls=%fused_computation.1 | convolution fusion | flops 4028104704 | bytes 2363392 | tf_op jit(solution)/shard_map/dot_general | solution.py:646
  90.2 5.0 %shard_map.109 = (f32[32,40,128]{2,1,0:T(8,128)S(1)}, f32[32,40,128]{2,1,0:T(8,128)S(1)}, f32[8,16,128]{2,1,0:T(8,128)S(1)}, f32[248,128]{1,0:T(8,128)S(1)}, f32...) custom-call(s32[2]{0:T(128)S(1)} %pad_add_fusion.refs_0_, f32[8,16,128]{2,1,0:T(8,128)S(1)} %get-tuple-element.95.refs_1_, ...), custom_call_target="tpu_custom_call" | custom-call | tf_op jit(solution)/shard_map/pallas_call | solution.py:596
  95.7 4.2 %collective-permute-start.17 = (f32[248,128]{1,0:T(8,128)S(1)}, f32[248,128]{1,0:T(8,128)S(1)}, u32[]{:S(2)}, u32[]{:S(2)}) collective-permute-start(f32[248,128]{1,0:T(8,128)S(1)} %get-tuple-element.102), channel_id=1, source_target_pairs={{0,7},{1,0},{2,1},{3,2},{4,3},{5,4},{6,5},{7,6},{8,15},{9,8},{10,9... | collective-permute-start | bytes 380936 | tf_op jit(solution)/shard_map/ppermute | solution.py:668
  100.0 3.0 %collective-permute-done.16.refs_1_.refs_13_ = f32[248,128]{1,0:T(8,128)S(1)} collective-permute-done((f32[248,128]{1,0:T(8,128)S(1)}, f32[248,128]{1,0:T(8,128)S(1)}, u32[]{:S(2)}, u32[]{:S(2)}) %collective-permute-start.16) | collective-permute-done | bytes 127008 | tf_op jit(solution)/shard_map/ppermute | solution.py:668
  103.4 4.2 %shard_map.110 = (f32[32,40,128]{2,1,0:T(8,128)S(1)}, f32[8,16,128]{2,1,0:T(8,128)S(1)}, f32[200,128]{1,0:T(8,128)S(1)}, f32[200,128]{1,0:T(8,128)S(1)}) custom-call(f32[8,16,128]{2,1,0:T(8,128)S(1)} %get-tuple-element.100.refs_0_, f32[248,128]{1,0:T(8,128)S(1)} %collective-permute-done.16.refs_1_.refs_13_, ...), custom_call_target="tpu_custom_call" | custom-call | tf_op jit(solution)/shard_map/pallas_call | solution.py:596
  107.6 4.7 %collective-permute-start.19 = (f32[200,128]{1,0:T(8,128)S(1)}, f32[200,128]{1,0:T(8,128)S(1)}, u32[]{:S(2)}, u32[]{:S(2)}) collective-permute-start(f32[200,128]{1,0:T(8,128)S(1)} %get-tuple-element.107), channel_id=1, source_target_pairs={{0,7},{1,0},{2,1},{3,2},{4,3},{5,4},{6,5},{7,6},{8,15},{9,8},{10,9... | collective-permute-start | bytes 307208 | tf_op jit(solution)/shard_map/ppermute | solution.py:668
  112.3 2.6 %collective-permute-done.18.refs_2_ = f32[200,128]{1,0:T(8,128)S(1)} collective-permute-done((f32[200,128]{1,0:T(8,128)S(1)}, f32[200,128]{1,0:T(8,128)S(1)}, u32[]{:S(2)}, u32[]{:S(2)}) %collective-permute-start.18) | collective-permute-done | bytes 102432 | tf_op jit(solution)/shard_map/ppermute | solution.py:668
  115.0 4.6 %shard_map.111 = (f32[32,40,128]{2,1,0:T(8,128)S(1)}, f32[32,40,128]{2,1,0:T(8,128)S(1)}, f32[8,16,128]{2,1,0:T(8,128)S(1)}, f32[248,128]{1,0:T(8,128)S(1)}, f32...) custom-call(s32[2]{0:T(128)S(1)} %pad_add_fusion.refs_0_, f32[8,16,128]{2,1,0:T(8,128)S(1)} %get-tuple-element.105.refs_1_, ...), custom_call_target="tpu_custom_call" | custom-call | tf_op jit(solution)/shard_map/pallas_call | solution.py:596
  119.6 4.8 %collective-permute-start.21 = (f32[248,128]{1,0:T(8,128)S(1)}, f32[248,128]{1,0:T(8,128)S(1)}, u32[]{:S(2)}, u32[]{:S(2)}) collective-permute-start(f32[248,128]{1,0:T(8,128)S(1)} %get-tuple-element.112), channel_id=1, source_target_pairs={{0,7},{1,0},{2,1},{3,2},{4,3},{5,4},{6,5},{7,6},{8,15},{9,8},{10,9... | collective-permute-start | bytes 380936 | tf_op jit(solution)/shard_map/ppermute | solution.py:668
  124.4 2.8 %collective-permute-done.20.refs_1_.refs_13_ = f32[248,128]{1,0:T(8,128)S(1)} collective-permute-done((f32[248,128]{1,0:T(8,128)S(1)}, f32[248,128]{1,0:T(8,128)S(1)}, u32[]{:S(2)}, u32[]{:S(2)}) %collective-permute-start.20) | collective-permute-done | bytes 127008 | tf_op jit(solution)/shard_map/ppermute | solution.py:668
  127.2 4.2 %shard_map.112 = (f32[32,40,128]{2,1,0:T(8,128)S(1)}, f32[8,16,128]{2,1,0:T(8,128)S(1)}, f32[200,128]{1,0:T(8,128)S(1)}, f32[200,128]{1,0:T(8,128)S(1)}) custom-call(f32[8,16,128]{2,1,0:T(8,128)S(1)} %get-tuple-element.110.refs_0_, f32[248,128]{1,0:T(8,128)S(1)} %collective-permute-done.20.refs_1_.refs_13_, ...), custom_call_target="tpu_custom_call" | custom-call | tf_op jit(solution)/shard_map/pallas_call | solution.py:596
  131.5 4.8 %collective-permute-start.23 = (f32[200,128]{1,0:T(8,128)S(1)}, f32[200,128]{1,0:T(8,128)S(1)}, u32[]{:S(2)}, u32[]{:S(2)}) collective-permute-start(f32[200,128]{1,0:T(8,128)S(1)} %get-tuple-element.117), channel_id=1, source_target_pairs={{0,7},{1,0},{2,1},{3,2},{4,3},{5,4},{6,5},{7,6},{8,15},{9,8},{10,9... | collective-permute-start | bytes 307208 | tf_op jit(solution)/shard_map/ppermute | solution.py:668
  136.3 2.6 %collective-permute-done.22.refs_2_ = f32[200,128]{1,0:T(8,128)S(1)} collective-permute-done((f32[200,128]{1,0:T(8,128)S(1)}, f32[200,128]{1,0:T(8,128)S(1)}, u32[]{:S(2)}, u32[]{:S(2)}) %collective-permute-start.22) | collective-permute-done | bytes 102432 | tf_op jit(solution)/shard_map/ppermute | solution.py:668
  138.9 4.8 %shard_map.113 = f32[8,32,128]{2,1,0:T(8,128)} custom-call(s32[2]{0:T(128)S(1)} %pad_add_fusion.refs_0_, f32[8,16,128]{2,1,0:T(8,128)S(1)} %get-tuple-element.115.refs_1_, f32[200,128]{1,0:T(8,128)S(1)} %collective-permute-done.22.refs_2_, f32[200,128]{1,0:T(8,128)S(1)} %collective-permute-done.23.refs_3_, ...), custom_call_target="tpu_custom_call" | custom-call | tf_op jit(solution)/shard_map/pallas_call | solution.py:596
  (45 shorter events, 11.5 us)
Async XLA Ops:
  3.8 18.8 %collective-permute-start = (f32[1352,128]{1,0:T(8,128)}, f32[1352,128]{1,0:T(8,128)S(1)}, u32[]{:S(2)}, u32[]{:S(2)}) collective-permute-start(f32[1352,128]{1,0:T(8,128)} %get-tuple-element.62.refs_1_), channel_id=1, source_target_pairs={{0,16},{8,24},{16,0},{24,8},{1,17},{9,25},{17,1},{25,9},{2,18},{10... | collective-permute-start | bytes 2076680 | tf_op jit(solution)/shard_map/ppermute | solution.py:618
  6.8 8.5 %collective-permute-start.3 = (f32[296,128]{1,0:T(8,128)}, f32[296,128]{1,0:T(8,128)S(1)}, u32[]{:S(2)}, u32[]{:S(2)}) collective-permute-start(f32[296,128]{1,0:T(8,128)} %get-tuple-element.63), channel_id=1, source_target_pairs={{0,1},{1,2},{2,3},{3,4},{4,5},{5,6},{6,7},{7,0},{8,9},{9,10},{10,1... | collective-permute-start | bytes 454664 | tf_op jit(solution)/shard_map/ppermute | solution.py:668
  8.3 14.2 %collective-permute-start.4 = (f32[296,128]{1,0:T(8,128)}, f32[296,128]{1,0:T(8,128)S(1)}, u32[]{:S(2)}, u32[]{:S(2)}) collective-permute-start(f32[296,128]{1,0:T(8,128)} %get-tuple-element.64), channel_id=1, source_target_pairs={{0,7},{1,0},{2,1},{3,2},{4,3},{5,4},{6,5},{7,6},{8,15},{9,8},{10,9... | collective-permute-start | bytes 454664 | tf_op jit(solution)/shard_map/ppermute | solution.py:668
  11.6 20.8 %collective-permute-start.1 = (f32[1352,128]{1,0:T(8,128)}, f32[1352,128]{1,0:T(8,128)S(1)}, u32[]{:S(2)}, u32[]{:S(2)}) collective-permute-start(f32[1352,128]{1,0:T(8,128)} %get-tuple-element.62.refs_1_), channel_id=1, source_target_pairs={{0,8},{8,0},{16,24},{24,16},{1,9},{9,1},{17,25},{25,17},{2,10},{10... | collective-permute-start | bytes 2076680 | tf_op jit(solution)/shard_map/ppermute | solution.py:620
  22.6 11.3 %collective-permute-start.2 = (f32[1352,128]{1,0:T(8,128)S(1)}, f32[1352,128]{1,0:T(8,128)S(1)}, u32[]{:S(2)}, u32[]{:S(2)}) collective-permute-start(f32[1352,128]{1,0:T(8,128)S(1)} %collective-permute-done.refs_2_), channel_id=1, source_target_pairs={{0,8},{8,0},{16,24},{24,16},{1,9},{9,1},{17,25},{25,17},{2,10},{10... | collective-permute-start | bytes 2076680 | tf_op jit(solution)/shard_map/ppermute | solution.py:620
  22.6 9.7 %collective-permute-start.5 = (f32[592,128]{1,0:T(8,128)S(1)}, f32[592,128]{1,0:T(8,128)S(1)}, u32[]{:S(2)}, u32[]{:S(2)}) collective-permute-start(f32[592,128]{1,0:T(8,128)S(1)} %constant_dynamic-update-slice_fusion.refs_5_), channel_id=1, source_target_pairs={{0,16},{8,24},{16,0},{24,8},{1,17},{9,25},{17,1},{25,9},{2,18},{10... | collective-permute-start | bytes 909320 | tf_op jit(solution)/shard_map/ppermute | solution.py:618
  24.4 7.9 %collective-permute-start.6 = (f32[592,128]{1,0:T(8,128)S(1)}, f32[592,128]{1,0:T(8,128)S(1)}, u32[]{:S(2)}, u32[]{:S(2)}) collective-permute-start(f32[592,128]{1,0:T(8,128)S(1)} %constant_dynamic-update-slice_fusion.refs_5_), channel_id=1, source_target_pairs={{0,8},{8,0},{16,24},{24,16},{1,9},{9,1},{17,25},{25,17},{2,10},{10... | collective-permute-start | bytes 909320 | tf_op jit(solution)/shard_map/ppermute | solution.py:620
  32.2 1.6 %collective-permute-start.7 = (f32[592,128]{1,0:T(8,128)S(1)}, f32[592,128]{1,0:T(8,128)S(1)}, u32[]{:S(2)}, u32[]{:S(2)}) collective-permute-start(f32[592,128]{1,0:T(8,128)S(1)} %collective-permute-done.5.refs_6_), channel_id=1, source_target_pairs={{0,8},{8,0},{16,24},{24,16},{1,9},{9,1},{17,25},{25,17},{2,10},{10... | collective-permute-start | bytes 909320 | tf_op jit(solution)/shard_map/ppermute | solution.py:620
  33.8 1.1 copy-start
  42.9 8.6 %collective-permute-start.8 = (f32[248,128]{1,0:T(8,128)S(1)}, f32[248,128]{1,0:T(8,128)S(1)}, u32[]{:S(2)}, u32[]{:S(2)}) collective-permute-start(f32[248,128]{1,0:T(8,128)S(1)} %get-tuple-element.66), channel_id=1, source_target_pairs={{0,1},{1,2},{2,3},{3,4},{4,5},{5,6},{6,7},{7,0},{8,9},{9,10},{10,1... | collective-permute-start | bytes 380936 | tf_op jit(solution)/shard_map/ppermute | solution.py:668
  44.7 7.9 %collective-permute-start.9 = (f32[248,128]{1,0:T(8,128)S(1)}, f32[248,128]{1,0:T(8,128)S(1)}, u32[]{:S(2)}, u32[]{:S(2)}) collective-permute-start(f32[248,128]{1,0:T(8,128)S(1)} %get-tuple-element.67), channel_id=1, source_target_pairs={{0,7},{1,0},{2,1},{3,2},{4,3},{5,4},{6,5},{7,6},{8,15},{9,8},{10,9... | collective-permute-start | bytes 380936 | tf_op jit(solution)/shard_map/ppermute | solution.py:668
  56.8 7.5 %collective-permute-start.10 = (f32[200,128]{1,0:T(8,128)S(1)}, f32[200,128]{1,0:T(8,128)S(1)}, u32[]{:S(2)}, u32[]{:S(2)}) collective-permute-start(f32[200,128]{1,0:T(8,128)S(1)} %get-tuple-element.85), channel_id=1, source_target_pairs={{0,1},{1,2},{2,3},{3,4},{4,5},{5,6},{6,7},{7,0},{8,9},{9,10},{10,1... | collective-permute-start | bytes 307208 | tf_op jit(solution)/shard_map/ppermute | solution.py:668
  57.1 7.4 %collective-permute-start.11 = (f32[200,128]{1,0:T(8,128)S(1)}, f32[200,128]{1,0:T(8,128)S(1)}, u32[]{:S(2)}, u32[]{:S(2)}) collective-permute-start(f32[200,128]{1,0:T(8,128)S(1)} %get-tuple-element.86), channel_id=1, source_target_pairs={{0,7},{1,0},{2,1},{3,2},{4,3},{5,4},{6,5},{7,6},{8,15},{9,8},{10,9... | collective-permute-start | bytes 307208 | tf_op jit(solution)/shard_map/ppermute | solution.py:668
  69.0 7.8 %collective-permute-start.12 = (f32[248,128]{1,0:T(8,128)S(1)}, f32[248,128]{1,0:T(8,128)S(1)}, u32[]{:S(2)}, u32[]{:S(2)}) collective-permute-start(f32[248,128]{1,0:T(8,128)S(1)} %get-tuple-element.91), channel_id=1, source_target_pairs={{0,1},{1,2},{2,3},{3,4},{4,5},{5,6},{6,7},{7,0},{8,9},{9,10},{10,1... | collective-permute-start | bytes 380936 | tf_op jit(solution)/shard_map/ppermute | solution.py:668
  69.6 8.4 %collective-permute-start.13 = (f32[248,128]{1,0:T(8,128)S(1)}, f32[248,128]{1,0:T(8,128)S(1)}, u32[]{:S(2)}, u32[]{:S(2)}) collective-permute-start(f32[248,128]{1,0:T(8,128)S(1)} %get-tuple-element.92), channel_id=1, source_target_pairs={{0,7},{1,0},{2,1},{3,2},{4,3},{5,4},{6,5},{7,6},{8,15},{9,8},{10,9... | collective-permute-start | bytes 380936 | tf_op jit(solution)/shard_map/ppermute | solution.py:668
  82.2 8.0 %collective-permute-start.14 = (f32[200,128]{1,0:T(8,128)S(1)}, f32[200,128]{1,0:T(8,128)S(1)}, u32[]{:S(2)}, u32[]{:S(2)}) collective-permute-start(f32[200,128]{1,0:T(8,128)S(1)} %get-tuple-element.96), channel_id=1, source_target_pairs={{0,1},{1,2},{2,3},{3,4},{4,5},{5,6},{6,7},{7,0},{8,9},{9,10},{10,1... | collective-permute-start | bytes 307208 | tf_op jit(solution)/shard_map/ppermute | solution.py:668
  82.3 7.9 %collective-permute-start.15 = (f32[200,128]{1,0:T(8,128)S(1)}, f32[200,128]{1,0:T(8,128)S(1)}, u32[]{:S(2)}, u32[]{:S(2)}) collective-permute-start(f32[200,128]{1,0:T(8,128)S(1)} %get-tuple-element.97), channel_id=1, source_target_pairs={{0,7},{1,0},{2,1},{3,2},{4,3},{5,4},{6,5},{7,6},{8,15},{9,8},{10,9... | collective-permute-start | bytes 307208 | tf_op jit(solution)/shard_map/ppermute | solution.py:668
  95.2 7.7 %collective-permute-start.16 = (f32[248,128]{1,0:T(8,128)S(1)}, f32[248,128]{1,0:T(8,128)S(1)}, u32[]{:S(2)}, u32[]{:S(2)}) collective-permute-start(f32[248,128]{1,0:T(8,128)S(1)} %get-tuple-element.101), channel_id=1, source_target_pairs={{0,1},{1,2},{2,3},{3,4},{4,5},{5,6},{6,7},{7,0},{8,9},{9,10},{10,1... | collective-permute-start | bytes 380936 | tf_op jit(solution)/shard_map/ppermute | solution.py:668
  95.7 7.6 %collective-permute-start.17 = (f32[248,128]{1,0:T(8,128)S(1)}, f32[248,128]{1,0:T(8,128)S(1)}, u32[]{:S(2)}, u32[]{:S(2)}) collective-permute-start(f32[248,128]{1,0:T(8,128)S(1)} %get-tuple-element.102), channel_id=1, source_target_pairs={{0,7},{1,0},{2,1},{3,2},{4,3},{5,4},{6,5},{7,6},{8,15},{9,8},{10,9... | collective-permute-start | bytes 380936 | tf_op jit(solution)/shard_map/ppermute | solution.py:668
  107.6 7.4 %collective-permute-start.18 = (f32[200,128]{1,0:T(8,128)S(1)}, f32[200,128]{1,0:T(8,128)S(1)}, u32[]{:S(2)}, u32[]{:S(2)}) collective-permute-start(f32[200,128]{1,0:T(8,128)S(1)} %get-tuple-element.106), channel_id=1, source_target_pairs={{0,1},{1,2},{2,3},{3,4},{4,5},{5,6},{6,7},{7,0},{8,9},{9,10},{10,1... | collective-permute-start | bytes 307208 | tf_op jit(solution)/shard_map/ppermute | solution.py:668
  107.6 7.3 %collective-permute-start.19 = (f32[200,128]{1,0:T(8,128)S(1)}, f32[200,128]{1,0:T(8,128)S(1)}, u32[]{:S(2)}, u32[]{:S(2)}) collective-permute-start(f32[200,128]{1,0:T(8,128)S(1)} %get-tuple-element.107), channel_id=1, source_target_pairs={{0,7},{1,0},{2,1},{3,2},{4,3},{5,4},{6,5},{7,6},{8,15},{9,8},{10,9... | collective-permute-start | bytes 307208 | tf_op jit(solution)/shard_map/ppermute | solution.py:668
  119.6 7.7 %collective-permute-start.20 = (f32[248,128]{1,0:T(8,128)S(1)}, f32[248,128]{1,0:T(8,128)S(1)}, u32[]{:S(2)}, u32[]{:S(2)}) collective-permute-start(f32[248,128]{1,0:T(8,128)S(1)} %get-tuple-element.111), channel_id=1, source_target_pairs={{0,1},{1,2},{2,3},{3,4},{4,5},{5,6},{6,7},{7,0},{8,9},{9,10},{10,1... | collective-permute-start | bytes 380936 | tf_op jit(solution)/shard_map/ppermute | solution.py:668
  119.6 7.6 %collective-permute-start.21 = (f32[248,128]{1,0:T(8,128)S(1)}, f32[248,128]{1,0:T(8,128)S(1)}, u32[]{:S(2)}, u32[]{:S(2)}) collective-permute-start(f32[248,128]{1,0:T(8,128)S(1)} %get-tuple-element.112), channel_id=1, source_target_pairs={{0,7},{1,0},{2,1},{3,2},{4,3},{5,4},{6,5},{7,6},{8,15},{9,8},{10,9... | collective-permute-start | bytes 380936 | tf_op jit(solution)/shard_map/ppermute | solution.py:668
  131.4 7.5 %collective-permute-start.22 = (f32[200,128]{1,0:T(8,128)S(1)}, f32[200,128]{1,0:T(8,128)S(1)}, u32[]{:S(2)}, u32[]{:S(2)}) collective-permute-start(f32[200,128]{1,0:T(8,128)S(1)} %get-tuple-element.116), channel_id=1, source_target_pairs={{0,1},{1,2},{2,3},{3,4},{4,5},{5,6},{6,7},{7,0},{8,9},{9,10},{10,1... | collective-permute-start | bytes 307208 | tf_op jit(solution)/shard_map/ppermute | solution.py:668
  131.5 7.4 %collective-permute-start.23 = (f32[200,128]{1,0:T(8,128)S(1)}, f32[200,128]{1,0:T(8,128)S(1)}, u32[]{:S(2)}, u32[]{:S(2)}) collective-permute-start(f32[200,128]{1,0:T(8,128)S(1)} %get-tuple-element.117), channel_id=1, source_target_pairs={{0,7},{1,0},{2,1},{3,2},{4,3},{5,4},{6,5},{7,6},{8,15},{9,8},{10,9... | collective-permute-start | bytes 307208 | tf_op jit(solution)/shard_map/ppermute | solution.py:668

commit v3 on v2

--- a/solution.py
+++ b/solution.py
@@ -16,6 +16,10 @@
 F_OWN, M_OWN = 12, 24
 HALO_B, SKIP_B, HALO_X, SKIP_X = 4, 2, 3, 1
 REACH_B, REACH_X = 14, 12
+FIRST_ROWS = (7, 6, 3, 3, 3)
+FIRST_AT = (0, 56, 104, 128, 152)
+FIRST_WELLS, FIRST_MID, FIRST_SIZE = 176, 184, 248
+OWN_WELLS, LATE_MID, LATE_BELOW, LATE_ABOVE = 1024, 256, 320, 384
 ROWS = 32
 
 
@@ -235,28 +239,25 @@
 
 def first_kernel(use_list, *refs):
     if use_list:
-        counts, cells, owners, starts, log, sto, per, bp, rows, own, up, down, tmp, masked = refs
+        counts, cells, owners, starts, log, sto, per, bp, rows, own, late, up, down, tmp, masked = refs
     else:
-        log, sto, per, bp, own, up, down, tmp = refs
-    for ref, at in ((own, 1344), (up, 288), (down, 288)):
+        log, sto, per, bp, own, late, up, down, tmp = refs
+    for ref, at in ((own, OWN_WELLS), (up, FIRST_WELLS), (down, FIRST_WELLS)):
         ref[ds(at, WELLS), :] = jnp.zeros((WELLS, 128), jnp.float32)
     if use_list:
         for j, value in enumerate(listed_wells(rows, counts, cells, owners, starts, masked)):
-            for ref, at in ((own, 1344), (up, 288), (down, 288)):
+            for ref, at in ((own, OWN_WELLS), (up, FIRST_WELLS), (down, FIRST_WELLS)):
                 ref[ds(at + j, 1), :] = value
     odd = lanes((16, 128)) % 2 == 1
     fields = (log, sto, per, bp.at[0], bp.at[1])
     for f, ref in enumerate(fields):
         for x in range(8):
-            own[ds(f * 256 + x * 32, 32), :] = ref[x]
-    for f in range(2):
+            out, at = (own, f * 256) if f < 4 else (late, 0)
+            out[ds(at + x * 32, 32), :] = ref[x]
+    for f, (number, at) in enumerate(zip(FIRST_ROWS, FIRST_AT)):
         for x in range(8):
-            up[ds(f * 64 + x * 8, 8), :] = fields[f][x, ds(24, 8), :]
-            down[ds(f * 64 + x * 8, 8), :] = fields[f][x, ds(0, 8), :]
-    for f in range(3):
-        for x in range(8):
-            up[ds(128 + f * 32 + x * 4, 4), :] = fields[f + 2][x, ds(28, 4), :]
-            down[ds(128 + f * 32 + x * 4, 4), :] = fields[f + 2][x, ds(0, 4), :]
+            up[ds(at + x * number, number), :] = fields[f][x, ds(32 - number, number), :]
+            down[ds(at + x * number, number), :] = fields[f][x, ds(0, number), :]
     for i in range(4):
         tmp[0, i] = log[2 * i] + log[2 * i + 1]
         tmp[1, i] = sto[2 * i] + sto[2 * i + 1]
@@ -267,9 +268,9 @@
         value = 0.125 * jnp.where(
             odd, second + pltpu.roll(second, 1, 1), first + pltpu.roll(first, 127, 1)
         )
-        own[ds(1280 + 16 * i, 16), :] = value
-        up[ds(224 + 16 * i, 16), :] = value
-        down[ds(224 + 16 * i, 16), :] = value
+        late[ds(LATE_MID + 16 * i, 16), :] = value
+        up[ds(FIRST_MID + 16 * i, 16), :] = value
+        down[ds(FIRST_MID + 16 * i, 16), :] = value
 
 
 def faces(e, kx, ky, kz, count, size, shift, factor, unroll):
@@ -302,51 +303,61 @@
     )
 
 
+def blank(number):
+    return jnp.zeros((number, 128), jnp.float32)
+
+
+def place_rows(buf, slab, own, at, halo, f, x, keep_low, keep_high):
+    number, start = FIRST_ROWS[f], FIRST_AT[f] + x * FIRST_ROWS[f]
+    under, over = halo[ds(start, number), :], halo[ds(FIRST_MID + start, number), :]
+    if f >= 2:
+        under, over = under * keep_low, over * keep_high
+    buf[slab, ds(F_OWN, ROWS), :] = own[ds(at, ROWS), :]
+    buf[slab, ds(F_OWN - number, number), :] = under
+    buf[slab, ds(F_OWN + ROWS, number), :] = over
+    buf[slab, ds(0, F_OWN - number), :] = blank(F_OWN - number)
+    buf[slab, ds(F_OWN + ROWS + number, F_OWN - number), :] = blank(F_OWN - number)
+
+
+def tile_of(index, gx, tiles):
+    half = tiles // 2
+    k, other = index % half, index // half
+    return ((gx // 2 + half - k) % half) * 2 + (gx % 2 + other) % 2
+
+
+def change_terms(x, kx, ky, kz, per, bp):
+    rows, plus, minus = ds(8, 40), ds(9, 40), ds(7, 40)
+    face = kz[x, rows, :]
+    c, p = per[x + 1, rows, :], bp[x + 1, rows, :]
+    total = kx[x, rows, :] * (c + per[x, rows, :]) * (p - bp[x, rows, :])
+    total = total + kx[x + 1, rows, :] * (c + per[x + 2, rows, :]) * (p - bp[x + 2, rows, :])
+    total = total + ky[x, minus, :] * (c + per[x + 1, minus, :]) * (p - bp[x + 1, minus, :])
+    total = total + ky[x, rows, :] * (c + per[x + 1, plus, :]) * (p - bp[x + 1, plus, :])
+    flux = face * (c + pltpu.roll(c, 127, 1)) * (p - pltpu.roll(p, 127, 1))
+    return 0.5 * (total + flux - pltpu.roll(flux, 1, 1))
+
+
 def second_kernel(nx, n_gy, unroll, *refs):
     tiles = nx // 8
     place = refs[0]
     owns, halos = refs[1 : 1 + tiles], refs[1 + tiles : 1 + 2 * tiles]
-    (kx, ky, kz, w, diag, sto_out, d_one, bp_out, mkx, mky, mkz, mw, mdiag, ckx, cky, ckz, cw) = refs[
-        1 + 2 * tiles : 18 + 2 * tiles
-    ]
-    b_out, x_out, b1_own, up, down, wells = refs[18 + 2 * tiles : 24 + 2 * tiles]
-    e, sto, per, bp0, bp1, x_a, x_b, b_buf, f_tmp, e_mid, s_mid, e_co, s_co, m_tmp, m_tmp2 = refs[24 + 2 * tiles :]
+    kx, ky, kz, w, diag, sto_out, per, bp0 = refs[1 + 2 * tiles : 9 + 2 * tiles]
+    b_out, x_out, b1_own, up, down, wells = refs[9 + 2 * tiles : 15 + 2 * tiles]
+    e, sto, x_a, x_b, b_buf, f_tmp = refs[15 + 2 * tiles :]
     gx, gy = place[0], place[1]
     first, last = gy == 0, gy == n_gy - 1
-    for buf in (e, per, bp0, bp1, x_a, x_b):
+    for buf in (e, per, bp0, x_a, x_b):
         zero_ends(buf, nx)
-    half, core = tiles // 2, gx % 2
-
-    def tile_of(index):
-        k, other = index % half, index // half
-        return ((gx // 2 + half - k) % half) * 2 + (core + other) % 2
-
-    blank = jnp.zeros((4, 128), jnp.float32)
-    blank8 = jnp.zeros((8, 128), jnp.float32)
     keep_low = jnp.where(first, 0.0, 1.0)
     keep_high = jnp.where(last, 0.0, 1.0)
     for index in range(tiles):
         own, halo = owns[index], halos[index]
-        base = tile_of(index) * 8
-
-        def body(x, own=own, halo=halo, base=base):
-            for f, buf in enumerate((e, sto, per, bp0, bp1)):
+        base = tile_of(index, gx, tiles) * 8
+
+        for x in range(8):
+            for f, buf in enumerate((e, sto, per, bp0)):
                 slab = base + x + (0 if f == 1 else 1)
-                buf[slab, ds(12, 32), :] = own[ds(f * 256 + x * 32, 32), :]
-                if f < 2:
-                    buf[slab, ds(4, 8), :] = halo[ds(f * 64 + x * 8, 8), :]
-                    buf[slab, ds(44, 8), :] = halo[ds(296 + f * 64 + x * 8, 8), :]
-                    buf[slab, ds(0, 4), :] = blank
-                    buf[slab, ds(52, 4), :] = blank
-                else:
-                    at = 128 + (f - 2) * 32 + x * 4
-                    buf[slab, ds(0, 8), :] = blank8
-                    buf[slab, ds(48, 8), :] = blank8
-                    buf[slab, ds(8, 4), :] = halo[ds(at, 4), :] * keep_low
-                    buf[slab, ds(44, 4), :] = halo[ds(296 + at, 4), :] * keep_high
-
-        for x in range(8):
-            body(x)
+                place_rows(buf, slab, own, f * 256 + x * 32, halo, f, x, keep_low, keep_high)
     fine_inside = inside(FR, F_OWN, ROWS, first, last)
 
     def exps(x):
@@ -361,60 +372,65 @@
     def diagonals(x):
         value = diagonal(sto[x, ds(4, 48), :], kx, ky, kz, x, 4, 48, 1)
         w[x, ds(4, 48), :] = jnp.where(win_inside, OMEGA / value, 0.0)
-        w[x, ds(0, 4), :] = blank
-        w[x, ds(52, 4), :] = blank
+        w[x, ds(0, 4), :] = blank(4)
+        w[x, ds(52, 4), :] = blank(4)
         diag[x] = value[8:40]
         sto_out[x] = sto[x, ds(8, 40), :]
 
     loop(nx, diagonals, unroll)
 
     def changes(x):
-        rows, plus, minus = ds(8, 40), ds(9, 40), ds(7, 40)
-        kl, kr, kp, km, face = kx[x, rows, :], kx[x + 1, rows, :], ky[x, rows, :], ky[x, minus, :], kz[x, rows, :]
-        c = per[x + 1, rows, :]
-        weights = (
-            kl * 0.5 * (c + per[x, rows, :]),
-            kr * 0.5 * (c + per[x + 2, rows, :]),
-            km * 0.5 * (c + per[x + 1, minus, :]),
-            kp * 0.5 * (c + per[x + 1, plus, :]),
-            face * 0.5 * (c + pltpu.roll(c, 127, 1)),
-        )
-        for t, bp in enumerate((bp0, bp1)):
-            p = bp[x + 1, rows, :]
-            total = weights[0] * (p - bp[x, rows, :]) + weights[1] * (p - bp[x + 2, rows, :])
-            total = total + weights[2] * (p - bp[x + 1, minus, :]) + weights[3] * (p - bp[x + 1, plus, :])
-            flux = weights[4] * (p - pltpu.roll(p, 127, 1))
-            total = total + flux - pltpu.roll(flux, 1, 1)
-            if t == 0:
-                b_buf[x, rows, :] = -total
-            else:
-                d_one[x] = total
+        b_buf[x, ds(8, 40), :] = -change_terms(x, kx, ky, kz, per, bp0)
 
     loop(nx, changes, unroll)
-    for x in range(10):
-        bp_out[0, x] = bp0[gx * 8 + x]
-        bp_out[1, x] = bp1[gx * 8 + x]
-
     lane = lanes((WELLS, 128))
     listed = 128 // tiles
-    for refs_of, at, out in ((owns, 1344, wells), (halos, 288, up), (halos, 584, down)):
+    for refs_of, at, out in ((owns, OWN_WELLS, wells), (halos, FIRST_WELLS, up), (halos, FIRST_MID + FIRST_WELLS, down)):
         value = refs_of[0][ds(at, WELLS), :]
         for index in range(1, tiles):
             moved = pltpu.roll(refs_of[index][ds(at, WELLS), :], index * listed, 1)
             value = jnp.where(lane >= index * listed, moved, value)
         out[ds(out.shape[0] - WELLS, WELLS), :] = value
+    begin_solve(b_buf, x_a, x_b, (kx, ky, kz, w), diag, f_tmp, b_out, x_out, b1_own, up, down, nx, unroll)
+
+
+def third_kernel(nx, n_gy, unroll, *refs):
+    tiles = nx // 8
+    half = tiles // 2
+    place = refs[0]
+    lates, halos = refs[1 : 1 + tiles], refs[1 + tiles : 1 + 2 * tiles]
+    kx, ky, kz, per, bp0 = refs[1 + 2 * tiles : 6 + 2 * tiles]
+    d_one, bp_out, mkx, mky, mkz, mw, mdiag, ckx, cky, ckz, cw = refs[6 + 2 * tiles : 17 + 2 * tiles]
+    bp1, e_mid, s_mid, e_co, s_co, m_tmp, m_tmp2 = refs[17 + 2 * tiles :]
+    gx, gy = place[0], place[1]
+    first, last = gy == 0, gy == n_gy - 1
+    keep_low = jnp.where(first, 0.0, 1.0)
+    keep_high = jnp.where(last, 0.0, 1.0)
+    zero_ends(bp1, nx)
+    for index in range(tiles):
+        base = tile_of(index, gx, tiles) * 8 + 1
+        for x in range(8):
+            place_rows(bp1, base + x, lates[index], x * 32, halos[index], 4, x, keep_low, keep_high)
+
+    def changes(x):
+        d_one[x] = change_terms(x, kx, ky, kz, per, bp1)
+
+    loop(nx, changes, unroll)
+    for x in range(10):
+        bp_out[0, x] = bp0[gx * 8 + x]
+        bp_out[1, x] = bp1[gx * 8 + x]
 
     count = nx // 4
     odd = lanes((16, 128)) % 2 == 1
     for index in range(tiles):
-        own, halo = owns[index], halos[index]
-        tile = tile_of(index)
+        late = lates[index]
+        tile = tile_of(index, gx, tiles)
         upper = tile >= half
         base = jnp.where(upper, tile - half, tile) * 4
         mask = odd == upper
         for i in range(4):
-            for start, ref, at in ((8, halo, 224 + 16 * i), (24, own, 1280 + 16 * i), (40, halo, 520 + 16 * i)):
-                value = ref[ds(at, 16), :]
+            for start, at in ((8, LATE_BELOW), (24, LATE_MID), (40, LATE_ABOVE)):
+                value = late[ds(at + 16 * i, 16), :]
                 left, right = pltpu.roll(value, 127, 1), pltpu.roll(value, 1, 1)
                 log_part, sto_part = jnp.where(odd, right, value), jnp.where(odd, value, left)
                 rows = ds(start, 16)
@@ -447,7 +463,6 @@
                 diag_l[i, rows, :] = value
                 diag_l[i, ds(0, 8), :] = edge
                 diag_l[i, ds(size - 8, 8), :] = edge
-    begin_solve(b_buf, x_a, x_b, (kx, ky, kz, w), diag, f_tmp, b_out, x_out, b1_own, up, down, nx, unroll)
 
 
 def forward(below, above, up, down):
@@ -610,14 +625,21 @@
     return [(i, (i + step) % count) for i in range(count)]
 
 
-def gathered(array, tiles):
+def same_core(array, tiles):
     half = tiles // 2
-    same = [array]
+    parts = []
     for k in range(1, half):
         perm = [(2 * a + c, 2 * ((a + k) % half) + c) for a in range(half) for c in range(2)]
-        same.append(lax.ppermute(array, "gx", perm))
-    swap = [(i, i ^ 1) for i in range(tiles)]
-    return same + [lax.ppermute(part, "gx", swap) for part in same]
+        parts.append(lax.ppermute(array, "gx", perm))
+    return parts
+
+
+def other_core(array, tiles):
+    return lax.ppermute(array, "gx", [(i, i ^ 1) for i in range(tiles)])
+
+
+def all_parts(array, swapped, same, tiles):
+    return [array] + list(same) + [swapped] + [other_core(part, tiles) for part in same]
 
 
 def gathered_wells(rows, cells, counts, owners, starts):
@@ -671,19 +693,25 @@
     listed, samples = well_rows.shape
     owners = well_owner.reshape(listed)
     use_list = n_gy == 8 and tiles * listed == 128
-    own, up, down = call(
+    own, late, up, down = call(
         functools.partial(first_kernel, use_list),
-        [(1344 + WELLS, 128), (288 + WELLS, 128), (288 + WELLS, 128)],
+        [(OWN_WELLS + WELLS, 128), (LATE_BELOW, 128), (FIRST_SIZE, 128), (FIRST_SIZE, 128)],
         [(2, 4, 32, 128)] + ([(128, samples)] if use_list else []),
         ([well_counts, well_cells, owners, well_start] if use_list else [])
         + [log_perm, storage, perturb, base_press]
         + ([well_rows] if use_list else []),
-        0,
+        4 if use_list else 0,
         60 * 2**20,
     )
     below, above = exchange(up, down)
-    owns = gathered(own, tiles)
-    halos = gathered(jnp.concatenate([below, above], axis=0), tiles)
+    own_same, own_swapped = same_core(own, tiles), other_core(own, tiles)
+    halo = jnp.concatenate([below[:FIRST_MID], above[:FIRST_MID]], axis=0)
+    halo_same, halo_swapped = same_core(halo, tiles), other_core(halo, tiles)
+    late = jnp.concatenate([late, below[FIRST_MID:], above[FIRST_MID:]], axis=0)
+    late_same, late_swapped = same_core(late, tiles), other_core(late, tiles)
+    own_same, halo_same = lax.optimization_barrier((own_same, halo_same))
+    owns = all_parts(own, own_swapped, own_same, tiles)
+    halos = all_parts(halo, halo_swapped, halo_same, tiles)
 
     fine, fine_pad, mid, mid_pad = (nx, FR, 128), (nx + 2, FR, 128), (count, MR, 128), (count + 2, MR, 128)
     coarse, coarse_pad = (half, CR, 128), (half + 2, CR, 128)
@@ -695,24 +723,29 @@
     mid_shapes = [(count + 1, MR, 128), mid, mid, mid, mid]
     coarse_shapes = [(half + 1, CR, 128), coarse, coarse, coarse]
     outs = call(
-        functools.partial(second_kernel, nx, n_gy, min(unroll, 16)),
+        functools.partial(second_kernel, nx, n_gy, unroll),
         coeff_shapes
-        + [window, window, (2, 10, FR, 128)]
-        + mid_shapes
-        + coarse_shapes
+        + [window, fine_pad, fine_pad]
         + [window, window, b1_shape, message_b, message_b, (WELLS, 128)],
-        [fine_pad, fine, fine_pad, fine_pad, fine_pad, fine_pad, fine_pad, fine, (nx // 2, FR, 128)]
-        + [mid_pad, mid, coarse_pad, coarse, mid, mid],
+        [fine_pad, fine, fine_pad, fine_pad, fine, (nx // 2, FR, 128)],
         [place] + owns + halos,
         1,
     )
-    coeffs, (sto, d_one, bp) = outs[:5], outs[5:8]
-    levels = list(outs[8:17])
-    coeffs = list(coeffs)
-    begun = outs[17:22]
+    coeffs, sto, begun = list(outs[:5]), outs[5], outs[8:13]
+    own_wells = outs[13]
+    late_same, _ = lax.optimization_barrier((late_same, begun))
+    lates, begun = lax.optimization_barrier((all_parts(late, late_swapped, late_same, tiles), begun))
+    later = call(
+        functools.partial(third_kernel, nx, n_gy, unroll),
+        [window, (2, 10, FR, 128)] + mid_shapes + coarse_shapes,
+        [fine_pad, mid_pad, mid, coarse_pad, coarse, mid, mid],
+        [place] + lates + halos + list(outs[:3]) + list(outs[6:8]),
+        1,
+    )
+    d_one, bp, levels = later[0], later[1], list(later[2:])
     wells = None
     if use_list:
-        lists = [outs[22], begun[3][-WELLS:], begun[4][-WELLS:]]
+        lists = [own_wells, begun[3][-WELLS:], begun[4][-WELLS:]]
     else:
         wells = gathered_wells(well_rows, well_cells, well_counts, owners, well_start)
     scratch = [fine_pad, fine_pad, fine, (nx // 2, FR, 128)]

time: 144 us -> 130 us (0.903)
  waiting for transfers between devices: 43.5 us -> 32.8 us
  Pallas kernels: 46.8 us -> 42.9 us
    ppermute x6 -> x9, waiting for transfers between devices: 16.4 us -> 8.58 us  [the longest x3 6.47 us: same_core(): parts.append(lax.ppermute(array, 'gx', perm))]
    ppermute x9, waiting for transfers between devices: 24.2 us -> 20.1 us  [exchange(): lax.ppermute(up, 'gy', up_perm)]
    pallas_call x10 -> x11, Pallas kernels: 46.8 us -> 42.9 us  [call(): pl.pallas_call(kernel, out_shape=[jax.ShapeDtypeStruct(shape, f32) for sh...]
    ppermute x6 -> x9, starting transfers between devices: 5.07 us -> 6.4 us  [the longest x3 5.33 us: same_core(): parts.append(lax.ppermute(array, 'gx', perm))]
  transfers between devices with their start and end apart: 24 -> 27, of which waited for: 15 -> 18; matrix products, arithmetic and copies ran while one was open for 2% -> 3% of each run, Pallas kernels for 0% -> 7%
where the time goes in v3:
time: 130 us
  starting transfers between devices  49.4 us (38%)
  Pallas kernels  42.9 us (33%)
  waiting for transfers between devices  32.8 us (25%)
  matrix products  2.63 us (2%)
  other arithmetic  1.62 us (1%)
    pallas_call x11, Pallas kernels, call(): pl.pallas_call(kernel, out_shape=[jax.ShapeDtypeStruct(shape, f32) for sh...  42.9 us
    ppermute x9, starting transfers between devices, exchange(): lax.ppermute(down, 'gy', down_perm)  38.2 us
    ppermute x9, waiting for transfers between devices, exchange(): lax.ppermute(up, 'gy', up_perm)  20.1 us
    ppermute x3, waiting for transfers between devices, same_core(): parts.append(lax.ppermute(array, 'gx', perm))  6.47 us
    ppermute x3, starting transfers between devices, same_core(): parts.append(lax.ppermute(array, 'gx', perm))  5.33 us
    ppermute x9, starting transfers between devices, exchange(): lax.ppermute(up, 'gy', up_perm)  4.82 us
    ppermute x9, waiting for transfers between devices, exchange(): lax.ppermute(down, 'gy', down_perm)  4.14 us
    dot_general x1, matrix products, part(): return jnp.dot(left, right, precision=lax.Precision.HIGHEST)  2.63 us
  transfers between devices with their start and end apart: 27, of which 18 were waited for; matrix products, arithmetic and copies ran while one was open for 3% of the time, Pallas kernels for 7%

profile of v3, /device:TPU:0, one launch (start us, length us, event | category | flops | bytes accessed | tf_op | source)
XLA Modules:
  0.0 130.3 jit_solution(7059208538097684227)
XLA Ops:
  0.6 2.4 %shard_map.104 = (f32[1032,128]{1,0:T(8,128)}, f32[320,128]{1,0:T(8,128)}, f32[248,128]{1,0:T(8,128)}, f32[248,128]{1,0:T(8,128)}) custom-call(s32[32]{0:T(128)} %refs_0_.1, s32[32]{0:T(128)} %refs_1_.1, s32[32]{0:T(128)} %bitcast.15, s32[32]{0:T(128)} %refs_3_.1, f32[8,32,128]{2,1,0:T(8,128)} %refs_4_.1, f32[8,32,128]{2,1,0:T(8,128)} %refs_5_.1, ...), custom_call_target="tpu_custom_call" | custom-call | tf_op jit(solution)/shard_map/pallas_call | solution.py:611
  3.0 3.0 %collective-permute-start.3 = (f32[1032,128]{1,0:T(8,128)}, f32[1032,128]{1,0:T(8,128)S(1)}, u32[]{:S(2)}, u32[]{:S(2)}) collective-permute-start(f32[1032,128]{1,0:T(8,128)} %get-tuple-element.80.refs_1_), channel_id=1, source_target_pairs={{0,16},{8,24},{16,0},{24,8},{1,17},{9,25},{17,1},{25,9},{2,18},{10... | collective-permute-start | bytes 1585160 | tf_op jit(solution)/shard_map/ppermute | solution.py:633
  6.0 1.5 %collective-permute-start = (f32[248,128]{1,0:T(8,128)}, f32[248,128]{1,0:T(8,128)S(1)}, u32[]{:S(2)}, u32[]{:S(2)}) collective-permute-start(f32[248,128]{1,0:T(8,128)} %get-tuple-element.78), channel_id=1, source_target_pairs={{0,1},{1,2},{2,3},{3,4},{4,5},{5,6},{6,7},{7,0},{8,9},{9,10},{10,1... | collective-permute-start | bytes 380936 | tf_op jit(solution)/shard_map/ppermute | solution.py:690
  7.5 3.2 %collective-permute-start.1 = (f32[248,128]{1,0:T(8,128)}, f32[248,128]{1,0:T(8,128)S(1)}, u32[]{:S(2)}, u32[]{:S(2)}) collective-permute-start(f32[248,128]{1,0:T(8,128)} %get-tuple-element.79), channel_id=1, source_target_pairs={{0,7},{1,0},{2,1},{3,2},{4,3},{5,4},{6,5},{7,6},{8,15},{9,8},{10,9... | collective-permute-start | bytes 380936 | tf_op jit(solution)/shard_map/ppermute | solution.py:690
  10.8 3.2 %collective-permute-done = f32[248,128]{1,0:T(8,128)S(1)} collective-permute-done((f32[248,128]{1,0:T(8,128)}, f32[248,128]{1,0:T(8,128)S(1)}, u32[]{:S(2)}, u32[]{:S(2)}) %collective-permute-start) | collective-permute-done | bytes 127008 | tf_op jit(solution)/shard_map/ppermute | solution.py:690
  15.9 6.5 %collective-permute-done.4.refs_6_ = f32[368,128]{1,0:T(8,128)S(1)} collective-permute-done((f32[368,128]{1,0:T(8,128)S(1)}, f32[368,128]{1,0:T(8,128)S(1)}, u32[]{:S(2)}, u32[]{:S(2)}) %collective-permute-start.4) | collective-permute-done | bytes 188448 | tf_op jit(solution)/shard_map/ppermute | solution.py:633
  23.3 1.8 %collective-permute-start.2 = (f32[448,128]{1,0:T(8,128)S(1)}, f32[448,128]{1,0:T(8,128)S(1)}, u32[]{:S(2)}, u32[]{:S(2)}) collective-permute-start(f32[448,128]{1,0:T(8,128)S(1)} %pad_maximum_fusion.refs_1_), channel_id=1, source_target_pairs={{0,16},{8,24},{16,0},{24,8},{1,17},{9,25},{17,1},{25,9},{2,18},{10... | collective-permute-start | bytes 688136 | tf_op jit(solution)/shard_map/ppermute | solution.py:633
  26.8 5.1 %shard_map.105 = (f32[33,56,128]{2,1,0:T(8,128)S(1)}, f32[32,56,128]{2,1,0:T(8,128)S(1)}, f32[32,56,128]{2,1,0:T(8,128)S(1)}, f32[32,56,128]{2,1,0:T(8,128)S(1)}...) custom-call(s32[2]{0:T(128)S(1)} %pad_add_fusion.refs_0_, ...), custom_call_target="tpu_custom_call" | custom-call | tf_op jit(solution)/shard_map/pallas_call | solution.py:611
  34.9 3.2 %collective-permute-start.12 = (f32[248,128]{1,0:T(8,128)S(1)}, f32[248,128]{1,0:T(8,128)S(1)}, u32[]{:S(2)}, u32[]{:S(2)}) collective-permute-start(f32[248,128]{1,0:T(8,128)S(1)} %get-tuple-element.91), channel_id=1, source_target_pairs={{0,7},{1,0},{2,1},{3,2},{4,3},{5,4},{6,5},{7,6},{8,15},{9,8},{10,9... | collective-permute-start | bytes 380936 | tf_op jit(solution)/shard_map/ppermute | solution.py:690
  38.2 3.6 %shard_map.106 = (f32[32,40,128]{2,1,0:T(8,128)S(1)}, f32[2,10,56,128]{3,2,1,0:T(8,128)S(1)}, f32[9,64,128]{2,1,0:T(8,128)S(1)}, f32[8,64,128]{2,1,0:T(8,128)S(1...) custom-call(s32[2]{0:T(128)S(1)} %pad_add_fusion.refs_0_, ...), custom_call_target="tpu_custom_call" | custom-call | tf_op jit(solution)/shard_map/pallas_call | solution.py:611
  43.0 3.6 %shard_map.107 = (f32[32,40,128]{2,1,0:T(8,128)S(1)}, f32[8,16,128]{2,1,0:T(8,128)S(1)}, f32[200,128]{1,0:T(8,128)S(1)}, f32[200,128]{1,0:T(8,128)S(1)}) custom-call(f32[8,16,128]{2,1,0:T(8,128)S(1)} %get-tuple-element.89.refs_0_, f32[248,128]{1,0:T(8,128)S(1)} %collective-permute-done.11.refs_1_.refs_13_, ...), custom_call_target="tpu_custom_call" | custom-call | tf_op jit(solution)/shard_map/pallas_call | solution.py:611
  46.9 4.4 %collective-permute-start.14 = (f32[200,128]{1,0:T(8,128)S(1)}, f32[200,128]{1,0:T(8,128)S(1)}, u32[]{:S(2)}, u32[]{:S(2)}) collective-permute-start(f32[200,128]{1,0:T(8,128)S(1)} %get-tuple-element.116), channel_id=1, source_target_pairs={{0,7},{1,0},{2,1},{3,2},{4,3},{5,4},{6,5},{7,6},{8,15},{9,8},{10,9... | collective-permute-start | bytes 307208 | tf_op jit(solution)/shard_map/ppermute | solution.py:690
  51.4 2.7 %collective-permute-done.13.refs_2_ = f32[200,128]{1,0:T(8,128)S(1)} collective-permute-done((f32[200,128]{1,0:T(8,128)S(1)}, f32[200,128]{1,0:T(8,128)S(1)}, u32[]{:S(2)}, u32[]{:S(2)}) %collective-permute-start.13) | collective-permute-done | bytes 102432 | tf_op jit(solution)/shard_map/ppermute | solution.py:690
  54.3 4.0 %shard_map.108 = (f32[32,40,128]{2,1,0:T(8,128)S(1)}, f32[32,40,128]{2,1,0:T(8,128)S(1)}, f32[8,16,128]{2,1,0:T(8,128)S(1)}, f32[248,128]{1,0:T(8,128)S(1)}, f32...) custom-call(s32[2]{0:T(128)S(1)} %pad_add_fusion.refs_0_, f32[8,16,128]{2,1,0:T(8,128)S(1)} %get-tuple-element.114.refs_1_, ...), custom_call_target="tpu_custom_call" | custom-call | tf_op jit(solution)/shard_map/pallas_call | solution.py:611
  59.0 4.1 %collective-permute-start.16 = (f32[248,128]{1,0:T(8,128)S(1)}, f32[248,128]{1,0:T(8,128)S(1)}, u32[]{:S(2)}, u32[]{:S(2)}) collective-permute-start(f32[248,128]{1,0:T(8,128)S(1)} %get-tuple-element.122), channel_id=1, source_target_pairs={{0,7},{1,0},{2,1},{3,2},{4,3},{5,4},{6,5},{7,6},{8,15},{9,8},{10,9... | collective-permute-start | bytes 380936 | tf_op jit(solution)/shard_map/ppermute | solution.py:690
  63.2 3.0 %collective-permute-done.15.refs_1_.refs_13_ = f32[248,128]{1,0:T(8,128)S(1)} collective-permute-done((f32[248,128]{1,0:T(8,128)S(1)}, f32[248,128]{1,0:T(8,128)S(1)}, u32[]{:S(2)}, u32[]{:S(2)}) %collective-permute-start.15) | collective-permute-done | bytes 127008 | tf_op jit(solution)/shard_map/ppermute | solution.py:690
  67.2 3.6 %shard_map.109 = (f32[32,40,128]{2,1,0:T(8,128)S(1)}, f32[8,16,128]{2,1,0:T(8,128)S(1)}, f32[200,128]{1,0:T(8,128)S(1)}, f32[200,128]{1,0:T(8,128)S(1)}) custom-call(f32[8,16,128]{2,1,0:T(8,128)S(1)} %get-tuple-element.120.refs_0_, f32[248,128]{1,0:T(8,128)S(1)} %collective-permute-done.15.refs_1_.refs_13_, ...), custom_call_target="tpu_custom_call" | custom-call | tf_op jit(solution)/shard_map/pallas_call | solution.py:611
  71.0 4.7 %collective-permute-start.18 = (f32[200,128]{1,0:T(8,128)S(1)}, f32[200,128]{1,0:T(8,128)S(1)}, u32[]{:S(2)}, u32[]{:S(2)}) collective-permute-start(f32[200,128]{1,0:T(8,128)S(1)} %get-tuple-element.127), channel_id=1, source_target_pairs={{0,7},{1,0},{2,1},{3,2},{4,3},{5,4},{6,5},{7,6},{8,15},{9,8},{10,9... | collective-permute-start | bytes 307208 | tf_op jit(solution)/shard_map/ppermute | solution.py:690
  76.1 2.6 %fusion = f32[1280,256]{1,0:T(8,128)S(1)} fusion(s32[1024]{0:T(1024)S(1)} %bitcast.14, f32[1024,128]{1,0:T(8,128)S(1)} %get-tuple-element.158, f32[1024,128]{1,0:T(8,128)S(1)} %get-tuple-element.157), kind=kOutput, calls=%fused_computation.1 | convolution fusion | flops 4028104704 | bytes 2363392 | tf_op jit(solution)/shard_map/dot_general | solution.py:668
  79.0 4.6 %shard_map.110 = (f32[32,40,128]{2,1,0:T(8,128)S(1)}, f32[32,40,128]{2,1,0:T(8,128)S(1)}, f32[8,16,128]{2,1,0:T(8,128)S(1)}, f32[248,128]{1,0:T(8,128)S(1)}, f32...) custom-call(s32[2]{0:T(128)S(1)} %pad_add_fusion.refs_0_, f32[8,16,128]{2,1,0:T(8,128)S(1)} %get-tuple-element.125.refs_1_, ...), custom_call_target="tpu_custom_call" | custom-call | tf_op jit(solution)/shard_map/pallas_call | solution.py:611
  84.2 4.1 %collective-permute-start.20 = (f32[248,128]{1,0:T(8,128)S(1)}, f32[248,128]{1,0:T(8,128)S(1)}, u32[]{:S(2)}, u32[]{:S(2)}) collective-permute-start(f32[248,128]{1,0:T(8,128)S(1)} %get-tuple-element.132), channel_id=1, source_target_pairs={{0,7},{1,0},{2,1},{3,2},{4,3},{5,4},{6,5},{7,6},{8,15},{9,8},{10,9... | collective-permute-start | bytes 380936 | tf_op jit(solution)/shard_map/ppermute | solution.py:690
  88.3 3.0 %collective-permute-done.19.refs_1_.refs_13_ = f32[248,128]{1,0:T(8,128)S(1)} collective-permute-done((f32[248,128]{1,0:T(8,128)S(1)}, f32[248,128]{1,0:T(8,128)S(1)}, u32[]{:S(2)}, u32[]{:S(2)}) %collective-permute-start.19) | collective-permute-done | bytes 127008 | tf_op jit(solution)/shard_map/ppermute | solution.py:690
  91.8 3.6 %shard_map.111 = (f32[32,40,128]{2,1,0:T(8,128)S(1)}, f32[8,16,128]{2,1,0:T(8,128)S(1)}, f32[200,128]{1,0:T(8,128)S(1)}, f32[200,128]{1,0:T(8,128)S(1)}) custom-call(f32[8,16,128]{2,1,0:T(8,128)S(1)} %get-tuple-element.130.refs_0_, f32[248,128]{1,0:T(8,128)S(1)} %collective-permute-done.19.refs_1_.refs_13_, ...), custom_call_target="tpu_custom_call" | custom-call | tf_op jit(solution)/shard_map/pallas_call | solution.py:611
  95.5 4.7 %collective-permute-start.22 = (f32[200,128]{1,0:T(8,128)S(1)}, f32[200,128]{1,0:T(8,128)S(1)}, u32[]{:S(2)}, u32[]{:S(2)}) collective-permute-start(f32[200,128]{1,0:T(8,128)S(1)} %get-tuple-element.137), channel_id=1, source_target_pairs={{0,7},{1,0},{2,1},{3,2},{4,3},{5,4},{6,5},{7,6},{8,15},{9,8},{10,9... | collective-permute-start | bytes 307208 | tf_op jit(solution)/shard_map/ppermute | solution.py:690
  100.2 2.6 %collective-permute-done.21.refs_2_ = f32[200,128]{1,0:T(8,128)S(1)} collective-permute-done((f32[200,128]{1,0:T(8,128)S(1)}, f32[200,128]{1,0:T(8,128)S(1)}, u32[]{:S(2)}, u32[]{:S(2)}) %collective-permute-start.21) | collective-permute-done | bytes 102432 | tf_op jit(solution)/shard_map/ppermute | solution.py:690
  102.8 4.2 %shard_map.112 = (f32[32,40,128]{2,1,0:T(8,128)S(1)}, f32[32,40,128]{2,1,0:T(8,128)S(1)}, f32[8,16,128]{2,1,0:T(8,128)S(1)}, f32[248,128]{1,0:T(8,128)S(1)}, f32...) custom-call(s32[2]{0:T(128)S(1)} %pad_add_fusion.refs_0_, f32[8,16,128]{2,1,0:T(8,128)S(1)} %get-tuple-element.135.refs_1_, ...), custom_call_target="tpu_custom_call" | custom-call | tf_op jit(solution)/shard_map/pallas_call | solution.py:611
  107.1 4.8 %collective-permute-start.24 = (f32[248,128]{1,0:T(8,128)S(1)}, f32[248,128]{1,0:T(8,128)S(1)}, u32[]{:S(2)}, u32[]{:S(2)}) collective-permute-start(f32[248,128]{1,0:T(8,128)S(1)} %get-tuple-element.142), channel_id=1, source_target_pairs={{0,7},{1,0},{2,1},{3,2},{4,3},{5,4},{6,5},{7,6},{8,15},{9,8},{10,9... | collective-permute-start | bytes 380936 | tf_op jit(solution)/shard_map/ppermute | solution.py:690
  111.8 2.8 %collective-permute-done.23.refs_1_.refs_13_ = f32[248,128]{1,0:T(8,128)S(1)} collective-permute-done((f32[248,128]{1,0:T(8,128)S(1)}, f32[248,128]{1,0:T(8,128)S(1)}, u32[]{:S(2)}, u32[]{:S(2)}) %collective-permute-start.23) | collective-permute-done | bytes 127008 | tf_op jit(solution)/shard_map/ppermute | solution.py:690
  114.7 3.6 %shard_map.113 = (f32[32,40,128]{2,1,0:T(8,128)S(1)}, f32[8,16,128]{2,1,0:T(8,128)S(1)}, f32[200,128]{1,0:T(8,128)S(1)}, f32[200,128]{1,0:T(8,128)S(1)}) custom-call(f32[8,16,128]{2,1,0:T(8,128)S(1)} %get-tuple-element.140.refs_0_, f32[248,128]{1,0:T(8,128)S(1)} %collective-permute-done.23.refs_1_.refs_13_, ...), custom_call_target="tpu_custom_call" | custom-call | tf_op jit(solution)/shard_map/pallas_call | solution.py:611
  118.4 4.8 %collective-permute-start.26 = (f32[200,128]{1,0:T(8,128)S(1)}, f32[200,128]{1,0:T(8,128)S(1)}, u32[]{:S(2)}, u32[]{:S(2)}) collective-permute-start(f32[200,128]{1,0:T(8,128)S(1)} %get-tuple-element.147), channel_id=1, source_target_pairs={{0,7},{1,0},{2,1},{3,2},{4,3},{5,4},{6,5},{7,6},{8,15},{9,8},{10,9... | collective-permute-start | bytes 307208 | tf_op jit(solution)/shard_map/ppermute | solution.py:690
  123.2 2.6 %collective-permute-done.25.refs_2_ = f32[200,128]{1,0:T(8,128)S(1)} collective-permute-done((f32[200,128]{1,0:T(8,128)S(1)}, f32[200,128]{1,0:T(8,128)S(1)}, u32[]{:S(2)}, u32[]{:S(2)}) %collective-permute-start.25) | collective-permute-done | bytes 102432 | tf_op jit(solution)/shard_map/ppermute | solution.py:690
  125.8 4.5 %shard_map.114 = f32[8,32,128]{2,1,0:T(8,128)} custom-call(s32[2]{0:T(128)S(1)} %pad_add_fusion.refs_0_, f32[8,16,128]{2,1,0:T(8,128)S(1)} %get-tuple-element.145.refs_1_, f32[200,128]{1,0:T(8,128)S(1)} %collective-permute-done.25.refs_2_, f32[200,128]{1,0:T(8,128)S(1)} %collective-permute-done.26.refs_3_, ...), custom_call_target="tpu_custom_call" | custom-call | tf_op jit(solution)/shard_map/pallas_call | solution.py:611
  (56 shorter events, 13.1 us)
Async XLA Ops:
  3.0 23.7 %copy-start = (f32[1032,128]{1,0:T(8,128)S(1)}, f32[1032,128]{1,0:T(8,128)}, u32[]{:S(2)}) copy-start(f32[1032,128]{1,0:T(8,128)} %get-tuple-element.80.refs_1_) | copy-start | bytes 1585156
  3.0 19.3 %collective-permute-start.3 = (f32[1032,128]{1,0:T(8,128)}, f32[1032,128]{1,0:T(8,128)S(1)}, u32[]{:S(2)}, u32[]{:S(2)}) collective-permute-start(f32[1032,128]{1,0:T(8,128)} %get-tuple-element.80.refs_1_), channel_id=1, source_target_pairs={{0,16},{8,24},{16,0},{24,8},{1,17},{9,25},{17,1},{25,9},{2,18},{10... | collective-permute-start | bytes 1585160 | tf_op jit(solution)/shard_map/ppermute | solution.py:633
  6.0 8.0 %collective-permute-start = (f32[248,128]{1,0:T(8,128)}, f32[248,128]{1,0:T(8,128)S(1)}, u32[]{:S(2)}, u32[]{:S(2)}) collective-permute-start(f32[248,128]{1,0:T(8,128)} %get-tuple-element.78), channel_id=1, source_target_pairs={{0,1},{1,2},{2,3},{3,4},{4,5},{5,6},{6,7},{7,0},{8,9},{9,10},{10,1... | collective-permute-start | bytes 380936 | tf_op jit(solution)/shard_map/ppermute | solution.py:690
  7.5 7.7 %collective-permute-start.1 = (f32[248,128]{1,0:T(8,128)}, f32[248,128]{1,0:T(8,128)S(1)}, u32[]{:S(2)}, u32[]{:S(2)}) collective-permute-start(f32[248,128]{1,0:T(8,128)} %get-tuple-element.79), channel_id=1, source_target_pairs={{0,7},{1,0},{2,1},{3,2},{4,3},{5,4},{6,5},{7,6},{8,15},{9,8},{10,9... | collective-permute-start | bytes 380936 | tf_op jit(solution)/shard_map/ppermute | solution.py:690
  15.3 7.0 %collective-permute-start.4 = (f32[368,128]{1,0:T(8,128)S(1)}, f32[368,128]{1,0:T(8,128)S(1)}, u32[]{:S(2)}, u32[]{:S(2)}) collective-permute-start(f32[368,128]{1,0:T(8,128)S(1)} %pad_maximum_fusion.1.refs_5_), channel_id=1, source_target_pairs={{0,16},{8,24},{16,0},{24,8},{1,17},{9,25},{17,1},{25,9},{2,18},{10... | collective-permute-start | bytes 565256 | tf_op jit(solution)/shard_map/ppermute | solution.py:633
  15.9 10.8 %collective-permute-start.5 = (f32[1032,128]{1,0:T(8,128)}, f32[1032,128]{1,0:T(8,128)S(1)}, u32[]{:S(2)}, u32[]{:S(2)}) collective-permute-start(f32[1032,128]{1,0:T(8,128)} %get-tuple-element.80.refs_1_), channel_id=1, source_target_pairs={{0,8},{8,0},{16,24},{24,16},{1,9},{9,1},{17,25},{25,17},{2,10},{10... | collective-permute-start | bytes 1585160 | tf_op jit(solution)/shard_map/ppermute | solution.py:638
  22.3 4.4 %collective-permute-start.6 = (f32[1032,128]{1,0:T(8,128)S(1)}, f32[1032,128]{1,0:T(8,128)S(1)}, u32[]{:S(2)}, u32[]{:S(2)}) collective-permute-start(f32[1032,128]{1,0:T(8,128)S(1)} %collective-permute-done.3.refs_2_), channel_id=1, source_target_pairs={{0,8},{8,0},{16,24},{24,16},{1,9},{9,1},{17,25},{25,17},{2,10},{10... | collective-permute-start | bytes 1585160 | tf_op jit(solution)/shard_map/ppermute | solution.py:638
  23.3 8.6 %collective-permute-start.2 = (f32[448,128]{1,0:T(8,128)S(1)}, f32[448,128]{1,0:T(8,128)S(1)}, u32[]{:S(2)}, u32[]{:S(2)}) collective-permute-start(f32[448,128]{1,0:T(8,128)S(1)} %pad_maximum_fusion.refs_1_), channel_id=1, source_target_pairs={{0,16},{8,24},{16,0},{24,8},{1,17},{9,25},{17,1},{25,9},{2,18},{10... | collective-permute-start | bytes 688136 | tf_op jit(solution)/shard_map/ppermute | solution.py:633
  25.1 1.4 %collective-permute-start.7 = (f32[368,128]{1,0:T(8,128)S(1)}, f32[368,128]{1,0:T(8,128)S(1)}, u32[]{:S(2)}, u32[]{:S(2)}) collective-permute-start(f32[368,128]{1,0:T(8,128)S(1)} %pad_maximum_fusion.1.refs_5_), channel_id=1, source_target_pairs={{0,8},{8,0},{16,24},{24,16},{1,9},{9,1},{17,25},{25,17},{2,10},{10... | collective-permute-start | bytes 565256 | tf_op jit(solution)/shard_map/ppermute | solution.py:638
  25.3 1.5 %collective-permute-start.8 = (f32[368,128]{1,0:T(8,128)S(1)}, f32[368,128]{1,0:T(8,128)S(1)}, u32[]{:S(2)}, u32[]{:S(2)}) collective-permute-start(f32[368,128]{1,0:T(8,128)S(1)} %collective-permute-done.4.refs_6_), channel_id=1, source_target_pairs={{0,8},{8,0},{16,24},{24,16},{1,9},{9,1},{17,25},{25,17},{2,10},{10... | collective-permute-start | bytes 565256 | tf_op jit(solution)/shard_map/ppermute | solution.py:638
  26.5 5.7 %collective-permute-start.9 = (f32[448,128]{1,0:T(8,128)S(1)}, f32[448,128]{1,0:T(8,128)S(1)}, u32[]{:S(2)}, u32[]{:S(2)}) collective-permute-start(f32[448,128]{1,0:T(8,128)S(1)} %pad_maximum_fusion.refs_1_), channel_id=1, source_target_pairs={{0,8},{8,0},{16,24},{24,16},{1,9},{9,1},{17,25},{25,17},{2,10},{10... | collective-permute-start | bytes 688136 | tf_op jit(solution)/shard_map/ppermute | solution.py:638
  31.9 1.6 %collective-permute-start.10 = (f32[448,128]{1,0:T(8,128)S(1)}, f32[448,128]{1,0:T(8,128)S(1)}, u32[]{:S(2)}, u32[]{:S(2)}) collective-permute-start(f32[448,128]{1,0:T(8,128)S(1)} %collective-permute-done.2.refs_2_), channel_id=1, source_target_pairs={{0,8},{8,0},{16,24},{24,16},{1,9},{9,1},{17,25},{25,17},{2,10},{10... | collective-permute-start | bytes 688136 | tf_op jit(solution)/shard_map/ppermute | solution.py:638
  33.4 8.5 %collective-permute-start.11 = (f32[248,128]{1,0:T(8,128)S(1)}, f32[248,128]{1,0:T(8,128)S(1)}, u32[]{:S(2)}, u32[]{:S(2)}) collective-permute-start(f32[248,128]{1,0:T(8,128)S(1)} %get-tuple-element.90), channel_id=1, source_target_pairs={{0,1},{1,2},{2,3},{3,4},{4,5},{5,6},{6,7},{7,0},{8,9},{9,10},{10,1... | collective-permute-start | bytes 380936 | tf_op jit(solution)/shard_map/ppermute | solution.py:690
  34.9 8.0 %collective-permute-start.12 = (f32[248,128]{1,0:T(8,128)S(1)}, f32[248,128]{1,0:T(8,128)S(1)}, u32[]{:S(2)}, u32[]{:S(2)}) collective-permute-start(f32[248,128]{1,0:T(8,128)S(1)} %get-tuple-element.91), channel_id=1, source_target_pairs={{0,7},{1,0},{2,1},{3,2},{4,3},{5,4},{6,5},{7,6},{8,15},{9,8},{10,9... | collective-permute-start | bytes 380936 | tf_op jit(solution)/shard_map/ppermute | solution.py:690
  46.6 7.5 %collective-permute-start.13 = (f32[200,128]{1,0:T(8,128)S(1)}, f32[200,128]{1,0:T(8,128)S(1)}, u32[]{:S(2)}, u32[]{:S(2)}) collective-permute-start(f32[200,128]{1,0:T(8,128)S(1)} %get-tuple-element.115), channel_id=1, source_target_pairs={{0,1},{1,2},{2,3},{3,4},{4,5},{5,6},{6,7},{7,0},{8,9},{9,10},{10,1... | collective-permute-start | bytes 307208 | tf_op jit(solution)/shard_map/ppermute | solution.py:690
  46.9 7.4 %collective-permute-start.14 = (f32[200,128]{1,0:T(8,128)S(1)}, f32[200,128]{1,0:T(8,128)S(1)}, u32[]{:S(2)}, u32[]{:S(2)}) collective-permute-start(f32[200,128]{1,0:T(8,128)S(1)} %get-tuple-element.116), channel_id=1, source_target_pairs={{0,7},{1,0},{2,1},{3,2},{4,3},{5,4},{6,5},{7,6},{8,15},{9,8},{10,9... | collective-permute-start | bytes 307208 | tf_op jit(solution)/shard_map/ppermute | solution.py:690
  58.4 7.8 %collective-permute-start.15 = (f32[248,128]{1,0:T(8,128)S(1)}, f32[248,128]{1,0:T(8,128)S(1)}, u32[]{:S(2)}, u32[]{:S(2)}) collective-permute-start(f32[248,128]{1,0:T(8,128)S(1)} %get-tuple-element.121), channel_id=1, source_target_pairs={{0,1},{1,2},{2,3},{3,4},{4,5},{5,6},{6,7},{7,0},{8,9},{9,10},{10,1... | collective-permute-start | bytes 380936 | tf_op jit(solution)/shard_map/ppermute | solution.py:690
  59.0 8.2 %collective-permute-start.16 = (f32[248,128]{1,0:T(8,128)S(1)}, f32[248,128]{1,0:T(8,128)S(1)}, u32[]{:S(2)}, u32[]{:S(2)}) collective-permute-start(f32[248,128]{1,0:T(8,128)S(1)} %get-tuple-element.122), channel_id=1, source_target_pairs={{0,7},{1,0},{2,1},{3,2},{4,3},{5,4},{6,5},{7,6},{8,15},{9,8},{10,9... | collective-permute-start | bytes 380936 | tf_op jit(solution)/shard_map/ppermute | solution.py:690
  70.9 8.0 %collective-permute-start.17 = (f32[200,128]{1,0:T(8,128)S(1)}, f32[200,128]{1,0:T(8,128)S(1)}, u32[]{:S(2)}, u32[]{:S(2)}) collective-permute-start(f32[200,128]{1,0:T(8,128)S(1)} %get-tuple-element.126), channel_id=1, source_target_pairs={{0,1},{1,2},{2,3},{3,4},{4,5},{5,6},{6,7},{7,0},{8,9},{9,10},{10,1... | collective-permute-start | bytes 307208 | tf_op jit(solution)/shard_map/ppermute | solution.py:690
  71.0 8.0 %collective-permute-start.18 = (f32[200,128]{1,0:T(8,128)S(1)}, f32[200,128]{1,0:T(8,128)S(1)}, u32[]{:S(2)}, u32[]{:S(2)}) collective-permute-start(f32[200,128]{1,0:T(8,128)S(1)} %get-tuple-element.127), channel_id=1, source_target_pairs={{0,7},{1,0},{2,1},{3,2},{4,3},{5,4},{6,5},{7,6},{8,15},{9,8},{10,9... | collective-permute-start | bytes 307208 | tf_op jit(solution)/shard_map/ppermute | solution.py:690
  83.6 7.7 %collective-permute-start.19 = (f32[248,128]{1,0:T(8,128)S(1)}, f32[248,128]{1,0:T(8,128)S(1)}, u32[]{:S(2)}, u32[]{:S(2)}) collective-permute-start(f32[248,128]{1,0:T(8,128)S(1)} %get-tuple-element.131), channel_id=1, source_target_pairs={{0,1},{1,2},{2,3},{3,4},{4,5},{5,6},{6,7},{7,0},{8,9},{9,10},{10,1... | collective-permute-start | bytes 380936 | tf_op jit(solution)/shard_map/ppermute | solution.py:690
  84.2 7.6 %collective-permute-start.20 = (f32[248,128]{1,0:T(8,128)S(1)}, f32[248,128]{1,0:T(8,128)S(1)}, u32[]{:S(2)}, u32[]{:S(2)}) collective-permute-start(f32[248,128]{1,0:T(8,128)S(1)} %get-tuple-element.132), channel_id=1, source_target_pairs={{0,7},{1,0},{2,1},{3,2},{4,3},{5,4},{6,5},{7,6},{8,15},{9,8},{10,9... | collective-permute-start | bytes 380936 | tf_op jit(solution)/shard_map/ppermute | solution.py:690
  95.4 7.4 %collective-permute-start.21 = (f32[200,128]{1,0:T(8,128)S(1)}, f32[200,128]{1,0:T(8,128)S(1)}, u32[]{:S(2)}, u32[]{:S(2)}) collective-permute-start(f32[200,128]{1,0:T(8,128)S(1)} %get-tuple-element.136), channel_id=1, source_target_pairs={{0,1},{1,2},{2,3},{3,4},{4,5},{5,6},{6,7},{7,0},{8,9},{9,10},{10,1... | collective-permute-start | bytes 307208 | tf_op jit(solution)/shard_map/ppermute | solution.py:690
  95.5 7.3 %collective-permute-start.22 = (f32[200,128]{1,0:T(8,128)S(1)}, f32[200,128]{1,0:T(8,128)S(1)}, u32[]{:S(2)}, u32[]{:S(2)}) collective-permute-start(f32[200,128]{1,0:T(8,128)S(1)} %get-tuple-element.137), channel_id=1, source_target_pairs={{0,7},{1,0},{2,1},{3,2},{4,3},{5,4},{6,5},{7,6},{8,15},{9,8},{10,9... | collective-permute-start | bytes 307208 | tf_op jit(solution)/shard_map/ppermute | solution.py:690
  107.0 7.7 %collective-permute-start.23 = (f32[248,128]{1,0:T(8,128)S(1)}, f32[248,128]{1,0:T(8,128)S(1)}, u32[]{:S(2)}, u32[]{:S(2)}) collective-permute-start(f32[248,128]{1,0:T(8,128)S(1)} %get-tuple-element.141), channel_id=1, source_target_pairs={{0,1},{1,2},{2,3},{3,4},{4,5},{5,6},{6,7},{7,0},{8,9},{9,10},{10,1... | collective-permute-start | bytes 380936 | tf_op jit(solution)/shard_map/ppermute | solution.py:690
  107.1 7.6 %collective-permute-start.24 = (f32[248,128]{1,0:T(8,128)S(1)}, f32[248,128]{1,0:T(8,128)S(1)}, u32[]{:S(2)}, u32[]{:S(2)}) collective-permute-start(f32[248,128]{1,0:T(8,128)S(1)} %get-tuple-element.142), channel_id=1, source_target_pairs={{0,7},{1,0},{2,1},{3,2},{4,3},{5,4},{6,5},{7,6},{8,15},{9,8},{10,9... | collective-permute-start | bytes 380936 | tf_op jit(solution)/shard_map/ppermute | solution.py:690
  118.3 7.5 %collective-permute-start.25 = (f32[200,128]{1,0:T(8,128)S(1)}, f32[200,128]{1,0:T(8,128)S(1)}, u32[]{:S(2)}, u32[]{:S(2)}) collective-permute-start(f32[200,128]{1,0:T(8,128)S(1)} %get-tuple-element.146), channel_id=1, source_target_pairs={{0,1},{1,2},{2,3},{3,4},{4,5},{5,6},{6,7},{7,0},{8,9},{9,10},{10,1... | collective-permute-start | bytes 307208 | tf_op jit(solution)/shard_map/ppermute | solution.py:690
  118.4 7.4 %collective-permute-start.26 = (f32[200,128]{1,0:T(8,128)S(1)}, f32[200,128]{1,0:T(8,128)S(1)}, u32[]{:S(2)}, u32[]{:S(2)}) collective-permute-start(f32[200,128]{1,0:T(8,128)S(1)} %get-tuple-element.147), channel_id=1, source_target_pairs={{0,7},{1,0},{2,1},{3,2},{4,3},{5,4},{6,5},{7,6},{8,15},{9,8},{10,9... | collective-permute-start | bytes 307208 | tf_op jit(solution)/shard_map/ppermute | solution.py:690

commit v4 on v3

--- a/solution.py
+++ b/solution.py
@@ -734,7 +734,8 @@
     coeffs, sto, begun = list(outs[:5]), outs[5], outs[8:13]
     own_wells = outs[13]
     late_same, _ = lax.optimization_barrier((late_same, begun))
-    lates, begun = lax.optimization_barrier((all_parts(late, late_swapped, late_same, tiles), begun))
+    begun = list(begun)
+    lates, begun[4] = lax.optimization_barrier((all_parts(late, late_swapped, late_same, tiles), begun[4]))
     later = call(
         functools.partial(third_kernel, nx, n_gy, unroll),
         [window, (2, 10, FR, 128)] + mid_shapes + coarse_shapes,

time: 130 us -> 130 us (level)
  transfers between devices with their start and end apart: 27 -> 27, of which waited for: 18 -> 14; matrix products, arithmetic and copies ran while one was open for 3% -> 3% of each run, Pallas kernels for 7% -> 7%
where the time goes in v4:
time: 130 us
  starting transfers between devices  49 us (38%)
  Pallas kernels  43 us (33%)
  waiting for transfers between devices  32.5 us (25%)
  matrix products  2.63 us (2%)
  other arithmetic  1.62 us (1%)
    pallas_call x11, Pallas kernels, call(): pl.pallas_call(kernel, out_shape=[jax.ShapeDtypeStruct(shape, f32) for sh...  43 us
    ppermute x9, starting transfers between devices, exchange(): lax.ppermute(down, 'gy', down_perm)  38 us
    ppermute x9, waiting for transfers between devices, exchange(): lax.ppermute(up, 'gy', up_perm)  20.3 us
    ppermute x3, waiting for transfers between devices, same_core(): parts.append(lax.ppermute(array, 'gx', perm))  6.47 us
    ppermute x3, starting transfers between devices, same_core(): parts.append(lax.ppermute(array, 'gx', perm))  5.33 us
    ppermute x9, starting transfers between devices, exchange(): lax.ppermute(up, 'gy', up_perm)  4.95 us
    ppermute x9, waiting for transfers between devices, exchange(): lax.ppermute(down, 'gy', down_perm)  3.34 us
    dot_general x1, matrix products, part(): return jnp.dot(left, right, precision=lax.Precision.HIGHEST)  2.63 us
  transfers between devices with their start and end apart: 27, of which 14 were waited for; matrix products, arithmetic and copies ran while one was open for 3% of the time, Pallas kernels for 7%

profile of v4, /device:TPU:0, one launch (start us, length us, event | category | flops | bytes accessed | tf_op | source)
XLA Modules:
  0.0 129.6 jit_solution(11691194286645369320)
XLA Ops:
  0.6 2.4 %shard_map.104 = (f32[1032,128]{1,0:T(8,128)}, f32[320,128]{1,0:T(8,128)}, f32[248,128]{1,0:T(8,128)}, f32[248,128]{1,0:T(8,128)}) custom-call(s32[32]{0:T(128)} %refs_0_.1, s32[32]{0:T(128)} %refs_1_.1, s32[32]{0:T(128)} %bitcast.15, s32[32]{0:T(128)} %refs_3_.1, f32[8,32,128]{2,1,0:T(8,128)} %refs_4_.1, f32[8,32,128]{2,1,0:T(8,128)} %refs_5_.1, ...), custom_call_target="tpu_custom_call" | custom-call | tf_op jit(solution)/shard_map/pallas_call | solution.py:611
  3.0 3.0 %collective-permute-start = (f32[1032,128]{1,0:T(8,128)}, f32[1032,128]{1,0:T(8,128)S(1)}, u32[]{:S(2)}, u32[]{:S(2)}) collective-permute-start(f32[1032,128]{1,0:T(8,128)} %get-tuple-element.73.refs_1_), channel_id=1, source_target_pairs={{0,16},{8,24},{16,0},{24,8},{1,17},{9,25},{17,1},{25,9},{2,18},{10... | collective-permute-start | bytes 1585160 | tf_op jit(solution)/shard_map/ppermute | solution.py:633
  7.5 3.2 %collective-permute-start.2 = (f32[248,128]{1,0:T(8,128)}, f32[248,128]{1,0:T(8,128)S(1)}, u32[]{:S(2)}, u32[]{:S(2)}) collective-permute-start(f32[248,128]{1,0:T(8,128)} %get-tuple-element.75), channel_id=1, source_target_pairs={{0,7},{1,0},{2,1},{3,2},{4,3},{5,4},{6,5},{7,6},{8,15},{9,8},{10,9... | collective-permute-start | bytes 380936 | tf_op jit(solution)/shard_map/ppermute | solution.py:690
  10.8 3.2 %collective-permute-done.1 = f32[248,128]{1,0:T(8,128)S(1)} collective-permute-done((f32[248,128]{1,0:T(8,128)}, f32[248,128]{1,0:T(8,128)S(1)}, u32[]{:S(2)}, u32[]{:S(2)}) %collective-permute-start.1) | collective-permute-done | bytes 127008 | tf_op jit(solution)/shard_map/ppermute | solution.py:690
  15.9 6.5 %collective-permute-done.3.refs_6_ = f32[368,128]{1,0:T(8,128)S(1)} collective-permute-done((f32[368,128]{1,0:T(8,128)S(1)}, f32[368,128]{1,0:T(8,128)S(1)}, u32[]{:S(2)}, u32[]{:S(2)}) %collective-permute-start.3) | collective-permute-done | bytes 188448 | tf_op jit(solution)/shard_map/ppermute | solution.py:633
  23.3 1.8 %collective-permute-start.9 = (f32[448,128]{1,0:T(8,128)S(1)}, f32[448,128]{1,0:T(8,128)S(1)}, u32[]{:S(2)}, u32[]{:S(2)}) collective-permute-start(f32[448,128]{1,0:T(8,128)S(1)} %pad_maximum_fusion.refs_1_), channel_id=1, source_target_pairs={{0,16},{8,24},{16,0},{24,8},{1,17},{9,25},{17,1},{25,9},{2,18},{10... | collective-permute-start | bytes 688136 | tf_op jit(solution)/shard_map/ppermute | solution.py:633
  26.8 5.1 %shard_map.105 = (f32[33,56,128]{2,1,0:T(8,128)S(1)}, f32[32,56,128]{2,1,0:T(8,128)S(1)}, f32[32,56,128]{2,1,0:T(8,128)S(1)}, f32[32,56,128]{2,1,0:T(8,128)S(1)}...) custom-call(s32[2]{0:T(128)S(1)} %pad_add_fusion.refs_0_, ...), custom_call_target="tpu_custom_call" | custom-call | tf_op jit(solution)/shard_map/pallas_call | solution.py:611
  31.9 1.5 %collective-permute-start.8 = (f32[248,128]{1,0:T(8,128)S(1)}, f32[248,128]{1,0:T(8,128)S(1)}, u32[]{:S(2)}, u32[]{:S(2)}) collective-permute-start(f32[248,128]{1,0:T(8,128)S(1)} %get-tuple-element.79), channel_id=1, source_target_pairs={{0,1},{1,2},{2,3},{3,4},{4,5},{5,6},{6,7},{7,0},{8,9},{9,10},{10,1... | collective-permute-start | bytes 380936 | tf_op jit(solution)/shard_map/ppermute | solution.py:690
  34.9 3.2 %collective-permute-start.12 = (f32[248,128]{1,0:T(8,128)S(1)}, f32[248,128]{1,0:T(8,128)S(1)}, u32[]{:S(2)}, u32[]{:S(2)}) collective-permute-start(f32[248,128]{1,0:T(8,128)S(1)} %get-tuple-element.85), channel_id=1, source_target_pairs={{0,7},{1,0},{2,1},{3,2},{4,3},{5,4},{6,5},{7,6},{8,15},{9,8},{10,9... | collective-permute-start | bytes 380936 | tf_op jit(solution)/shard_map/ppermute | solution.py:690
  38.1 3.6 %shard_map.106 = (f32[32,40,128]{2,1,0:T(8,128)S(1)}, f32[2,10,56,128]{3,2,1,0:T(8,128)S(1)}, f32[9,64,128]{2,1,0:T(8,128)S(1)}, f32[8,64,128]{2,1,0:T(8,128)S(1...) custom-call(s32[2]{0:T(128)S(1)} %pad_add_fusion.refs_0_, ...), custom_call_target="tpu_custom_call" | custom-call | tf_op jit(solution)/shard_map/pallas_call | solution.py:611
  43.0 3.6 %shard_map.107 = (f32[32,40,128]{2,1,0:T(8,128)S(1)}, f32[8,16,128]{2,1,0:T(8,128)S(1)}, f32[200,128]{1,0:T(8,128)S(1)}, f32[200,128]{1,0:T(8,128)S(1)}) custom-call(f32[8,16,128]{2,1,0:T(8,128)S(1)} %get-tuple-element.78.refs_0_, f32[248,128]{1,0:T(8,128)S(1)} %collective-permute-done.8.refs_1_.refs_13_, ...), custom_call_target="tpu_custom_call" | custom-call | tf_op jit(solution)/shard_map/pallas_call | solution.py:611
  46.7 4.7 %collective-permute-start.14 = (f32[200,128]{1,0:T(8,128)S(1)}, f32[200,128]{1,0:T(8,128)S(1)}, u32[]{:S(2)}, u32[]{:S(2)}) collective-permute-start(f32[200,128]{1,0:T(8,128)S(1)} %get-tuple-element.108), channel_id=1, source_target_pairs={{0,7},{1,0},{2,1},{3,2},{4,3},{5,4},{6,5},{7,6},{8,15},{9,8},{10,9... | collective-permute-start | bytes 307208 | tf_op jit(solution)/shard_map/ppermute | solution.py:690
  51.4 2.8 %collective-permute-done.13.refs_2_ = f32[200,128]{1,0:T(8,128)S(1)} collective-permute-done((f32[200,128]{1,0:T(8,128)S(1)}, f32[200,128]{1,0:T(8,128)S(1)}, u32[]{:S(2)}, u32[]{:S(2)}) %collective-permute-start.13) | collective-permute-done | bytes 102432 | tf_op jit(solution)/shard_map/ppermute | solution.py:690
  54.2 4.0 %shard_map.108 = (f32[32,40,128]{2,1,0:T(8,128)S(1)}, f32[32,40,128]{2,1,0:T(8,128)S(1)}, f32[8,16,128]{2,1,0:T(8,128)S(1)}, f32[248,128]{1,0:T(8,128)S(1)}, f32...) custom-call(s32[2]{0:T(128)S(1)} %pad_add_fusion.refs_0_, f32[8,16,128]{2,1,0:T(8,128)S(1)} %get-tuple-element.106.refs_1_, ...), custom_call_target="tpu_custom_call" | custom-call | tf_op jit(solution)/shard_map/pallas_call | solution.py:611
  58.3 4.7 %collective-permute-start.16 = (f32[248,128]{1,0:T(8,128)S(1)}, f32[248,128]{1,0:T(8,128)S(1)}, u32[]{:S(2)}, u32[]{:S(2)}) collective-permute-start(f32[248,128]{1,0:T(8,128)S(1)} %get-tuple-element.114), channel_id=1, source_target_pairs={{0,7},{1,0},{2,1},{3,2},{4,3},{5,4},{6,5},{7,6},{8,15},{9,8},{10,9... | collective-permute-start | bytes 380936 | tf_op jit(solution)/shard_map/ppermute | solution.py:690
  63.0 3.0 %collective-permute-done.15.refs_1_.refs_13_ = f32[248,128]{1,0:T(8,128)S(1)} collective-permute-done((f32[248,128]{1,0:T(8,128)S(1)}, f32[248,128]{1,0:T(8,128)S(1)}, u32[]{:S(2)}, u32[]{:S(2)}) %collective-permute-start.15) | collective-permute-done | bytes 127008 | tf_op jit(solution)/shard_map/ppermute | solution.py:690
  66.1 3.6 %shard_map.109 = (f32[32,40,128]{2,1,0:T(8,128)S(1)}, f32[8,16,128]{2,1,0:T(8,128)S(1)}, f32[200,128]{1,0:T(8,128)S(1)}, f32[200,128]{1,0:T(8,128)S(1)}) custom-call(f32[8,16,128]{2,1,0:T(8,128)S(1)} %get-tuple-element.112.refs_0_, f32[248,128]{1,0:T(8,128)S(1)} %collective-permute-done.15.refs_1_.refs_13_, ...), custom_call_target="tpu_custom_call" | custom-call | tf_op jit(solution)/shard_map/pallas_call | solution.py:611
  69.9 4.8 %collective-permute-start.18 = (f32[200,128]{1,0:T(8,128)S(1)}, f32[200,128]{1,0:T(8,128)S(1)}, u32[]{:S(2)}, u32[]{:S(2)}) collective-permute-start(f32[200,128]{1,0:T(8,128)S(1)} %get-tuple-element.119), channel_id=1, source_target_pairs={{0,7},{1,0},{2,1},{3,2},{4,3},{5,4},{6,5},{7,6},{8,15},{9,8},{10,9... | collective-permute-start | bytes 307208 | tf_op jit(solution)/shard_map/ppermute | solution.py:690
  75.1 2.6 %fusion = f32[1280,256]{1,0:T(8,128)S(1)} fusion(s32[1024]{0:T(1024)S(1)} %bitcast.14, f32[1024,128]{1,0:T(8,128)S(1)} %get-tuple-element.150, f32[1024,128]{1,0:T(8,128)S(1)} %get-tuple-element.149), kind=kOutput, calls=%fused_computation.1 | convolution fusion | flops 4028104704 | bytes 2363392 | tf_op jit(solution)/shard_map/dot_general | solution.py:668
  77.9 4.6 %shard_map.110 = (f32[32,40,128]{2,1,0:T(8,128)S(1)}, f32[32,40,128]{2,1,0:T(8,128)S(1)}, f32[8,16,128]{2,1,0:T(8,128)S(1)}, f32[248,128]{1,0:T(8,128)S(1)}, f32...) custom-call(s32[2]{0:T(128)S(1)} %pad_add_fusion.refs_0_, f32[8,16,128]{2,1,0:T(8,128)S(1)} %get-tuple-element.117.refs_1_, ...), custom_call_target="tpu_custom_call" | custom-call | tf_op jit(solution)/shard_map/pallas_call | solution.py:611
  82.7 4.5 %collective-permute-start.20 = (f32[248,128]{1,0:T(8,128)S(1)}, f32[248,128]{1,0:T(8,128)S(1)}, u32[]{:S(2)}, u32[]{:S(2)}) collective-permute-start(f32[248,128]{1,0:T(8,128)S(1)} %get-tuple-element.124), channel_id=1, source_target_pairs={{0,7},{1,0},{2,1},{3,2},{4,3},{5,4},{6,5},{7,6},{8,15},{9,8},{10,9... | collective-permute-start | bytes 380936 | tf_op jit(solution)/shard_map/ppermute | solution.py:690
  87.2 3.0 %collective-permute-done.19.refs_1_.refs_13_ = f32[248,128]{1,0:T(8,128)S(1)} collective-permute-done((f32[248,128]{1,0:T(8,128)S(1)}, f32[248,128]{1,0:T(8,128)S(1)}, u32[]{:S(2)}, u32[]{:S(2)}) %collective-permute-start.19) | collective-permute-done | bytes 127008 | tf_op jit(solution)/shard_map/ppermute | solution.py:690
  91.0 3.6 %shard_map.111 = (f32[32,40,128]{2,1,0:T(8,128)S(1)}, f32[8,16,128]{2,1,0:T(8,128)S(1)}, f32[200,128]{1,0:T(8,128)S(1)}, f32[200,128]{1,0:T(8,128)S(1)}) custom-call(f32[8,16,128]{2,1,0:T(8,128)S(1)} %get-tuple-element.122.refs_0_, f32[248,128]{1,0:T(8,128)S(1)} %collective-permute-done.19.refs_1_.refs_13_, ...), custom_call_target="tpu_custom_call" | custom-call | tf_op jit(solution)/shard_map/pallas_call | solution.py:611
  94.7 4.7 %collective-permute-start.22 = (f32[200,128]{1,0:T(8,128)S(1)}, f32[200,128]{1,0:T(8,128)S(1)}, u32[]{:S(2)}, u32[]{:S(2)}) collective-permute-start(f32[200,128]{1,0:T(8,128)S(1)} %get-tuple-element.129), channel_id=1, source_target_pairs={{0,7},{1,0},{2,1},{3,2},{4,3},{5,4},{6,5},{7,6},{8,15},{9,8},{10,9... | collective-permute-start | bytes 307208 | tf_op jit(solution)/shard_map/ppermute | solution.py:690
  99.4 2.7 %collective-permute-done.21.refs_2_ = f32[200,128]{1,0:T(8,128)S(1)} collective-permute-done((f32[200,128]{1,0:T(8,128)S(1)}, f32[200,128]{1,0:T(8,128)S(1)}, u32[]{:S(2)}, u32[]{:S(2)}) %collective-permute-start.21) | collective-permute-done | bytes 102432 | tf_op jit(solution)/shard_map/ppermute | solution.py:690
  102.1 4.2 %shard_map.112 = (f32[32,40,128]{2,1,0:T(8,128)S(1)}, f32[32,40,128]{2,1,0:T(8,128)S(1)}, f32[8,16,128]{2,1,0:T(8,128)S(1)}, f32[248,128]{1,0:T(8,128)S(1)}, f32...) custom-call(s32[2]{0:T(128)S(1)} %pad_add_fusion.refs_0_, f32[8,16,128]{2,1,0:T(8,128)S(1)} %get-tuple-element.127.refs_1_, ...), custom_call_target="tpu_custom_call" | custom-call | tf_op jit(solution)/shard_map/pallas_call | solution.py:611
  107.1 4.0 %collective-permute-start.24 = (f32[248,128]{1,0:T(8,128)S(1)}, f32[248,128]{1,0:T(8,128)S(1)}, u32[]{:S(2)}, u32[]{:S(2)}) collective-permute-start(f32[248,128]{1,0:T(8,128)S(1)} %get-tuple-element.134), channel_id=1, source_target_pairs={{0,7},{1,0},{2,1},{3,2},{4,3},{5,4},{6,5},{7,6},{8,15},{9,8},{10,9... | collective-permute-start | bytes 380936 | tf_op jit(solution)/shard_map/ppermute | solution.py:690
  111.1 3.0 %collective-permute-done.23.refs_1_.refs_13_ = f32[248,128]{1,0:T(8,128)S(1)} collective-permute-done((f32[248,128]{1,0:T(8,128)S(1)}, f32[248,128]{1,0:T(8,128)S(1)}, u32[]{:S(2)}, u32[]{:S(2)}) %collective-permute-start.23) | collective-permute-done | bytes 127008 | tf_op jit(solution)/shard_map/ppermute | solution.py:690
  114.1 3.6 %shard_map.113 = (f32[32,40,128]{2,1,0:T(8,128)S(1)}, f32[8,16,128]{2,1,0:T(8,128)S(1)}, f32[200,128]{1,0:T(8,128)S(1)}, f32[200,128]{1,0:T(8,128)S(1)}) custom-call(f32[8,16,128]{2,1,0:T(8,128)S(1)} %get-tuple-element.132.refs_0_, f32[248,128]{1,0:T(8,128)S(1)} %collective-permute-done.23.refs_1_.refs_13_, ...), custom_call_target="tpu_custom_call" | custom-call | tf_op jit(solution)/shard_map/pallas_call | solution.py:611
  118.4 4.0 %collective-permute-start.26 = (f32[200,128]{1,0:T(8,128)S(1)}, f32[200,128]{1,0:T(8,128)S(1)}, u32[]{:S(2)}, u32[]{:S(2)}) collective-permute-start(f32[200,128]{1,0:T(8,128)S(1)} %get-tuple-element.139), channel_id=1, source_target_pairs={{0,7},{1,0},{2,1},{3,2},{4,3},{5,4},{6,5},{7,6},{8,15},{9,8},{10,9... | collective-permute-start | bytes 307208 | tf_op jit(solution)/shard_map/ppermute | solution.py:690
  122.5 2.6 %collective-permute-done.25.refs_2_ = f32[200,128]{1,0:T(8,128)S(1)} collective-permute-done((f32[200,128]{1,0:T(8,128)S(1)}, f32[200,128]{1,0:T(8,128)S(1)}, u32[]{:S(2)}, u32[]{:S(2)}) %collective-permute-start.25) | collective-permute-done | bytes 102432 | tf_op jit(solution)/shard_map/ppermute | solution.py:690
  125.1 4.5 %shard_map.114 = f32[8,32,128]{2,1,0:T(8,128)} custom-call(s32[2]{0:T(128)S(1)} %pad_add_fusion.refs_0_, f32[8,16,128]{2,1,0:T(8,128)S(1)} %get-tuple-element.137.refs_1_, f32[200,128]{1,0:T(8,128)S(1)} %collective-permute-done.25.refs_2_, f32[200,128]{1,0:T(8,128)S(1)} %collective-permute-done.26.refs_3_, ...), custom_call_target="tpu_custom_call" | custom-call | tf_op jit(solution)/shard_map/pallas_call | solution.py:611
  (56 shorter events, 12.2 us)
Async XLA Ops:
  3.0 23.7 %copy-start = (f32[1032,128]{1,0:T(8,128)S(1)}, f32[1032,128]{1,0:T(8,128)}, u32[]{:S(2)}) copy-start(f32[1032,128]{1,0:T(8,128)} %get-tuple-element.73.refs_1_) | copy-start | bytes 1585156
  3.0 19.3 %collective-permute-start = (f32[1032,128]{1,0:T(8,128)}, f32[1032,128]{1,0:T(8,128)S(1)}, u32[]{:S(2)}, u32[]{:S(2)}) collective-permute-start(f32[1032,128]{1,0:T(8,128)} %get-tuple-element.73.refs_1_), channel_id=1, source_target_pairs={{0,16},{8,24},{16,0},{24,8},{1,17},{9,25},{17,1},{25,9},{2,18},{10... | collective-permute-start | bytes 1585160 | tf_op jit(solution)/shard_map/ppermute | solution.py:633
  6.0 8.0 %collective-permute-start.1 = (f32[248,128]{1,0:T(8,128)}, f32[248,128]{1,0:T(8,128)S(1)}, u32[]{:S(2)}, u32[]{:S(2)}) collective-permute-start(f32[248,128]{1,0:T(8,128)} %get-tuple-element.74), channel_id=1, source_target_pairs={{0,1},{1,2},{2,3},{3,4},{4,5},{5,6},{6,7},{7,0},{8,9},{9,10},{10,1... | collective-permute-start | bytes 380936 | tf_op jit(solution)/shard_map/ppermute | solution.py:690
  7.5 7.7 %collective-permute-start.2 = (f32[248,128]{1,0:T(8,128)}, f32[248,128]{1,0:T(8,128)S(1)}, u32[]{:S(2)}, u32[]{:S(2)}) collective-permute-start(f32[248,128]{1,0:T(8,128)} %get-tuple-element.75), channel_id=1, source_target_pairs={{0,7},{1,0},{2,1},{3,2},{4,3},{5,4},{6,5},{7,6},{8,15},{9,8},{10,9... | collective-permute-start | bytes 380936 | tf_op jit(solution)/shard_map/ppermute | solution.py:690
  15.3 7.0 %collective-permute-start.3 = (f32[368,128]{1,0:T(8,128)S(1)}, f32[368,128]{1,0:T(8,128)S(1)}, u32[]{:S(2)}, u32[]{:S(2)}) collective-permute-start(f32[368,128]{1,0:T(8,128)S(1)} %pad_maximum_fusion.1.refs_5_), channel_id=1, source_target_pairs={{0,16},{8,24},{16,0},{24,8},{1,17},{9,25},{17,1},{25,9},{2,18},{10... | collective-permute-start | bytes 565256 | tf_op jit(solution)/shard_map/ppermute | solution.py:633
  15.9 10.8 %collective-permute-start.4 = (f32[1032,128]{1,0:T(8,128)}, f32[1032,128]{1,0:T(8,128)S(1)}, u32[]{:S(2)}, u32[]{:S(2)}) collective-permute-start(f32[1032,128]{1,0:T(8,128)} %get-tuple-element.73.refs_1_), channel_id=1, source_target_pairs={{0,8},{8,0},{16,24},{24,16},{1,9},{9,1},{17,25},{25,17},{2,10},{10... | collective-permute-start | bytes 1585160 | tf_op jit(solution)/shard_map/ppermute | solution.py:638
  22.3 4.4 %collective-permute-start.5 = (f32[1032,128]{1,0:T(8,128)S(1)}, f32[1032,128]{1,0:T(8,128)S(1)}, u32[]{:S(2)}, u32[]{:S(2)}) collective-permute-start(f32[1032,128]{1,0:T(8,128)S(1)} %collective-permute-done.refs_2_), channel_id=1, source_target_pairs={{0,8},{8,0},{16,24},{24,16},{1,9},{9,1},{17,25},{25,17},{2,10},{10... | collective-permute-start | bytes 1585160 | tf_op jit(solution)/shard_map/ppermute | solution.py:638
  23.3 10.1 %collective-permute-start.9 = (f32[448,128]{1,0:T(8,128)S(1)}, f32[448,128]{1,0:T(8,128)S(1)}, u32[]{:S(2)}, u32[]{:S(2)}) collective-permute-start(f32[448,128]{1,0:T(8,128)S(1)} %pad_maximum_fusion.refs_1_), channel_id=1, source_target_pairs={{0,16},{8,24},{16,0},{24,8},{1,17},{9,25},{17,1},{25,9},{2,18},{10... | collective-permute-start | bytes 688136 | tf_op jit(solution)/shard_map/ppermute | solution.py:633
  25.1 1.4 %collective-permute-start.6 = (f32[368,128]{1,0:T(8,128)S(1)}, f32[368,128]{1,0:T(8,128)S(1)}, u32[]{:S(2)}, u32[]{:S(2)}) collective-permute-start(f32[368,128]{1,0:T(8,128)S(1)} %pad_maximum_fusion.1.refs_5_), channel_id=1, source_target_pairs={{0,8},{8,0},{16,24},{24,16},{1,9},{9,1},{17,25},{25,17},{2,10},{10... | collective-permute-start | bytes 565256 | tf_op jit(solution)/shard_map/ppermute | solution.py:638
  25.3 1.5 %collective-permute-start.7 = (f32[368,128]{1,0:T(8,128)S(1)}, f32[368,128]{1,0:T(8,128)S(1)}, u32[]{:S(2)}, u32[]{:S(2)}) collective-permute-start(f32[368,128]{1,0:T(8,128)S(1)} %collective-permute-done.3.refs_6_), channel_id=1, source_target_pairs={{0,8},{8,0},{16,24},{24,16},{1,9},{9,1},{17,25},{25,17},{2,10},{10... | collective-permute-start | bytes 565256 | tf_op jit(solution)/shard_map/ppermute | solution.py:638
  26.5 7.0 %collective-permute-start.10 = (f32[448,128]{1,0:T(8,128)S(1)}, f32[448,128]{1,0:T(8,128)S(1)}, u32[]{:S(2)}, u32[]{:S(2)}) collective-permute-start(f32[448,128]{1,0:T(8,128)S(1)} %pad_maximum_fusion.refs_1_), channel_id=1, source_target_pairs={{0,8},{8,0},{16,24},{24,16},{1,9},{9,1},{17,25},{25,17},{2,10},{10... | collective-permute-start | bytes 688136 | tf_op jit(solution)/shard_map/ppermute | solution.py:638
  31.9 9.9 %collective-permute-start.8 = (f32[248,128]{1,0:T(8,128)S(1)}, f32[248,128]{1,0:T(8,128)S(1)}, u32[]{:S(2)}, u32[]{:S(2)}) collective-permute-start(f32[248,128]{1,0:T(8,128)S(1)} %get-tuple-element.79), channel_id=1, source_target_pairs={{0,1},{1,2},{2,3},{3,4},{4,5},{5,6},{6,7},{7,0},{8,9},{9,10},{10,1... | collective-permute-start | bytes 380936 | tf_op jit(solution)/shard_map/ppermute | solution.py:690
  33.4 1.5 %collective-permute-start.11 = (f32[448,128]{1,0:T(8,128)S(1)}, f32[448,128]{1,0:T(8,128)S(1)}, u32[]{:S(2)}, u32[]{:S(2)}) collective-permute-start(f32[448,128]{1,0:T(8,128)S(1)} %collective-permute-done.9.refs_2_), channel_id=1, source_target_pairs={{0,8},{8,0},{16,24},{24,16},{1,9},{9,1},{17,25},{25,17},{2,10},{10... | collective-permute-start | bytes 688136 | tf_op jit(solution)/shard_map/ppermute | solution.py:638
  34.9 8.1 %collective-permute-start.12 = (f32[248,128]{1,0:T(8,128)S(1)}, f32[248,128]{1,0:T(8,128)S(1)}, u32[]{:S(2)}, u32[]{:S(2)}) collective-permute-start(f32[248,128]{1,0:T(8,128)S(1)} %get-tuple-element.85), channel_id=1, source_target_pairs={{0,7},{1,0},{2,1},{3,2},{4,3},{5,4},{6,5},{7,6},{8,15},{9,8},{10,9... | collective-permute-start | bytes 380936 | tf_op jit(solution)/shard_map/ppermute | solution.py:690
  46.6 7.6 %collective-permute-start.13 = (f32[200,128]{1,0:T(8,128)S(1)}, f32[200,128]{1,0:T(8,128)S(1)}, u32[]{:S(2)}, u32[]{:S(2)}) collective-permute-start(f32[200,128]{1,0:T(8,128)S(1)} %get-tuple-element.107), channel_id=1, source_target_pairs={{0,1},{1,2},{2,3},{3,4},{4,5},{5,6},{6,7},{7,0},{8,9},{9,10},{10,1... | collective-permute-start | bytes 307208 | tf_op jit(solution)/shard_map/ppermute | solution.py:690
  46.7 7.5 %collective-permute-start.14 = (f32[200,128]{1,0:T(8,128)S(1)}, f32[200,128]{1,0:T(8,128)S(1)}, u32[]{:S(2)}, u32[]{:S(2)}) collective-permute-start(f32[200,128]{1,0:T(8,128)S(1)} %get-tuple-element.108), channel_id=1, source_target_pairs={{0,7},{1,0},{2,1},{3,2},{4,3},{5,4},{6,5},{7,6},{8,15},{9,8},{10,9... | collective-permute-start | bytes 307208 | tf_op jit(solution)/shard_map/ppermute | solution.py:690
  58.3 7.7 %collective-permute-start.15 = (f32[248,128]{1,0:T(8,128)S(1)}, f32[248,128]{1,0:T(8,128)S(1)}, u32[]{:S(2)}, u32[]{:S(2)}) collective-permute-start(f32[248,128]{1,0:T(8,128)S(1)} %get-tuple-element.113), channel_id=1, source_target_pairs={{0,1},{1,2},{2,3},{3,4},{4,5},{5,6},{6,7},{7,0},{8,9},{9,10},{10,1... | collective-permute-start | bytes 380936 | tf_op jit(solution)/shard_map/ppermute | solution.py:690
  58.3 7.8 %collective-permute-start.16 = (f32[248,128]{1,0:T(8,128)S(1)}, f32[248,128]{1,0:T(8,128)S(1)}, u32[]{:S(2)}, u32[]{:S(2)}) collective-permute-start(f32[248,128]{1,0:T(8,128)S(1)} %get-tuple-element.114), channel_id=1, source_target_pairs={{0,7},{1,0},{2,1},{3,2},{4,3},{5,4},{6,5},{7,6},{8,15},{9,8},{10,9... | collective-permute-start | bytes 380936 | tf_op jit(solution)/shard_map/ppermute | solution.py:690
  69.8 8.0 %collective-permute-start.17 = (f32[200,128]{1,0:T(8,128)S(1)}, f32[200,128]{1,0:T(8,128)S(1)}, u32[]{:S(2)}, u32[]{:S(2)}) collective-permute-start(f32[200,128]{1,0:T(8,128)S(1)} %get-tuple-element.118), channel_id=1, source_target_pairs={{0,1},{1,2},{2,3},{3,4},{4,5},{5,6},{6,7},{7,0},{8,9},{9,10},{10,1... | collective-permute-start | bytes 307208 | tf_op jit(solution)/shard_map/ppermute | solution.py:690
  69.9 8.0 %collective-permute-start.18 = (f32[200,128]{1,0:T(8,128)S(1)}, f32[200,128]{1,0:T(8,128)S(1)}, u32[]{:S(2)}, u32[]{:S(2)}) collective-permute-start(f32[200,128]{1,0:T(8,128)S(1)} %get-tuple-element.119), channel_id=1, source_target_pairs={{0,7},{1,0},{2,1},{3,2},{4,3},{5,4},{6,5},{7,6},{8,15},{9,8},{10,9... | collective-permute-start | bytes 307208 | tf_op jit(solution)/shard_map/ppermute | solution.py:690
  82.5 7.7 %collective-permute-start.19 = (f32[248,128]{1,0:T(8,128)S(1)}, f32[248,128]{1,0:T(8,128)S(1)}, u32[]{:S(2)}, u32[]{:S(2)}) collective-permute-start(f32[248,128]{1,0:T(8,128)S(1)} %get-tuple-element.123), channel_id=1, source_target_pairs={{0,1},{1,2},{2,3},{3,4},{4,5},{5,6},{6,7},{7,0},{8,9},{9,10},{10,1... | collective-permute-start | bytes 380936 | tf_op jit(solution)/shard_map/ppermute | solution.py:690
  82.7 8.4 %collective-permute-start.20 = (f32[248,128]{1,0:T(8,128)S(1)}, f32[248,128]{1,0:T(8,128)S(1)}, u32[]{:S(2)}, u32[]{:S(2)}) collective-permute-start(f32[248,128]{1,0:T(8,128)S(1)} %get-tuple-element.124), channel_id=1, source_target_pairs={{0,7},{1,0},{2,1},{3,2},{4,3},{5,4},{6,5},{7,6},{8,15},{9,8},{10,9... | collective-permute-start | bytes 380936 | tf_op jit(solution)/shard_map/ppermute | solution.py:690
  94.7 7.5 %collective-permute-start.21 = (f32[200,128]{1,0:T(8,128)S(1)}, f32[200,128]{1,0:T(8,128)S(1)}, u32[]{:S(2)}, u32[]{:S(2)}) collective-permute-start(f32[200,128]{1,0:T(8,128)S(1)} %get-tuple-element.128), channel_id=1, source_target_pairs={{0,1},{1,2},{2,3},{3,4},{4,5},{5,6},{6,7},{7,0},{8,9},{9,10},{10,1... | collective-permute-start | bytes 307208 | tf_op jit(solution)/shard_map/ppermute | solution.py:690
  94.7 7.4 %collective-permute-start.22 = (f32[200,128]{1,0:T(8,128)S(1)}, f32[200,128]{1,0:T(8,128)S(1)}, u32[]{:S(2)}, u32[]{:S(2)}) collective-permute-start(f32[200,128]{1,0:T(8,128)S(1)} %get-tuple-element.129), channel_id=1, source_target_pairs={{0,7},{1,0},{2,1},{3,2},{4,3},{5,4},{6,5},{7,6},{8,15},{9,8},{10,9... | collective-permute-start | bytes 307208 | tf_op jit(solution)/shard_map/ppermute | solution.py:690
  106.3 7.8 %collective-permute-start.23 = (f32[248,128]{1,0:T(8,128)S(1)}, f32[248,128]{1,0:T(8,128)S(1)}, u32[]{:S(2)}, u32[]{:S(2)}) collective-permute-start(f32[248,128]{1,0:T(8,128)S(1)} %get-tuple-element.133), channel_id=1, source_target_pairs={{0,1},{1,2},{2,3},{3,4},{4,5},{5,6},{6,7},{7,0},{8,9},{9,10},{10,1... | collective-permute-start | bytes 380936 | tf_op jit(solution)/shard_map/ppermute | solution.py:690
  107.1 7.0 %collective-permute-start.24 = (f32[248,128]{1,0:T(8,128)S(1)}, f32[248,128]{1,0:T(8,128)S(1)}, u32[]{:S(2)}, u32[]{:S(2)}) collective-permute-start(f32[248,128]{1,0:T(8,128)S(1)} %get-tuple-element.134), channel_id=1, source_target_pairs={{0,7},{1,0},{2,1},{3,2},{4,3},{5,4},{6,5},{7,6},{8,15},{9,8},{10,9... | collective-permute-start | bytes 380936 | tf_op jit(solution)/shard_map/ppermute | solution.py:690
  117.7 7.4 %collective-permute-start.25 = (f32[200,128]{1,0:T(8,128)S(1)}, f32[200,128]{1,0:T(8,128)S(1)}, u32[]{:S(2)}, u32[]{:S(2)}) collective-permute-start(f32[200,128]{1,0:T(8,128)S(1)} %get-tuple-element.138), channel_id=1, source_target_pairs={{0,1},{1,2},{2,3},{3,4},{4,5},{5,6},{6,7},{7,0},{8,9},{9,10},{10,1... | collective-permute-start | bytes 307208 | tf_op jit(solution)/shard_map/ppermute | solution.py:690
  118.4 6.7 %collective-permute-start.26 = (f32[200,128]{1,0:T(8,128)S(1)}, f32[200,128]{1,0:T(8,128)S(1)}, u32[]{:S(2)}, u32[]{:S(2)}) collective-permute-start(f32[200,128]{1,0:T(8,128)S(1)} %get-tuple-element.139), channel_id=1, source_target_pairs={{0,7},{1,0},{2,1},{3,2},{4,3},{5,4},{6,5},{7,6},{8,15},{9,8},{10,9... | collective-permute-start | bytes 307208 | tf_op jit(solution)/shard_map/ppermute | solution.py:690
